TPU v7x, 128 devices: a whole 4x4x4 slice. The times are simulated.
128 devices in a mesh: seq: 16 (over z, y), head: 8 (over x, core).
Axes of the slice: x: 4, y: 4, z: 4, core: 2. Of those that a mesh axis runs over, the one named last changes fastest.
Arguments:
- queries: bfloat16 [2048, 5120], P(None, 'head'), may hold values from -6 to 6
- doc_keys: bfloat16 [8192, 1024], P('seq', 'head'), may hold values from -6 to 6
- doc_values: bfloat16 [8192, 1024], P('seq', 'head'), may hold values from -6 to 6
- self_keys: bfloat16 [2048, 1024], P(None, 'head'), may hold values from -6 to 6
- self_values: bfloat16 [2048, 1024], P(None, 'head'), may hold values from -6 to 6
- out_grads: bfloat16 [2048, 5120], P(None, 'head'), may hold values from -96 to 96
- lengths: int32 [4], replicated, may hold values from 1 to 512, as said below
- query_weight: bfloat16 [5120, 5120], P('seq', 'head'), may hold values from -0.078125 to 0.078125
Outputs:
- input_grads: bfloat16 [2048, 5120], P('seq', 'head')
- doc_key_grads: float32 [8192, 1024], P('seq', 'head')
- doc_value_grads: float32 [8192, 1024], P('seq', 'head')
- self_key_grads: float32 [2048, 1024], P('seq', 'head')
- self_value_grads: float32 [2048, 1024], P('seq', 'head')
Inputs may be any that keep to these rules, and one draw needn't show every extreme that they name: `lengths`: at least one response has all 512 tokens in every draw.
All inputs are finite; a program needn't handle non-finite values.
Results may differ from a plain program's by a relative error of at most 0.025.
Values may be sent and summed in bfloat16 or wider, within the bound.
No kernel may reach another device: no remote copies, remote signals or barrier semaphores. Data moves between devices by JAX's collectives and lax.ppermute only.
A program may use at most 128 MiB of HBM per device.

v0:
```python
import math

import jax
import jax.numpy as jnp
from jax import lax
from jax.sharding import PartitionSpec as P

HQ = 40
KVH = 8
HD = 128
L = 512


def combine_stats(former, latter):
    top = jnp.maximum(former[0], latter[0])
    scale_one = jnp.exp(former[0] - top)
    scale_two = jnp.exp(latter[0] - top)
    return (top,) + tuple(
        (
            first_term * scale_one + second_term * scale_two
            for first_term, second_term in zip(former[1:], latter[1:])
        )
    )


def doc_scores(qblock, key_block):
    factor = qblock.shape[-1] ** (-0.5)
    return factor * jnp.einsum(
        "tkgd,jkd->kgtj", qblock, key_block, preferred_element_type=jnp.float32
    )


def value_prods(gblock, value_block):
    return jnp.einsum("tkgd,jkd->kgtj", gblock, value_block, preferred_element_type=jnp.float32)


def block_core(qblock, gblock, log_block, delta_block, key_block, value_block):
    scores = doc_scores(qblock, key_block)
    probs = jnp.exp(scores - log_block[..., None])
    dprods = value_prods(gblock, value_block)
    dscores = (probs * (dprods - delta_block[..., None])).astype(jnp.bfloat16)
    return (probs, dscores)


def body(queries, doc_keys, doc_values, self_keys, self_values, out_grads, lengths, query_weight):
    rows_all = queries.shape[0]
    kv_local = doc_keys.shape[1] // HD
    head_group = HQ // KVH
    doc_rows = doc_keys.shape[0]
    factor = HD ** (-0.5)
    own_rows = rows_all // lax.axis_size("seq")
    own_start = lax.axis_index("seq") * own_rows
    block_rows = math.gcd(rows_all, 512)
    blocks = rows_all // block_rows
    positions = jnp.arange(rows_all, dtype=jnp.int32)
    owner = positions // L
    table = jnp.where(
        owner[:, None] == jnp.arange(lengths.shape[0], dtype=jnp.int32)[None, :],
        lengths[None, :],
        0,
    )
    valid = positions % L < jnp.sum(table, axis=1)
    masked = out_grads * valid[:, None].astype(out_grads.dtype)
    q_four = queries.reshape(rows_all, kv_local, head_group, HD)
    g_four = masked.reshape(rows_all, kv_local, head_group, HD)
    keys_three = doc_keys.reshape(doc_rows, kv_local, HD)
    values_three = doc_values.reshape(doc_rows, kv_local, HD)
    q_blocks = q_four.reshape(blocks, block_rows, kv_local, head_group, HD)
    g_blocks = g_four.reshape(blocks, block_rows, kv_local, head_group, HD)
    self_keys_three = self_keys.reshape(rows_all, kv_local, HD)
    self_values_three = self_values.reshape(rows_all, kv_local, HD)

    def to_rows(stacked):
        return jnp.moveaxis(stacked, 0, 2).reshape(kv_local, head_group, rows_all)

    def to_blocks(rowwise):
        return jnp.moveaxis(rowwise.reshape(kv_local, head_group, blocks, block_rows), 2, 0)

    def take_own(whole):
        return lax.dynamic_slice_in_dim(whole, own_start, own_rows, 2)

    def place_own(whole, own_part):
        return lax.dynamic_update_slice_in_dim(whole, own_part, own_start, 2)

    window = max(own_rows, L)
    key_start = own_start // L * L
    q_own = lax.dynamic_slice_in_dim(q_four, own_start, own_rows, 0)
    g_own = lax.dynamic_slice_in_dim(g_four, own_start, own_rows, 0)
    key_window = lax.dynamic_slice_in_dim(self_keys_three, key_start, window, 0)
    value_window = lax.dynamic_slice_in_dim(self_values_three, key_start, window, 0)
    row_ids = own_start + jnp.arange(own_rows, dtype=jnp.int32)
    key_ids = key_start + jnp.arange(window, dtype=jnp.int32)
    allowed = (key_ids[None, :] // L == row_ids[:, None] // L) & (
        key_ids[None, :] <= row_ids[:, None]
    )
    self_raw = doc_scores(q_own, key_window)
    self_top = jnp.max(jnp.where(allowed, self_raw, -jnp.inf), axis=3)
    self_weights = jnp.where(allowed, jnp.exp(self_raw - self_top[..., None]), 0.0)
    self_total = jnp.sum(self_weights, axis=3)
    self_dprods = value_prods(g_own, value_window)

    def stats_plain(qblock):
        scores = doc_scores(qblock, keys_three)
        top = jnp.max(scores, axis=3)
        return (top, jnp.sum(jnp.exp(scores - top[..., None]), axis=3))

    block_top, block_total = lax.map(stats_plain, q_blocks)
    top_all = to_rows(block_top)
    total_all = to_rows(block_total)
    joined_top, joined_total = combine_stats(
        (take_own(top_all), take_own(total_all)), (self_top, self_total)
    )
    top_all = place_own(top_all, joined_top)
    total_all = place_own(total_all, joined_total)
    row_top = lax.pmax(top_all.astype(jnp.bfloat16), "seq").astype(top_all.dtype)
    row_total = lax.psum(total_all * jnp.exp(top_all - row_top), "seq")
    log_sum = row_top + jnp.log(row_total)
    log_blocks = to_blocks(log_sum)

    def delta_block(items):
        qblock, gblock, log_block = items
        probs = jnp.exp(doc_scores(qblock, keys_three) - log_block[..., None])
        return jnp.sum(probs * value_prods(gblock, values_three), axis=3)

    partial_delta = to_rows(lax.map(delta_block, (q_blocks, g_blocks, log_blocks)))
    self_probs = jnp.where(allowed, jnp.exp(self_raw - take_own(log_sum)[..., None]), 0.0)
    self_delta = jnp.sum(self_probs * self_dprods, axis=3)
    partial_delta = place_own(partial_delta, take_own(partial_delta) + self_delta)
    row_delta = lax.psum(partial_delta, "seq")
    delta_blocks = to_blocks(row_delta)
    zero_grads = jnp.zeros((doc_rows, kv_local, HD), jnp.float32)

    def grad_step(carry, items):
        qblock, gblock, log_block, delta_block = items
        probs, dscores = block_core(
            qblock, gblock, log_block, delta_block, keys_three, values_three
        )
        key_acc = carry[0] + factor * jnp.einsum(
            "kgtj,tkgd->jkd", dscores, qblock, preferred_element_type=jnp.float32
        )
        value_acc = carry[1] + jnp.einsum(
            "kgtj,tkgd->jkd", probs.astype(jnp.bfloat16), gblock, preferred_element_type=jnp.float32
        )
        return (
            (key_acc, value_acc),
            factor
            * jnp.einsum("kgtj,jkd->tkgd", dscores, keys_three, preferred_element_type=jnp.float32),
        )

    (key_grads, value_grads), query_blocks = lax.scan(
        lambda carry, items: grad_step(carry, items),
        (zero_grads, zero_grads),
        (q_blocks, g_blocks, log_blocks, delta_blocks),
    )
    query_doc = lax.psum_scatter(
        query_blocks.reshape(rows_all, kv_local * head_group * HD).astype(jnp.bfloat16),
        "seq",
        scatter_dimension=0,
        tiled=True,
    ).astype(jnp.float32)
    self_probs = jnp.where(allowed, jnp.exp(self_raw - take_own(log_sum)[..., None]), 0.0)
    self_dscores = (self_probs * (self_dprods - take_own(row_delta)[..., None])).astype(
        jnp.bfloat16
    )
    query_self = factor * jnp.einsum(
        "kgtj,jkd->tkgd", self_dscores, key_window, preferred_element_type=jnp.float32
    )
    query_rows = lax.dynamic_slice_in_dim(q_four, key_start, window, 0)
    grad_rows = lax.dynamic_slice_in_dim(g_four, key_start, window, 0)
    keys_owned = lax.dynamic_slice_in_dim(self_keys_three, own_start, own_rows, 0)
    values_owned = lax.dynamic_slice_in_dim(self_values_three, own_start, own_rows, 0)
    log_rows = lax.dynamic_slice_in_dim(log_sum, key_start, window, 2)
    delta_rows = lax.dynamic_slice_in_dim(row_delta, key_start, window, 2)
    later = (row_ids[None, :] // L == key_ids[:, None] // L) & (
        row_ids[None, :] <= key_ids[:, None]
    )
    owner_scores = doc_scores(query_rows, keys_owned)
    owner_probs = jnp.where(later, jnp.exp(owner_scores - log_rows[..., None]), 0.0)
    owner_dprods = value_prods(grad_rows, values_owned)
    owner_dscores = (owner_probs * (owner_dprods - delta_rows[..., None])).astype(jnp.bfloat16)
    key_self_own = (
        factor
        * jnp.einsum(
            "kgtj,tkgd->jkd", owner_dscores, query_rows, preferred_element_type=jnp.float32
        )
    ).reshape(own_rows, kv_local * HD)
    value_self_own = jnp.einsum(
        "kgtj,tkgd->jkd",
        owner_probs.astype(jnp.bfloat16),
        grad_rows,
        preferred_element_type=jnp.float32,
    ).reshape(own_rows, kv_local * HD)
    query_grads = (query_doc + query_self.reshape(own_rows, kv_local * head_group * HD)).astype(
        jnp.bfloat16
    )
    input_terms = lax.dot_general(
        query_grads,
        lax.all_gather(query_weight, "seq", axis=0, tiled=True),
        (((1,), (1,)), ((), ())),
        preferred_element_type=jnp.float32,
    )
    input_grads = lax.psum_scatter(
        input_terms.astype(jnp.bfloat16), "head", scatter_dimension=1, tiled=True
    )
    return (
        input_grads,
        key_grads.reshape(doc_rows, kv_local * HD),
        value_grads.reshape(doc_rows, kv_local * HD),
        key_self_own,
        value_self_own,
    )


def solution(mesh):
    in_specs = (
        P(None, "head"),
        P("seq", "head"),
        P("seq", "head"),
        P(None, "head"),
        P(None, "head"),
        P(None, "head"),
        P(),
        P("seq", "head"),
    )
    out_specs = (
        P("seq", "head"),
        P("seq", "head"),
        P("seq", "head"),
        P("seq", "head"),
        P("seq", "head"),
    )
    return jax.shard_map(body, mesh=mesh, in_specs=in_specs, out_specs=out_specs, check_vma=False)
```

profile of v0, /device:TPU:2, one launch (start us, length us, event | category | flops | bytes accessed | tf_op | source)
XLA Modules:
  0.0 532.7 jit_solution(4837922335884204800)
XLA Ops:
  7.4 3.0 copy.81
  10.4 3.9 reshape_reshape.6
  14.2 5.6 %copy.89 = bf16[4,512,1,5,128]{4,1,3,2,0:T(8,128)(2,1)} copy(bf16[4,512,1,5,128]{1,0,4,3,2:T(4,128)(2,1)} %reshape_reshape.6) | data formatting | bytes 5242880
  19.8 11.4 %while.37 = (s32[]{:T(128)}, f32[4,1,5,512]{3,2,1,0:T(8,128)S(1)}, f32[4,1,5,512]{3,2,1,0:T(8,128)S(1)}, bf16[4,512,1,5,128]{4,1,3,2,0:T(8,128)(2,1)}, bf16[512,1,128]{2,0,1:T(8,128)(2,1)S(1)}, /*index=5*/s32[]{:T(128)}) while((s32[]{:T(128)}, f32[4,1,5,512]{3,2,1,0:T(8,128)S(1)}, f32[4,1,5,512]{3,2,1,0:T(8,128)S(1)}, ...), condition=%wide.region_4.5_spmd, body=%wide.region_1.4_spmd.sunk | while | flops 342092800 | bytes 11368533 | solution.py:107
  33.1 75.9 %pmax.7 = bf16[1,5,2048]{2,1,0:T(8,128)(2,1)S(1)} all-reduce(bf16[1,5,2048]{2,1,0:T(8,128)(2,1)S(1)} %convert_element_type.44), channel_id=1, replica_groups=mesh['seq'=16,'head'=8] {'seq'}, use_global_device_ids=true, to_apply=%region_6.7 | all-reduce | flops 10240 | bytes 40960 | tf_op jit(solution)/shard_map/pmax | solution.py:115
  109.0 69.6 %psum.14 = f32[1,5,2048]{2,1,0:T(8,128)S(1)} all-reduce(f32[1,5,2048]{2,1,0:T(8,128)S(1)} %fusion.98), channel_id=1, replica_groups=mesh['seq'=16,'head'=8] {'seq'}, use_global_device_ids=true, to_apply=%region_8.9 | all-reduce | flops 10240 | bytes 81920 | tf_op jit(solution)/shard_map/psum | solution.py:116
  178.7 4.5 copy.85
  183.3 3.5 broadcast_multiply_fusion
  186.7 5.5 %reshape_reshape.7 = bf16[4,512,1,5,128]{1,0,4,3,2:T(4,128)(2,1)} reshape(bf16[2048,640]{0,1:T(8,128)(2,1)} %broadcast_multiply_fusion) | data formatting | bytes 5242880 | tf_op jit(solution)/shard_map/reshape;reshape | solution.py:69
  192.3 5.6 %copy.90 = bf16[4,512,1,5,128]{4,1,3,2,0:T(8,128)(2,1)} copy(bf16[4,512,1,5,128]{1,0,4,3,2:T(4,128)(2,1)} %reshape_reshape.7) | data formatting | bytes 5242880
  197.9 17.8 %while.38 = (s32[]{:T(128)}, f32[4,1,5,512]{3,2,1,0:T(8,128)S(1)}, bf16[4,512,1,5,128]{4,1,3,2,0:T(8,128)(2,1)}, bf16[512,1,128]{2,0,1:T(8,128)(2,1)S(1)}, f32[4...) while((s32[]{:T(128)}, f32[4,1,5,512]{3,2,1,0:T(8,128)S(1)}, ...), condition=%wide.region_11.12_spmd, body=%wide.region_9.11_spmd.sunk | while | flops 676328960 | bytes 12132461 | solution.py:125
  218.1 70.3 %psum.15 = f32[1,5,2048]{2,1,0:T(8,128)} all-reduce(f32[1,5,2048]{2,1,0:T(8,128)S(1)} %constant_dynamic-update-slice_fusion), channel_id=1, replica_groups=mesh['seq'=16,'head'=8] {'seq'}, use_global_device_ids=true, to_apply=%region_13.14 | all-reduce | flops 10240 | bytes 81920 | tf_op jit(solution)/shard_map/psum | solution.py:129
  288.4 59.0 %while.39 = (s32[]{:T(128)}, f32[512,1,128]{0,2,1:T(8,128)}, f32[512,1,128]{0,2,1:T(8,128)}, bf16[4,512,1,5,128]{4,1,3,2,0:T(8,128)(2,1)}, bf16[4,512,1,5,128]{4...) while((s32[]{:T(128)}, f32[512,1,128]{0,2,1:T(8,128)}, ...), condition=%wide.region_15.16_spmd.clone, body=%wide.region_14.15_spmd.clone.sunk | while | flops 1688862720 | bytes 73079080 | solution.py:150
  296.5 4.1 fusion.175
  305.9 2.9 fusion.173
  311.2 4.1 fusion.175
  320.6 2.9 fusion.173
  326.0 4.1 fusion.175
  340.8 4.1 fusion.175
  347.5 3.6 copy.121
  356.2 68.9 %reduce-scatter.7.cloned.1.call-done = bf16[128,640]{1,0:T(8,128)(2,1)} async-done(((bf16[2048,640]{1,0:T(8,128)(2,1)}), bf16[128,640]{1,0:T(8,128)(2,1)}) %reduce-scatter.7.cloned.1.call-update) | async-done | bytes 163856
  427.2 61.8 %all-gather.2.cloned.1.call-done = bf16[5120,640]{1,0:T(8,128)(2,1)} async-done(((bf16[320,640]{1,0:T(8,128)(2,1)}), bf16[5120,640]{1,0:T(8,128)(2,1)}) %all-gather.2.cloned.1.call-update) | async-done | bytes 6553616 | tf_op jit(solution)/shard_map/all_gather | solution.py:198
  488.9 5.1 convolution_convert_fusion
  507.0 17.4 %reduce-scatter.9.cloned.1.call-done = bf16[640,128]{1,0:T(8,128)(2,1)} async-done(((bf16[5120,128]{1,0:T(8,128)(2,1)}), bf16[640,128]{1,0:T(8,128)(2,1)}) %reduce-scatter.9.cloned.1.call-update) | async-done | bytes 163856
  (170 shorter events, 91.8 us)
Async XLA Ops:
  7.2 24.3 %copy-start = (bf16[2048,128]{1,0:T(8,128)(2,1)S(1)}, bf16[2048,128]{1,0:T(8,128)(2,1)}, u32[]{:S(2)}) copy-start(bf16[2048,128]{1,0:T(8,128)(2,1)} %param.17) | copy-start | bytes 1572868
  7.2 417.9 %reduce-scatter.7.cloned.1.call-start = ((), (), s32[]{:S(2)}) async-start(), calls=%async_computation.3 | async-start | bytes 2785280
  7.2 24.0 %copy-start.20 = (s32[128]{0:T(128)}, s32[128]{0:T(128)S(1)}, u32[]{:S(2)}) copy-start(s32[128]{0:T(128)S(1)} %get-tuple-element.305) | copy-start | bytes 1540
  7.3 24.0 %copy-start.22 = (s32[128]{0:T(128)}, s32[128]{0:T(128)S(1)}, u32[]{:S(2)}) copy-start(s32[128]{0:T(128)S(1)} %get-tuple-element.306) | copy-start | bytes 1540
  7.3 24.0 %copy-start.16 = (s32[512]{0:T(512)}, s32[512]{0:T(512)S(1)}, u32[]{:S(2)}) copy-start(s32[512]{0:T(512)S(1)} %get-tuple-element.307) | copy-start | bytes 6148
  7.3 24.0 %copy-start.18 = (s32[512]{0:T(512)}, s32[512]{0:T(512)S(1)}, u32[]{:S(2)}) copy-start(s32[512]{0:T(512)S(1)} %get-tuple-element.308) | copy-start | bytes 6148
  10.4 3.9 copy-start.6
  14.2 5.6 %copy-start.2 = (bf16[512,128]{1,0:T(8,128)(2,1)S(1)}, bf16[512,128]{1,0:T(8,128)(2,1)}, u32[]{:S(2)}) copy-start(bf16[512,128]{1,0:T(8,128)(2,1)} %param.15) | copy-start | bytes 393220
  32.8 182.9 %copy-start.3 = (f32[1,5,128,512]{2,3,1,0:T(8,128)}, f32[1,5,128,512]{2,3,1,0:T(8,128)S(1)}, u32[]{:S(2)}) copy-start(f32[1,5,128,512]{2,3,1,0:T(8,128)S(1)} %get-tuple-element.302) | copy-start | bytes 3932164
  178.6 37.0 %copy-start.14 = (f32[5,128]{1,0:T(8,128)}, f32[5,128]{1,0:T(8,128)S(1)}, u32[]{:S(2)}) copy-start(f32[5,128]{1,0:T(8,128)S(1)} %fusion.122) | copy-start | bytes 7684
  178.7 4.5 copy-start.24
  192.3 5.6 %copy-start.7 = (bf16[512,128]{1,0:T(8,128)(2,1)S(1)}, bf16[512,128]{1,0:T(8,128)(2,1)}, u32[]{:S(2)}) copy-start(bf16[512,128]{1,0:T(8,128)(2,1)} %param.16) | copy-start | bytes 393220
  296.5 4.1 copy-start.12
  311.2 4.1 copy-start.12
  319.9 3.7 copy-start.1
  326.0 4.1 copy-start.12
  340.8 4.1 copy-start.12
  353.3 135.7 %all-gather.2.cloned.1.call-start = ((), (), s32[]{:S(2)}) async-start(), calls=%async_computation.2 | async-start | bytes 6963200 | tf_op jit(solution)/shard_map/all_gather | solution.py:198
  354.0 170.4 %reduce-scatter.9.cloned.1.call-start = ((), (), s32[]{:S(2)}) async-start(), calls=%async_computation.4 | async-start | bytes 1474560
  494.1 4.9 copy-start.17
  494.1 4.9 copy-start.19
  494.1 4.9 copy-start.21
  494.1 4.9 copy-start.23
  495.6 6.2 %copy-start.5 = (bf16[2048,640]{0,1:T(8,128)(2,1)S(1)}, bf16[2048,640]{0,1:T(8,128)(2,1)}, u32[]{:S(2)}) copy-start(bf16[2048,640]{0,1:T(8,128)(2,1)} %broadcast_multiply_fusion) | copy-start | bytes 7864324
  (19 other events, 37.8 us)
Sparse Core Ops, SparseCore 0:
  353.4 71.6 reduce-scatter.6
  427.2 61.6 all-gather.1
  495.7 28.6 reduce-scatter.8
where the time goes:
time: 538 us; the launch traced here: 533 us
  blocking collectives  216 us (40%)
  waiting for transfers between devices  149 us (28%)
  matrix products  91.4 us (17%)
  local copies, waits for them, and re-layouts  53.1 us (10%)
  between operations  14.2 us (3%)
  other arithmetic  8.71 us (2%)
    unnamed x5, waiting for transfers between devices  87 us
    pmax x1, blocking collectives, body(): lax.pmax(top_all.astype(jnp.bfloat16), 'seq').astype(top_all.dtype)  75.9 us
    psum x1, blocking collectives, body(): row_delta = lax.psum(partial_delta, 'seq')  70.3 us
    psum x1, blocking collectives, body(): row_total = lax.psum(total_all * jnp.exp(top_all - row_top), 'seq')  69.6 us
    all_gather x1, waiting for transfers between devices, body(): lax.all_gather(query_weight, 'seq', axis=0, tiled=True)  61.8 us
    unnamed x51, local copies, waits for them, and re-layouts  30.4 us
    dot_general x14, matrix products, doc_scores(): jnp.einsum('tkgd,jkd->kgtj', qblock, key_block, preferred_element_type=jn...  29.1 us
    dot_general x9, matrix products, value_prods(): jnp.einsum('tkgd,jkd->kgtj', gblock, value_block, preferred_element_type=...  21.7 us
  transfers between devices with their start and end apart: 3, of which 3 were waited for; matrix products, arithmetic and copies ran while one was open for 3% of the time, Pallas kernels for 0%

commit v1 on v0

v1 whole, which is shorter than its diff:
```python
import math

import jax
import jax.numpy as jnp
from jax import lax
from jax.experimental import pallas as pl
from jax.experimental.pallas import tpu as pltpu
from jax.sharding import PartitionSpec as P

HQ = 40
KVH = 8
HD = 128
L = 512
GROUP = HQ // KVH
FACTOR = HD ** (-0.5)
LOG_FACTOR = FACTOR * math.log2(math.e)
STATS = 16
BF16 = jnp.bfloat16
F32 = jnp.float32


def dot_nt(a, b):
    return lax.dot_general(a, b, (((1,), (1,)), ((), ())), preferred_element_type=F32)


def dot_nn(a, b):
    return lax.dot_general(a, b, (((1,), (0,)), ((), ())), preferred_element_type=F32)


def keep_valid(grads, length, start):
    rows = lax.broadcasted_iota(jnp.int32, grads.shape, 0) + start
    return jnp.where(rows < length, grads, jnp.zeros_like(grads))


def local_stats(scores, dprods):
    top = jnp.max(scores, axis=0, keepdims=True)
    weights = jnp.exp2(scores - top)
    total = jnp.sum(weights, axis=0, keepdims=True)
    mixed = jnp.sum(weights * dprods, axis=0, keepdims=True)
    return top, total, mixed


def stats_kernel(info, q_ref, g_ref, k_ref, v_ref, sk_ref, sv_ref, out_ref, own_ref):
    head = pl.program_id(0)
    slot = info[0]

    @pl.when(head == 0)
    def _():
        out_ref[...] = jnp.zeros_like(out_ref)
        own_ref[...] = jnp.zeros_like(own_ref)

    for block in range(q_ref.shape[0] // L):
        q = q_ref[block * L : (block + 1) * L, :]
        g = keep_valid(g_ref[block * L : (block + 1) * L, :], info[1 + block], 0)
        found = local_stats(dot_nt(k_ref[...], q) * LOG_FACTOR, dot_nt(v_ref[...], g))
        for part in range(L // HD):
            for kind in range(3):
                out_ref[block * (L // HD) + part, pl.ds(kind * GROUP + head, 1), :] = found[kind][
                    :, part * HD : (part + 1) * HD
                ]
    start = lax.rem(slot, L // HD) * HD
    q = q_ref[pl.ds(slot * HD, HD), :]
    g = keep_valid(g_ref[pl.ds(slot * HD, HD), :], info[1 + lax.div(slot, L // HD)], start)
    scores = dot_nt(sk_ref[...], q) * LOG_FACTOR
    keys = lax.broadcasted_iota(jnp.int32, scores.shape, 0)
    rows = lax.broadcasted_iota(jnp.int32, scores.shape, 1) + start
    found = local_stats(jnp.where(keys <= rows, scores, -jnp.inf), dot_nt(sv_ref[...], g))
    for kind in range(3):
        own_ref[pl.ds(kind * GROUP + head, 1), :] = found[kind]


def combine_kernel(parts_ref, own_ref, out_ref):
    parts = parts_ref[...]
    own = own_ref[...]
    top = jnp.maximum(jnp.max(parts[:, :GROUP], axis=0), own[:GROUP])
    own_scale = jnp.exp2(own[:GROUP] - top)
    scale = jnp.exp2(parts[:, :GROUP] - top[None])
    total = own[GROUP : 2 * GROUP] * own_scale + jnp.sum(parts[:, GROUP : 2 * GROUP] * scale, axis=0)
    mixed = own[2 * GROUP : 3 * GROUP] * own_scale + jnp.sum(
        parts[:, 2 * GROUP : 3 * GROUP] * scale, axis=0
    )
    log_sum = top + jnp.log2(total)
    delta = mixed / total
    rest = jnp.zeros((STATS - 2 * GROUP, HD), F32)
    final = jnp.concatenate([log_sum, delta, rest], axis=0)
    out_ref[...] = jnp.broadcast_to(final[None], out_ref.shape)


def score_grads(k, v, q, g, log_sum, delta, allowed=None):
    probs = jnp.exp2(dot_nt(k, q) * LOG_FACTOR - log_sum)
    if allowed is not None:
        probs = jnp.where(allowed, probs, 0.0)
    dscores = (probs * (dot_nt(v, g) - delta)).astype(BF16)
    return probs.astype(BF16), dscores


def grads_kernel(
    info, q_ref, g_ref, k_ref, v_ref, sk_ref, sv_ref, ok_ref, ov_ref, stat_ref,
    dq_ref, dk_ref, dv_ref, dqs_ref, dsk_ref, dsv_ref, kt_ref, skt_ref,
):
    head = pl.program_id(0)
    slot = info[0]
    per = L // HD

    @pl.when(head == 0)
    def _():
        dk_ref[...] = jnp.zeros_like(dk_ref)
        dv_ref[...] = jnp.zeros_like(dv_ref)
        dsk_ref[...] = jnp.zeros_like(dsk_ref)
        dsv_ref[...] = jnp.zeros_like(dsv_ref)
        kt_ref[...] = k_ref[...].T
        skt_ref[...] = sk_ref[...].T

    def row_stats(first, count, offset):
        return jnp.concatenate(
            [stat_ref[first + i, pl.ds(offset + head, 1), :] for i in range(count)], axis=1
        )

    dk = jnp.zeros(dk_ref.shape, F32)
    dv = jnp.zeros(dv_ref.shape, F32)
    for block in range(q_ref.shape[0] // L):
        q = q_ref[block * L : (block + 1) * L, :]
        g = keep_valid(g_ref[block * L : (block + 1) * L, :], info[1 + block], 0)
        log_sum = row_stats(block * per, per, 0)
        delta = row_stats(block * per, per, GROUP)
        probs, dscores = score_grads(k_ref[...], v_ref[...], q, g, log_sum, delta)
        dv = dv + dot_nn(probs, g)
        dk = dk + dot_nn(dscores, q)
        dq = dot_nn(kt_ref[...], dscores) * FACTOR
        dq_ref[block * L : (block + 1) * L, :] = dq.T.astype(BF16)
    dk_ref[...] += dk * FACTOR
    dv_ref[...] += dv

    response = lax.div(slot, per)
    start = lax.rem(slot, per) * HD
    q = q_ref[pl.ds(slot * HD, HD), :]
    g = keep_valid(g_ref[pl.ds(slot * HD, HD), :], info[1 + response], start)
    keys = lax.broadcasted_iota(jnp.int32, (L, HD), 0)
    rows = lax.broadcasted_iota(jnp.int32, (L, HD), 1) + start
    _, dscores = score_grads(
        sk_ref[...], sv_ref[...], q, g, row_stats(slot, 1, 0), row_stats(slot, 1, GROUP), keys <= rows
    )
    dqs_ref[...] = (dot_nn(skt_ref[...], dscores) * FACTOR).T

    q = q_ref[pl.ds(response * L, L), :]
    g = keep_valid(g_ref[pl.ds(response * L, L), :], info[1 + response], 0)
    keys = lax.broadcasted_iota(jnp.int32, (HD, L), 0) + start
    rows = lax.broadcasted_iota(jnp.int32, (HD, L), 1)
    first = response * per
    probs, dscores = score_grads(
        ok_ref[...], ov_ref[...], q, g, row_stats(first, per, 0), row_stats(first, per, GROUP), keys <= rows
    )
    dsk_ref[...] += dot_nn(dscores, q) * FACTOR
    dsv_ref[...] += dot_nn(probs, g)


def project_kernel(parts_ref, own_ref, w_ref, out_ref, dq_ref):
    @pl.when(pl.program_id(0) == 0)
    def _():
        total = own_ref[...]
        for part in range(parts_ref.shape[0]):
            total = total + parts_ref[part].astype(F32)
        dq_ref[...] = total.astype(BF16)

    out_ref[...] = dot_nt(dq_ref[...], w_ref[...])[None].astype(BF16)


def sum_kernel(parts_ref, out_ref):
    total = parts_ref[0].astype(F32)
    for part in range(1, parts_ref.shape[0]):
        total = total + parts_ref[part].astype(F32)
    out_ref[...] = total.astype(BF16)


def params(megabytes=48):
    return pltpu.CompilerParams(
        dimension_semantics=("arbitrary",), vmem_limit_bytes=megabytes * 1024 * 1024
    )


def body(queries, doc_keys, doc_values, self_keys, self_values, out_grads, lengths, query_weight):
    rows_all = queries.shape[0]
    doc_rows = doc_keys.shape[0]
    shards = lax.axis_size("seq")
    groups = lax.axis_size("head")
    own_rows = rows_all // shards
    per = L // own_rows
    slot = lax.axis_index("seq").astype(jnp.int32)
    info = jnp.concatenate([slot[None], lengths.astype(jnp.int32)])
    weight = lax.all_gather(query_weight, "seq", axis=0, tiled=True)

    rows_spec = pl.BlockSpec((rows_all, HD), lambda h, info: (0, h))
    doc_spec = pl.BlockSpec((doc_rows, HD), lambda h, info: (0, 0))
    response_spec = pl.BlockSpec((L, HD), lambda h, info: (info[0] // per, 0))
    own_spec = pl.BlockSpec((own_rows, HD), lambda h, info: (info[0], 0))
    stat_spec = pl.BlockSpec((shards, STATS, HD), lambda h, info: (0, 0, 0))

    stats, own_stats = pl.pallas_call(
        stats_kernel,
        grid_spec=pltpu.PrefetchScalarGridSpec(
            num_scalar_prefetch=1,
            grid=(GROUP,),
            in_specs=[rows_spec, rows_spec, doc_spec, doc_spec, response_spec, response_spec],
            out_specs=[stat_spec, pl.BlockSpec((STATS, HD), lambda h, info: (0, 0))],
        ),
        out_shape=[
            jax.ShapeDtypeStruct((shards, STATS, HD), F32),
            jax.ShapeDtypeStruct((STATS, HD), F32),
        ],
        compiler_params=params(),
        name="local_stats",
    )(info, queries, out_grads, doc_keys, doc_values, self_keys, self_values)
    parts = lax.all_to_all(stats, "seq", 0, 0, tiled=True)
    final = pl.pallas_call(
        combine_kernel,
        out_shape=jax.ShapeDtypeStruct((shards, STATS, HD), F32),
        name="combine_stats",
    )(parts, own_stats)
    final = lax.all_to_all(final, "seq", 0, 0, tiled=True)

    dq, dk, dv, dqs, dsk, dsv = pl.pallas_call(
        grads_kernel,
        grid_spec=pltpu.PrefetchScalarGridSpec(
            num_scalar_prefetch=1,
            grid=(GROUP,),
            in_specs=[
                rows_spec, rows_spec, doc_spec, doc_spec, response_spec, response_spec,
                own_spec, own_spec, stat_spec,
            ],
            out_specs=[
                rows_spec, doc_spec, doc_spec,
                pl.BlockSpec((own_rows, HD), lambda h, info: (0, h)),
                pl.BlockSpec((own_rows, HD), lambda h, info: (0, 0)),
                pl.BlockSpec((own_rows, HD), lambda h, info: (0, 0)),
            ],
            scratch_shapes=[pltpu.VMEM((HD, doc_rows), BF16), pltpu.VMEM((HD, L), BF16)],
        ),
        out_shape=[
            jax.ShapeDtypeStruct((rows_all, GROUP * HD), BF16),
            jax.ShapeDtypeStruct((doc_rows, HD), F32),
            jax.ShapeDtypeStruct((doc_rows, HD), F32),
            jax.ShapeDtypeStruct((own_rows, GROUP * HD), F32),
            jax.ShapeDtypeStruct((own_rows, HD), F32),
            jax.ShapeDtypeStruct((own_rows, HD), F32),
        ],
        compiler_params=params(),
        name="local_grads",
    )(
        info, queries, out_grads, doc_keys, doc_values, self_keys, self_values,
        self_keys, self_values, final,
    )
    width = GROUP * HD
    dq_parts = lax.all_to_all(dq.reshape(shards, own_rows, width), "seq", 0, 0, tiled=True)
    terms = pl.pallas_call(
        project_kernel,
        grid=(groups,),
        in_specs=[
            pl.BlockSpec((shards, own_rows, width), lambda i: (0, 0, 0)),
            pl.BlockSpec((own_rows, width), lambda i: (0, 0)),
            pl.BlockSpec((weight.shape[0] // groups, width), lambda i: (i, 0)),
        ],
        out_specs=pl.BlockSpec((1, own_rows, weight.shape[0] // groups), lambda i: (i, 0, 0)),
        out_shape=jax.ShapeDtypeStruct((groups, own_rows, weight.shape[0] // groups), BF16),
        scratch_shapes=[pltpu.VMEM((own_rows, width), BF16)],
        compiler_params=params(),
        name="project",
    )(dq_parts, dqs, weight)
    terms = lax.all_to_all(terms, "head", 0, 0, tiled=True)
    input_grads = pl.pallas_call(
        sum_kernel,
        out_shape=jax.ShapeDtypeStruct(terms.shape[1:], BF16),
        name="sum_groups",
    )(terms)
    return input_grads, dk, dv, dsk, dsv


def solution(mesh):
    in_specs = (
        P(None, "head"),
        P("seq", "head"),
        P("seq", "head"),
        P(None, "head"),
        P(None, "head"),
        P(None, "head"),
        P(),
        P("seq", "head"),
    )
    out_specs = (
        P("seq", "head"),
        P("seq", "head"),
        P("seq", "head"),
        P("seq", "head"),
        P("seq", "head"),
    )
    return jax.shard_map(body, mesh=mesh, in_specs=in_specs, out_specs=out_specs, check_vma=False)
```

time: 538 us -> 150 us (0.28)
  waiting for transfers between devices: 149 us -> 0.68 us
  blocking collectives: 216 us -> 85.7 us
  matrix products: 91.4 us -> 0 us
  local copies, waits for them, and re-layouts: 53.1 us -> 5.65 us
  Pallas kernels: 0 us -> 41.5 us
  other arithmetic: 8.71 us -> 0.73 us
    psum x2 -> x0, blocking collectives: 140 us -> none  [the longest x1 70.3 us: body(): row_delta = lax.psum(partial_delta, 'seq')]
    dot_general x39 -> x0, matrix products: 91.4 us -> none  [the longest x14 29.1 us: doc_scores(): jnp.einsum('tkgd,jkd->kgtj', qblock, key_block, preferred_element_type=jn...]
    unnamed x5 -> x1, waiting for transfers between devices: 87 us -> 0.68 us
    all_to_all x0 -> x4, blocking collectives: none -> 85.7 us  [the longest x1 34.7 us: body(): lax.all_to_all(dq.reshape(shards, own_rows, width), 'seq', 0, 0, tiled=True)]
    pmax x1 -> x0, blocking collectives: 75.9 us -> none  [body(): lax.pmax(top_all.astype(jnp.bfloat16), 'seq').astype(top_all.dtype)]
    all_gather x1, waiting for transfers between devices: 61.8 us -> 0.01 us  [body(): weight = lax.all_gather(query_weight, 'seq', axis=0, tiled=True)]
    pallas_call x0 -> x5, Pallas kernels: none -> 41.5 us  [the longest x1 19.8 us: body(): pl.pallas_call(grads_kernel, grid_spec=pltpu.PrefetchScalarGridSpec(num_s...]
    unnamed x51 -> x20, local copies, waits for them, and re-layouts: 30.4 us -> 5.65 us
  transfers between devices with their start and end apart: 3 -> 1, of which waited for: 3 -> 0; matrix products, arithmetic and copies ran while one was open for 3% -> 0% of each run, Pallas kernels for 0% -> 22%
where the time goes in v1:
time: 150 us; the launch traced here: 148 us
  blocking collectives  85.7 us (57%)
  Pallas kernels  41.5 us (28%)
  between operations  14.1 us (9%)
  local copies, waits for them, and re-layouts  5.65 us (4%)
    all_to_all x1, blocking collectives, body(): lax.all_to_all(dq.reshape(shards, own_rows, width), 'seq', 0, 0, tiled=True)  34.7 us
    all_to_all x1, blocking collectives, body(): terms = lax.all_to_all(terms, 'head', 0, 0, tiled=True)  22.2 us
    pallas_call x1, Pallas kernels, body(): pl.pallas_call(grads_kernel, grid_spec=pltpu.PrefetchScalarGridSpec(num_s...  19.8 us
    all_to_all x1, blocking collectives, body(): parts = lax.all_to_all(stats, 'seq', 0, 0, tiled=True)  15.9 us
    all_to_all x1, blocking collectives, body(): final = lax.all_to_all(final, 'seq', 0, 0, tiled=True)  12.8 us
    pallas_call x1, Pallas kernels, body(): pl.pallas_call(stats_kernel, grid_spec=pltpu.PrefetchScalarGridSpec(num_s...  11 us
    pallas_call x1, Pallas kernels, body(): pl.pallas_call(project_kernel, grid=(groups,), in_specs=[pl.BlockSpec((sh...  7 us
    unnamed x20, local copies, waits for them, and re-layouts  5.65 us
  transfers between devices with their start and end apart: 1, of which 0 were waited for; matrix products, arithmetic and copies ran while one was open for 0% of the time, Pallas kernels for 22%

profile of v1, /device:TPU:2, one launch (start us, length us, event | category | flops | bytes accessed | tf_op | source)
XLA Modules:
  0.0 148.4 jit_solution(10993837523870603452)
XLA Ops:
  7.2 0.0 all-gather.2.cloned.1.call-start
  7.2 0.7 all-gather.2.cloned.1.call-update
  7.9 0.7 pad_add_fusion.info
  8.6 0.0 copy-start
  8.6 1.7 %copy-done = bf16[2048,640]{1,0:T(8,128)(2,1)S(1)} copy-done((bf16[2048,640]{1,0:T(8,128)(2,1)S(1)}, bf16[2048,640]{1,0:T(8,128)(2,1)}, u32[]{:S(2)}) %copy-start) | copy-done | bytes 2621464
  10.4 1.0 copy-done.1
  11.4 1.0 copy-done.3
  12.5 0.9 copy-done.5
  13.4 0.9 copy-done.7
  14.3 11.0 %local_stats.1 = (f32[16,16,128]{2,1,0:T(8,128)S(1)}, f32[16,128]{1,0:T(8,128)S(1)}) custom-call(s32[5]{0:T(128)S(1)} %pad_add_fusion.info, bf16[2048,640]{1,0:T(8,128)(2,1)S(1)} %copy-done, bf16[2048,640]{1,0:T(8,128)(2,1)} %g_ref.3, bf16[512,128]{1,0:T(8,128)(2,1)S(1)} %copy-done.5, bf16[512,128]{1,0:T(8,128)(2,1)S(1)} %copy-done.7, ...), custom_call_target="tpu_custom_call" | custom-call | tf_op jit(solution)/shard_map/local_stats/pallas_call | solution.py:198
  25.3 0.0 copy-start.9
  25.3 15.9 %all_to_all.20.parts_ref = f32[16,16,128]{2,1,0:T(8,128)} all-to-all(f32[16,16,128]{2,1,0:T(8,128)S(1)} %get-tuple-element.13), channel_id=1, replica_groups=mesh['seq'=16,'head'=8] {'seq'}, dimensions={0} | all-to-all | bytes 262144 | tf_op jit(solution)/shard_map/all_to_all | solution.py:213
  41.2 0.0 copy-done.9
  41.2 1.6 %combine_stats.1 = f32[16,16,128]{2,1,0:T(8,128)} custom-call(f32[16,16,128]{2,1,0:T(8,128)} %all_to_all.20.parts_ref, f32[16,128]{1,0:T(8,128)} %copy-done.9), custom_call_target="tpu_custom_call" | custom-call | tf_op jit(solution)/shard_map/combine_stats/pallas_call | solution.py:214
  42.8 12.8 %all_to_all.21.stat_ref = f32[16,16,128]{2,1,0:T(8,128)S(1)} all-to-all(f32[16,16,128]{2,1,0:T(8,128)} %combine_stats.1), channel_id=1, replica_groups=mesh['seq'=16,'head'=8] {'seq'}, dimensions={0} | all-to-all | bytes 262144 | tf_op jit(solution)/shard_map/all_to_all | solution.py:219
  55.7 0.0 copy-done.2
  55.7 0.0 copy-done.4
  55.7 0.0 copy-done.6
  55.7 0.0 copy-done.8
  55.7 19.8 %local_grads.1 = (bf16[2048,640]{1,0:T(8,128)(2,1)S(1)}, f32[512,128]{1,0:T(8,128)}, f32[512,128]{1,0:T(8,128)}, f32[128,640]{1,0:T(8,128)S(1)}, f32[128,128]{1,0:T(8,128)}, /*index=5*/f32[128,128]{1,0:T(8,128)}) custom-call(s32[5]{0:T(128)S(1)} %pad_add_fusion.info, bf16[2048,640]{1,0:T(8,128)(2,1)} %q_ref.3, bf16[2048,640]{1,0:T(8,128)(2,1)} %g_ref.3, ...), custom_call_target="tpu_custom_call" | custom-call | tf_op jit(solution)/shard_map/local_grads/pallas_call | solution.py:221
  75.5 34.7 %all_to_all.22.parts_ref = bf16[16,128,640]{2,1,0:T(8,128)(2,1)S(1)} all-to-all(bf16[16,128,640]{2,1,0:T(8,128)(2,1)S(1)} %bitcast.2), channel_id=1, replica_groups=mesh['seq'=16,'head'=8] {'seq'}, dimensions={0} | all-to-all | bytes 5242880 | tf_op jit(solution)/shard_map/all_to_all | solution.py:253
  110.2 7.0 %project.1 = bf16[8,128,640]{2,1,0:T(8,128)(2,1)S(1)} custom-call(bf16[16,128,640]{2,1,0:T(8,128)(2,1)S(1)} %all_to_all.22.parts_ref, f32[128,640]{1,0:T(8,128)S(1)} %get-tuple-element.16.own_ref, bf16[5120,640]{1,0:T(8,128)(2,1)} %all-gather.2.cloned.1.call-done.w_ref), custom_call_target="tpu_custom_call" | custom-call | tf_op jit(solution)/shard_map/project/pallas_call | solution.py:254
  117.2 22.2 %all_to_all.23.parts_ref = bf16[8,128,640]{2,1,0:T(8,128)(2,1)} all-to-all(bf16[8,128,640]{2,1,0:T(8,128)(2,1)S(1)} %project.1), channel_id=1, replica_groups=mesh['seq'=16,'head'=8] {'head'}, dimensions={0} | all-to-all | bytes 2621440 | tf_op jit(solution)/shard_map/all_to_all | solution.py:268
  139.4 2.2 %sum_groups.1 = bf16[128,640]{1,0:T(8,128)(2,1)} custom-call(bf16[8,128,640]{2,1,0:T(8,128)(2,1)} %all_to_all.23.parts_ref), custom_call_target="tpu_custom_call" | custom-call | tf_op jit(solution)/shard_map/sum_groups/pallas_call | solution.py:269
  (9 shorter events, 0.0 us)
Async XLA Ops:
  7.2 103.0 %all-gather.2.cloned.1.call-start = ((), (), s32[]{:S(2)}) async-start(), calls=%async_computation.4 | async-start | bytes 6963200 | tf_op jit(solution)/shard_map/all_gather | solution.py:190
  8.6 1.7 %copy-start = (bf16[2048,640]{1,0:T(8,128)(2,1)S(1)}, bf16[2048,640]{1,0:T(8,128)(2,1)}, u32[]{:S(2)}) copy-start(bf16[2048,640]{1,0:T(8,128)(2,1)} %q_ref.3) | copy-start | bytes 7864324
  10.4 1.0 copy-start.1
  11.4 1.0 copy-start.3
  12.5 0.9 copy-start.5
  13.4 0.9 copy-start.7
  14.3 41.4 %copy-start.2 = (bf16[2048,128]{1,0:T(8,128)(2,1)S(1)}, bf16[2048,128]{1,0:T(8,128)(2,1)}, u32[]{:S(2)}) copy-start(bf16[2048,128]{1,0:T(8,128)(2,1)} %ok_ref.1) | copy-start | bytes 1572868
  14.3 41.4 %copy-start.4 = (bf16[2048,128]{1,0:T(8,128)(2,1)S(1)}, bf16[2048,128]{1,0:T(8,128)(2,1)}, u32[]{:S(2)}) copy-start(bf16[2048,128]{1,0:T(8,128)(2,1)} %ov_ref.1) | copy-start | bytes 1572868
  14.3 41.4 %copy-start.6 = (bf16[512,128]{1,0:T(8,128)(2,1)S(1)}, bf16[512,128]{1,0:T(8,128)(2,1)}, u32[]{:S(2)}) copy-start(bf16[512,128]{1,0:T(8,128)(2,1)} %k_ref.3) | copy-start | bytes 393220
  14.3 41.4 %copy-start.8 = (bf16[512,128]{1,0:T(8,128)(2,1)S(1)}, bf16[512,128]{1,0:T(8,128)(2,1)}, u32[]{:S(2)}) copy-start(bf16[512,128]{1,0:T(8,128)(2,1)} %v_ref.3) | copy-start | bytes 393220
  25.3 16.0 %copy-start.9 = (f32[16,128]{1,0:T(8,128)}, f32[16,128]{1,0:T(8,128)S(1)}, u32[]{:S(2)}) copy-start(f32[16,128]{1,0:T(8,128)S(1)} %get-tuple-element.14.own_ref) | copy-start | bytes 24580
Sparse Core Ops, SparseCore 0:
  10.1 66.6 all-gather.1

commit v2 on v1

v2 whole, which is shorter than its diff:
```python
import functools
import math

import jax
import jax.numpy as jnp
from jax import lax
from jax.experimental import pallas as pl
from jax.experimental.pallas import tpu as pltpu
from jax.sharding import Mesh, PartitionSpec as P

HQ = 40
KVH = 8
HD = 128
L = 512
GROUP = HQ // KVH
WIDTH = GROUP * HD
FACTOR = HD ** (-0.5)
LOG_FACTOR = FACTOR * math.log2(math.e)
STATS = 16
SIDE = 4
LOW = -1e30
BF16 = jnp.bfloat16
F32 = jnp.float32


def dot_nt(a, b):
    return lax.dot_general(a, b, (((1,), (1,)), ((), ())), preferred_element_type=F32)


def dot_nn(a, b):
    return lax.dot_general(a, b, (((1,), (0,)), ((), ())), preferred_element_type=F32)


def load_rows(ref):
    return ref[...].reshape(SIDE * HD, HD)


def load_valid(ref, info):
    pieces = []
    for response in range(SIDE):
        piece = ref[response]
        rows = lax.broadcasted_iota(jnp.int32, piece.shape, 0) + info[1] * HD
        pieces.append(jnp.where(rows < info[2 + response], piece, jnp.zeros_like(piece)))
    return jnp.concatenate(pieces, axis=0)


def load_own(ref, info, masked):
    piece = ref[info[0]]
    if not masked:
        return piece
    rows = lax.broadcasted_iota(jnp.int32, piece.shape, 0) + info[1] * HD
    return jnp.where(rows < info[2 + info[0]], piece, jnp.zeros_like(piece))


def own_lanes(row, info):
    pieces = [row[:, i * HD : (i + 1) * HD] for i in range(SIDE)]
    return sum(jnp.where(info[0] == i, piece, 0.0) for i, piece in enumerate(pieces))


def causal(info):
    keys = lax.broadcasted_iota(jnp.int32, (L, HD), 0)
    rows = lax.broadcasted_iota(jnp.int32, (L, HD), 1) + info[1] * HD
    return keys <= rows


def local_stats(scores, dprods):
    top = jnp.max(scores, axis=0, keepdims=True)
    weights = jnp.exp2(scores - top)
    total = jnp.sum(weights, axis=0, keepdims=True)
    mixed = jnp.sum(weights * dprods, axis=0, keepdims=True)
    return top, total, mixed


def merge(found):
    top = functools.reduce(jnp.maximum, [item[0] for item in found])
    scales = [jnp.exp2(item[0] - top) for item in found]
    total = sum(item[1] * scale for item, scale in zip(found, scales))
    mixed = sum(item[2] * scale for item, scale in zip(found, scales))
    return top, total, mixed


def stats_kernel(chunks, with_self, with_former, info, *refs):
    refs = list(refs)
    q_ref, g_ref = refs[:2]
    key_refs = refs[2 : 2 + chunks]
    value_refs = refs[2 + chunks : 2 + 2 * chunks]
    rest = refs[2 + 2 * chunks :]
    out_ref = rest[-1]
    head = pl.program_id(0)

    @pl.when(head == 0)
    def _():
        out_ref[...] = jnp.zeros_like(out_ref)

    q = load_rows(q_ref)
    g = load_valid(g_ref, info)
    found = [
        local_stats(dot_nt(k[...], q) * LOG_FACTOR, dot_nt(v[...], g))
        for k, v in zip(key_refs, value_refs)
    ]
    if with_self:
        q = load_own(q_ref, info, False)
        g = load_own(g_ref, info, True)
        scores = jnp.where(causal(info), dot_nt(rest[0][...], q) * LOG_FACTOR, -jnp.inf)
        own = local_stats(scores, dot_nt(rest[1][...], g))
        mine = lax.broadcasted_iota(jnp.int32, (1, SIDE * HD), 1) // HD == info[0]
        found.append(
            tuple(
                jnp.where(mine, jnp.concatenate([item] * SIDE, axis=1), other)
                for item, other in zip(own, (LOW, 0.0, 0.0))
            )
        )
    if with_former:
        found.append(tuple(rest[0][pl.ds(kind * GROUP + head, 1), :] for kind in range(3)))
    found = merge(found) if len(found) > 1 else found[0]
    for kind in range(3):
        out_ref[pl.ds(kind * GROUP + head, 1), :] = found[kind]


def score_grads(k, v, q, g, log_sum, delta, allowed=None):
    probs = jnp.exp2(dot_nt(k, q) * LOG_FACTOR - log_sum)
    if allowed is not None:
        probs = jnp.where(allowed, probs, 0.0)
    dscores = (probs * (dot_nt(v, g) - delta)).astype(BF16)
    return probs.astype(BF16), dscores


def grads_kernel(info, *refs):
    q_ref, g_ref = refs[:2]
    key_refs = refs[2:6]
    value_refs = refs[6:10]
    sk_ref, sv_ref = refs[10:12]
    part_refs = refs[12:16]
    dq_ref, dk_ref, dv_ref, dsk_ref, dsv_ref = refs[16:21]
    send_refs = refs[21:24]
    stat_ref, keyt_ref, skt_ref, dkey_ref, dvalue_ref, dself_key_ref, dself_value_ref = refs[24:]
    head = pl.program_id(0)

    @pl.when(head == 0)
    def _():
        parts = [
            tuple(ref[kind * GROUP : (kind + 1) * GROUP, :] for kind in range(3)) for ref in part_refs
        ]
        top, total, mixed = merge(parts)
        stat_ref[:GROUP, :] = top + jnp.log2(total)
        stat_ref[GROUP : 2 * GROUP, :] = mixed / total
        for i in range(SIDE):
            keyt_ref[i] = key_refs[i][...].T
        skt_ref[...] = sk_ref[...].T
        dkey_ref[...] = jnp.zeros_like(dkey_ref)
        dvalue_ref[...] = jnp.zeros_like(dvalue_ref)
        dself_key_ref[...] = jnp.zeros_like(dself_key_ref)
        dself_value_ref[...] = jnp.zeros_like(dself_value_ref)

    log_sum = stat_ref[pl.ds(head, 1), :]
    delta = stat_ref[pl.ds(GROUP + head, 1), :]
    q = load_rows(q_ref)
    g = load_valid(g_ref, info)
    dq = jnp.zeros((HD, SIDE * HD), F32)
    for i in range(SIDE):
        probs, dscores = score_grads(key_refs[i][...], value_refs[i][...], q, g, log_sum, delta)
        dvalue_ref[i] += dot_nn(probs, g)
        dkey_ref[i] += dot_nn(dscores, q)
        dq = dq + dot_nn(keyt_ref[i], dscores)

    q = load_own(q_ref, info, False)
    g = load_own(g_ref, info, True)
    probs, dscores = score_grads(
        sk_ref[...], sv_ref[...], q, g, own_lanes(log_sum, info), own_lanes(delta, info), causal(info)
    )
    dself_value_ref[...] += dot_nn(probs, g)
    dself_key_ref[...] += dot_nn(dscores, q)
    own = dot_nn(skt_ref[...], dscores)
    for response in range(SIDE):
        piece = dq[:, response * HD : (response + 1) * HD]
        piece = piece + jnp.where(response == info[0], own, 0.0)
        dq_ref[response] = (piece * FACTOR).T.astype(BF16)

    @pl.when(head == GROUP - 1)
    def _():
        def self_rows(place):
            return pl.ds(pl.multiple_of(lax.rem(info[1] + place, SIDE) * HD, HD), HD)

        dk_ref[...] = dkey_ref[0] * FACTOR
        dv_ref[...] = dvalue_ref[0]
        dsk_ref[...] = dself_key_ref[self_rows(0), :] * FACTOR
        dsv_ref[...] = dself_value_ref[self_rows(0), :]
        for send_ref, i, place in zip(send_refs, (1, 2, 3), (3, 1, 2)):
            send_ref[:L, :HD] = (dkey_ref[i] * FACTOR).astype(BF16)
            send_ref[:L, HD:] = dvalue_ref[i].astype(BF16)
            send_ref[L:, :HD] = (dself_key_ref[self_rows(place), :] * FACTOR).astype(BF16)
            send_ref[L:, HD:] = dself_value_ref[self_rows(place), :].astype(BF16)


def finish_kernel(dk_ref, dv_ref, dsk_ref, dsv_ref, a_ref, b_ref, c_ref, dk_out, dv_out, dsk_out, dsv_out):
    def total(own_ref, rows, columns):
        return own_ref[...] + sum(ref[rows, columns].astype(F32) for ref in (a_ref, b_ref, c_ref))

    doc, slots = slice(0, L), slice(L, L + HD)
    keys, values = slice(0, HD), slice(HD, 2 * HD)
    dk_out[...] = total(dk_ref, doc, keys)
    dv_out[...] = total(dv_ref, doc, values)
    dsk_out[...] = total(dsk_ref, slots, keys)
    dsv_out[...] = total(dsv_ref, slots, values)


def sum_kernel(parts_ref, out_ref):
    total = parts_ref[0].astype(F32)
    for part in range(1, parts_ref.shape[0]):
        total = total + parts_ref[part].astype(F32)
    out_ref[...] = total.astype(BF16)


def sum_turn_kernel(parts_ref, out_ref):
    total = parts_ref[0].astype(F32)
    for part in range(1, parts_ref.shape[0]):
        total = total + parts_ref[part].astype(F32)
    out_ref[...] = total.T.astype(BF16)


def project_kernel(info, *refs):
    grad_refs = refs[:4]
    weight_refs = refs[4:8]
    mine_ref, theirs_ref = refs[8:10]
    rows_ref = refs[10]
    for i, place in enumerate((0, 3, 1, 2)):
        at = pl.multiple_of(lax.rem(info[0] + place, SIDE) * HD, HD)
        rows_ref[pl.ds(at, HD), :] = grad_refs[i][...]
    depth = weight_refs[0].shape[0]
    for i, place in enumerate((0, 3, 1, 2)):
        block = lax.rem(info[1] + place, SIDE)
        terms = dot_nt(weight_refs[i][...], rows_ref[...]).astype(BF16)
        at = pl.ds(pl.multiple_of(lax.rem(block, 2) * depth, depth), depth)
        same = lax.div(block, 2) == info[2 + SIDE]

        @pl.when(same)
        def _():
            for response in range(SIDE):
                mine_ref[response, at, :] = terms[:, response * HD : (response + 1) * HD]

        @pl.when(jnp.logical_not(same))
        def _():
            for response in range(SIDE):
                theirs_ref[response, at, :] = terms[:, response * HD : (response + 1) * HD]


def params(megabytes=56):
    return pltpu.CompilerParams(vmem_limit_bytes=megabytes * 1024 * 1024)


def ring(step):
    return [(i, (i + step) % SIDE) for i in range(SIDE)]


def spread(array, axis):
    return [lax.ppermute(array, axis, ring(step)) for step in (1, 3, 2)]


def body(queries, doc_keys, doc_values, self_keys, self_values, out_grads, lengths, query_weight):
    doc_rows = doc_keys.shape[0]
    info = jnp.concatenate(
        [
            lax.axis_index("z").astype(jnp.int32)[None],
            lax.axis_index("y").astype(jnp.int32)[None],
            lengths.astype(jnp.int32),
            lax.axis_index("core").astype(jnp.int32)[None],
        ]
    )
    q_four = queries.reshape(SIDE, L, WIDTH)
    g_four = out_grads.reshape(SIDE, L, WIDTH)

    keys_low, values_low = (lax.ppermute(a, "y", ring(1)) for a in (doc_keys, doc_values))
    keys_high, values_high = (lax.ppermute(a, "y", ring(3)) for a in (doc_keys, doc_values))
    keys_far = lax.ppermute(keys_low, "y", ring(1))
    values_far = lax.ppermute(values_high, "y", ring(3))
    weight, _ = lax.optimization_barrier((query_weight, keys_low))
    weights = [query_weight] + spread(weight, "y")

    rows_spec = pl.BlockSpec((SIDE, HD, HD), lambda h, info: (0, info[1], h))
    doc_spec = pl.BlockSpec((doc_rows, HD), lambda h, info: (0, 0))
    response_spec = pl.BlockSpec((L, HD), lambda h, info: (info[0], 0))
    stat_spec = pl.BlockSpec((STATS, SIDE * HD), lambda h, info: (0, 0))
    stat_shape = jax.ShapeDtypeStruct((STATS, SIDE * HD), F32)

    def stats_call(keys, values, own=(), former=()):
        chunks = len(keys)
        elements = chunks * GROUP * SIDE * HD * doc_rows
        return pl.pallas_call(
            functools.partial(stats_kernel, chunks, bool(own), bool(former)),
            grid_spec=pltpu.PrefetchScalarGridSpec(
                num_scalar_prefetch=1,
                grid=(GROUP,),
                in_specs=[rows_spec] * 2
                + [doc_spec] * (2 * chunks)
                + [response_spec] * len(own)
                + [stat_spec] * len(former),
                out_specs=stat_spec,
            ),
            out_shape=stat_shape,
            compiler_params=params(),
            cost_estimate=pl.CostEstimate(
                flops=4 * elements * HD, bytes_accessed=2**21, transcendentals=elements
            ),
            name="local_stats",
        )(info, q_four, g_four, *keys, *values, *own, *former)

    stats = stats_call([doc_keys], [doc_values], own=(self_keys, self_values))
    stats = stats_call([keys_low, keys_high], [values_low, values_high], former=(stats,))
    stats = stats_call([keys_far], [values_far], former=(stats,))
    parts = [stats] + spread(stats, "z")

    elements = GROUP * SIDE * HD * doc_rows * SIDE
    dq, dk, dv, dsk, dsv, *sends = pl.pallas_call(
        grads_kernel,
        grid_spec=pltpu.PrefetchScalarGridSpec(
            num_scalar_prefetch=1,
            grid=(GROUP,),
            in_specs=[rows_spec] * 2 + [doc_spec] * 8 + [response_spec] * 2 + [stat_spec] * 4,
            out_specs=[pl.BlockSpec((SIDE, HD, HD), lambda h, info: (0, 0, h))]
            + [doc_spec] * 2
            + [pl.BlockSpec((HD, HD), lambda h, info: (0, 0))] * 2
            + [pl.BlockSpec((doc_rows + HD, 2 * HD), lambda h, info: (0, 0))] * 3,
            scratch_shapes=[
                pltpu.VMEM((STATS, SIDE * HD), F32),
                pltpu.VMEM((SIDE, HD, doc_rows), BF16),
                pltpu.VMEM((HD, L), BF16),
                pltpu.VMEM((SIDE, doc_rows, HD), F32),
                pltpu.VMEM((SIDE, doc_rows, HD), F32),
                pltpu.VMEM((L, HD), F32),
                pltpu.VMEM((L, HD), F32),
            ],
        ),
        out_shape=[jax.ShapeDtypeStruct((SIDE, HD, WIDTH), BF16)]
        + [jax.ShapeDtypeStruct((doc_rows, HD), F32)] * 2
        + [jax.ShapeDtypeStruct((HD, HD), F32)] * 2
        + [jax.ShapeDtypeStruct((doc_rows + HD, 2 * HD), BF16)] * 3,
        compiler_params=params(),
        cost_estimate=pl.CostEstimate(
            flops=10 * elements * HD, bytes_accessed=2**23, transcendentals=elements
        ),
        name="local_grads",
    )(
        info, q_four, g_four, doc_keys, keys_low, keys_high, keys_far,
        doc_values, values_low, values_high, values_far, self_keys, self_values, *parts,
    )
    backs = [lax.ppermute(a, "y", ring(step)) for a, step in zip(sends, (3, 1, 2))]

    dq_parts = lax.all_to_all(dq, "z", 0, 0, tiled=True)
    dq = pl.pallas_call(
        sum_kernel,
        out_shape=jax.ShapeDtypeStruct((HD, WIDTH), BF16),
        name="sum_shards",
    )(dq_parts)
    grads = [dq] + spread(dq, "z")
    columns = 2 * query_weight.shape[0]
    mine, theirs = pl.pallas_call(
        project_kernel,
        in_specs=[pl.BlockSpec(memory_space=pltpu.SMEM)]
        + [pl.BlockSpec(memory_space=pltpu.VMEM)] * 8,
        out_shape=[jax.ShapeDtypeStruct((SIDE, columns, HD), BF16)] * 2,
        scratch_shapes=[pltpu.VMEM((SIDE * HD, WIDTH), BF16)],
        compiler_params=params(32),
        name="project",
    )(info, *grads, *weights)
    theirs = lax.ppermute(theirs, "core", [(0, 1), (1, 0)])
    terms = (mine.astype(F32) + theirs.astype(F32)).astype(BF16)
    terms = lax.all_to_all(terms, "z", 0, 0, tiled=True)
    terms = lax.all_to_all(terms, "x", 0, 0, tiled=True)
    input_grads = pl.pallas_call(
        sum_turn_kernel,
        out_shape=jax.ShapeDtypeStruct((HD, columns), BF16),
        name="sum_groups",
    )(terms)
    dk, dv, dsk, dsv = pl.pallas_call(
        finish_kernel,
        out_shape=[jax.ShapeDtypeStruct((doc_rows, HD), F32)] * 2
        + [jax.ShapeDtypeStruct((HD, HD), F32)] * 2,
        name="sum_key_values",
    )(dk, dv, dsk, dsv, *backs)
    return input_grads, dk, dv, dsk, dsv


def solution(mesh):
    grid = Mesh(mesh.devices.reshape(SIDE, SIDE, SIDE, 2), ("z", "y", "x", "core"))
    seq, head = ("z", "y"), ("x", "core")
    in_specs = (
        P(None, head),
        P(seq, head),
        P(seq, head),
        P(None, head),
        P(None, head),
        P(None, head),
        P(),
        P(seq, head),
    )
    return jax.shard_map(
        body, mesh=grid, in_specs=in_specs, out_specs=(P(seq, head),) * 5, check_vma=False
    )
```

time: 150 us -> 142 us (0.947)
  blocking collectives: 85.7 us -> 14.7 us
  waiting for transfers between devices: 0.68 us -> 35.4 us
  starting transfers between devices: 0.04 us -> 33 us
  between operations: 14.1 us -> 0.81 us
  Pallas kernels: 41.5 us -> 49 us
    all_to_all x4 -> x1, blocking collectives: 85.7 us -> 14.7 us  [body(): terms = lax.all_to_all(terms, 'z', 0, 0, tiled=True)]
    ppermute x0 -> x19, waiting for transfers between devices: none -> 29.9 us  [the longest x3 14.6 us: body(): lax.ppermute(a, 'y', ring(step))]
    ppermute x0 -> x19, starting transfers between devices: none -> 24.5 us  [the longest x9 13.5 us: spread(): return [lax.ppermute(array, axis, ring(step)) for step in (1, 3, 2)]]
    all_to_all x0 -> x2, starting transfers between devices: none -> 8.49 us  [the longest x1 4.86 us: body(): terms = lax.all_to_all(terms, 'x', 0, 0, tiled=True)]
    pallas_call x4 -> x7, Pallas kernels: 21.7 us -> 29.3 us  [the longest x3 20.8 us: stats_call(): pl.pallas_call(functools.partial(stats_kernel, chunks, bool(own), bool(fo...]
    all_to_all x0 -> x2, waiting for transfers between devices: none -> 5.43 us  [the longest x1 5.43 us: body(): dq_parts = lax.all_to_all(dq, 'z', 0, 0, tiled=True)]
    unnamed x20 -> x40, local copies, waits for them, and re-layouts: 5.65 us -> 6.64 us
  transfers between devices with their start and end apart: 1 -> 21, of which waited for: 0 -> 11; matrix products, arithmetic and copies ran while one was open for 0% -> 1% of each run, Pallas kernels for 22% -> 13%
where the time goes in v2:
time: 142 us; the launch traced here: 141 us
  Pallas kernels  49 us (35%)
  waiting for transfers between devices  35.4 us (25%)
  starting transfers between devices  33 us (23%)
  blocking collectives  14.7 us (10%)
  local copies, waits for them, and re-layouts  6.64 us (5%)
  other arithmetic  1.48 us (1%)
    pallas_call x3, Pallas kernels, stats_call(): pl.pallas_call(functools.partial(stats_kernel, chunks, bool(own), bool(fo...  20.8 us
    pallas_call x1, Pallas kernels, body(): pl.pallas_call(grads_kernel, grid_spec=pltpu.PrefetchScalarGridSpec(num_s...  19.7 us
    all_to_all x1, blocking collectives, body(): terms = lax.all_to_all(terms, 'z', 0, 0, tiled=True)  14.7 us
    ppermute x3, waiting for transfers between devices, body(): lax.ppermute(a, 'y', ring(step))  14.6 us
    ppermute x9, starting transfers between devices, spread(): return [lax.ppermute(array, axis, ring(step)) for step in (1, 3, 2)]  13.5 us
    ppermute x9, waiting for transfers between devices, spread(): return [lax.ppermute(array, axis, ring(step)) for step in (1, 3, 2)]  12.3 us
    unnamed x40, local copies, waits for them, and re-layouts  6.64 us
    all_to_all x1, waiting for transfers between devices, body(): dq_parts = lax.all_to_all(dq, 'z', 0, 0, tiled=True)  5.43 us
  transfers between devices with their start and end apart: 21, of which 11 were waited for; matrix products, arithmetic and copies ran while one was open for 1% of the time, Pallas kernels for 13%

profile of v2, /device:TPU:2, one launch (start us, length us, event | category | flops | bytes accessed | tf_op | source)
XLA Modules:
  0.0 141.0 jit_solution(7348312616821557947)
XLA Ops:
  8.8 3.0 %collective-permute-start.5 = (bf16[512,128]{1,0:T(8,128)(2,1)S(1)}, bf16[512,128]{1,0:T(8,128)(2,1)S(1)}, u32[]{:S(2)}, u32[]{:S(2)}) collective-permute-start(bf16[512,128]{1,0:T(8,128)(2,1)S(1)} %collective-permute-done.4.refs_5_.refs_8_), channel_id=1, source_target_pairs={{0,24},{8,0},{16,8},{24,16},{1,25},{9,1},{17,9},{25,17},{2,26},{10... | collective-permute-start | bytes 393224 | tf_op jit(solution)/shard_map/ppermute | solution.py:275
  11.8 6.9 %local_stats.3.refs_6_ = f32[16,512]{1,0:T(8,128)} custom-call(s32[7]{0:T(128)} %pad_add_fusion.info, bf16[4,512,640]{2,1,0:T(8,128)(2,1)} %bitcast.5, bf16[4,512,640]{2,1,0:T(8,128)(2,1)} %bitcast.9, bf16[512,128]{1,0:T(8,128)(2,1)} %refs_2_.3, bf16[512,128]{1,0:T(8,128)(2,1)} %refs_6_.1, bf16[2048,128]{1,0:T(8,128)(2,1)} %refs_10_.1, ...), custom_call_target="tpu_custom_call" | custom-call | flops 671088640 | bytes 2097152 | tf_op jit(solution)/shard_map/local_stats/pallas_call | solution.py:288
  20.0 7.7 %local_stats.4.refs_4_ = f32[16,512]{1,0:T(8,128)} custom-call(s32[7]{0:T(128)} %pad_add_fusion.info, bf16[4,512,640]{2,1,0:T(8,128)(2,1)} %bitcast.6, bf16[4,512,640]{2,1,0:T(8,128)(2,1)} %bitcast.10, bf16[512,128]{1,0:T(8,128)(2,1)} %copy-done.8, bf16[512,128]{1,0:T(8,128)(2,1)} %copy-done.10, bf16[512,128]{1,0:T(8,128)(2,1)} %copy-done.11, ...), custom_call_target="tpu_custom_call" | custom-call | flops 1342177280 | bytes 2097152 | tf_op jit(solution)/shard_map/local_stats/pallas_call | solution.py:288
  29.0 6.2 %local_stats.5.refs_12_ = f32[16,512]{1,0:T(8,128)} custom-call(s32[7]{0:T(128)} %pad_add_fusion.info, bf16[4,512,640]{2,1,0:T(8,128)(2,1)} %bitcast.7, bf16[4,512,640]{2,1,0:T(8,128)(2,1)} %bitcast.11, bf16[512,128]{1,0:T(8,128)(2,1)} %copy-done.12, bf16[512,128]{1,0:T(8,128)(2,1)} %copy-done.13, f32[16,512]{1,0:T(8,128)} %local_stats.4.refs_4_), custom_call_target="tpu_custom_call" | custom-call | flops 671088640 | bytes 2097152 | tf_op jit(solution)/shard_map/local_stats/pallas_call | solution.py:288
  35.2 1.9 %collective-permute-start.6 = (f32[16,512]{1,0:T(8,128)}, f32[16,512]{1,0:T(8,128)S(1)}, u32[]{:S(2)}, u32[]{:S(2)}) collective-permute-start(f32[16,512]{1,0:T(8,128)} %local_stats.5.refs_12_), channel_id=1, source_target_pairs={{0,32},{32,64},{64,96},{96,0},{1,33},{33,65},{65,97},{97,1},{2,34}... | collective-permute-start | bytes 98312 | tf_op jit(solution)/shard_map/ppermute | solution.py:256
  37.2 2.1 %collective-permute-start.7 = (f32[16,512]{1,0:T(8,128)}, f32[16,512]{1,0:T(8,128)S(1)}, u32[]{:S(2)}, u32[]{:S(2)}) collective-permute-start(f32[16,512]{1,0:T(8,128)} %local_stats.5.refs_12_), channel_id=1, source_target_pairs={{0,96},{32,0},{64,32},{96,64},{1,97},{33,1},{65,33},{97,65},{2,98}... | collective-permute-start | bytes 98312 | tf_op jit(solution)/shard_map/ppermute | solution.py:256
  39.3 1.9 %collective-permute-start.8 = (f32[16,512]{1,0:T(8,128)}, f32[16,512]{1,0:T(8,128)S(1)}, u32[]{:S(2)}, u32[]{:S(2)}) collective-permute-start(f32[16,512]{1,0:T(8,128)} %local_stats.5.refs_12_), channel_id=1, source_target_pairs={{0,64},{32,96},{64,0},{96,32},{1,65},{33,97},{65,1},{97,33},{2,66}... | collective-permute-start | bytes 98312 | tf_op jit(solution)/shard_map/ppermute | solution.py:256
  41.4 3.5 %collective-permute-done.8.refs_15_ = f32[16,512]{1,0:T(8,128)S(1)} collective-permute-done((f32[16,512]{1,0:T(8,128)}, f32[16,512]{1,0:T(8,128)S(1)}, u32[]{:S(2)}, u32[]{:S(2)}) %collective-permute-start.8) | collective-permute-done | bytes 32800 | tf_op jit(solution)/shard_map/ppermute | solution.py:256
  45.5 19.7 %local_grads.1 = (bf16[4,128,640]{2,1,0:T(8,128)(2,1)}, f32[512,128]{1,0:T(8,128)}, f32[512,128]{1,0:T(8,128)}, f32[128,128]{1,0:T(8,128)}, f32[128,128]{1,0:T(8...) custom-call(s32[7]{0:T(128)} %pad_add_fusion.info, ...), custom_call_target="tpu_custom_call" | custom-call | flops 6710886400 | bytes 8388608 | tf_op jit(solution)/shard_map/local_grads/pallas_call | solution.py:313
  65.2 3.6 %all-to-all-start = ((bf16[4,128,640]{2,1,0:T(8,128)(2,1)}), bf16[4,128,640]{2,1,0:T(8,128)(2,1)S(1)}, u32[]{:S(2)}, u32[]{:S(2)}) async-start(bf16[4,128,640]{2,1,0:T(8,128)(2,1)} %get-tuple-element.20), calls=%async_computation | async-start | bytes 1310720 | tf_op jit(solution)/shard_map/all_to_all | solution.py:348
  68.9 3.2 %collective-permute-start.13 = (bf16[320,640]{1,0:T(8,128)(2,1)S(1)}, bf16[320,640]{1,0:T(8,128)(2,1)S(1)}, u32[]{:S(2)}, u32[]{:S(2)}) collective-permute-start(bf16[320,640]{1,0:T(8,128)(2,1)S(1)} %copy-done.1), channel_id=1, source_target_pairs={{0,24},{8,0},{16,8},{24,16},{1,25},{9,1},{17,9},{25,17},{2,26},{10... | collective-permute-start | bytes 1228808 | tf_op jit(solution)/shard_map/ppermute | solution.py:256
  72.1 5.4 %all-to-all-done.parts_ref = bf16[4,128,640]{2,1,0:T(8,128)(2,1)S(1)} async-done(((bf16[4,128,640]{2,1,0:T(8,128)(2,1)}), bf16[4,128,640]{2,1,0:T(8,128)(2,1)S(1)}, u32[]{:S(2)}, u32[]{:S(2)}) %all-to-all-start) | async-done | bytes 655392 | tf_op jit(solution)/shard_map/all_to_all | solution.py:348
  78.4 1.8 %sum_shards.1.refs_0_ = bf16[128,640]{1,0:T(8,128)(2,1)} custom-call(bf16[4,128,640]{2,1,0:T(8,128)(2,1)} %copy-done.4), custom_call_target="tpu_custom_call" | custom-call | tf_op jit(solution)/shard_map/sum_shards/pallas_call | solution.py:349
  82.9 3.5 %collective-permute-done.12.refs_5_ = bf16[320,640]{1,0:T(8,128)(2,1)S(1)} collective-permute-done((bf16[320,640]{1,0:T(8,128)(2,1)S(1)}, bf16[320,640]{1,0:T(8,128)(2,1)S(1)}, u32[]{:S(2)}, u32[]{:S(2)}) %collective-permute-start.12) | collective-permute-done | bytes 409632 | tf_op jit(solution)/shard_map/ppermute | solution.py:256
  88.4 4.7 %collective-permute-done.9.refs_1_ = bf16[128,640]{1,0:T(8,128)(2,1)S(1)} collective-permute-done((bf16[128,640]{1,0:T(8,128)(2,1)}, bf16[128,640]{1,0:T(8,128)(2,1)S(1)}, u32[]{:S(2)}, u32[]{:S(2)}) %collective-permute-start.9) | collective-permute-done | bytes 163872 | tf_op jit(solution)/shard_map/ppermute | solution.py:256
  94.0 2.5 %project.1 = (bf16[4,640,128]{2,1,0:T(8,128)(2,1)S(1)}, bf16[4,640,128]{2,1,0:T(8,128)(2,1)S(1)}) custom-call(s32[7]{0:T(128)S(1)} %copy-done.2, bf16[128,640]{1,0:T(8,128)(2,1)S(1)} %copy-done, bf16[128,640]{1,0:T(8,128)(2,1)S(1)} %collective-permute-done.9.refs_1_, bf16[128,640]{1,0:T(8,128)(2,1)S(1)} %collective-permute-done.10.refs_2_, ...), custom_call_target="tpu_custom_call" | custom-call | tf_op jit(solution)/shard_map/project/pallas_call | solution.py:356
  96.6 2.1 %collective-permute-done.15 = bf16[4,640,128]{2,1,0:T(8,128)(2,1)S(1)} collective-permute-done((bf16[4,640,128]{2,1,0:T(8,128)(2,1)S(1)}, bf16[4,640,128]{2,1,0:T(8,128)(2,1)S(1)}, u32[]{:S(2)}, u32[]{:S(2)}) %collective-permute-start.15) | collective-permute-done | bytes 655392 | tf_op jit(solution)/shard_map/ppermute | solution.py:365
  98.9 14.7 %all_to_all.15 = bf16[4,640,128]{2,1,0:T(8,128)(2,1)} all-to-all(bf16[4,640,128]{2,1,0:T(8,128)(2,1)S(1)} %add_convert_fusion), channel_id=1, replica_groups=mesh['z'=4,'y'=4,'x'=4,'core'=2] {'z'}, dimensions={0} | all-to-all | bytes 1310720 | tf_op jit(solution)/shard_map/all_to_all | solution.py:367
  113.6 4.9 %all-to-all-start.2 = ((bf16[4,640,128]{2,1,0:T(8,128)(2,1)}), bf16[4,640,128]{2,1,0:T(8,128)(2,1)S(1)}, u32[]{:S(2)}, u32[]{:S(2)}) async-start(bf16[4,640,128]{2,1,0:T(8,128)(2,1)} %all_to_all.15), calls=%async_computation.2 | async-start | bytes 1310720 | tf_op jit(solution)/shard_map/all_to_all | solution.py:368
  118.5 2.0 %collective-permute-start.17 = (bf16[640,256]{1,0:T(8,128)(2,1)S(1)}, bf16[640,256]{1,0:T(8,128)(2,1)S(1)}, u32[]{:S(2)}, u32[]{:S(2)}) collective-permute-start(bf16[640,256]{1,0:T(8,128)(2,1)S(1)} %copy-done.15), channel_id=1, source_target_pairs={{0,8},{8,16},{16,24},{24,0},{1,9},{9,17},{17,25},{25,1},{2,10},{10... | collective-permute-start | bytes 983048 | tf_op jit(solution)/shard_map/ppermute | solution.py:346
  120.5 8.6 %collective-permute-done.16.a_ref = bf16[640,256]{1,0:T(8,128)(2,1)S(1)} collective-permute-done((bf16[640,256]{1,0:T(8,128)(2,1)S(1)}, bf16[640,256]{1,0:T(8,128)(2,1)S(1)}, u32[]{:S(2)}, u32[]{:S(2)}) %collective-permute-start.16) | collective-permute-done | bytes 327712 | tf_op jit(solution)/shard_map/ppermute | solution.py:346
  129.1 6.0 %collective-permute-done.17.b_ref = bf16[640,256]{1,0:T(8,128)(2,1)S(1)} collective-permute-done((bf16[640,256]{1,0:T(8,128)(2,1)S(1)}, bf16[640,256]{1,0:T(8,128)(2,1)S(1)}, u32[]{:S(2)}, u32[]{:S(2)}) %collective-permute-start.17) | collective-permute-done | bytes 327712 | tf_op jit(solution)/shard_map/ppermute | solution.py:346
  136.0 2.3 %sum_key_values.1 = (f32[512,128]{1,0:T(8,128)}, f32[512,128]{1,0:T(8,128)}, f32[128,128]{1,0:T(8,128)}, f32[128,128]{1,0:T(8,128)}) custom-call(f32[512,128]{1,0:T(8,128)} %get-tuple-element.24.dk_ref, f32[512,128]{1,0:T(8,128)} %get-tuple-element.25.dv_ref, f32[128,128]{1,0:T(8,128)} %get-tuple-element.26.dsk_ref, f32[128,128]{1,0:T(8,128)} %get-tuple-element.27.dsv_ref, ...), custom_call_target="tpu_custom_call" | custom-call | tf_op jit(solution)/shard_map/sum_key_values/pallas_call | solution.py:374
  139.1 1.9 %sum_groups.1 = bf16[128,640]{1,0:T(8,128)(2,1)} custom-call(bf16[4,640,128]{2,1,0:T(8,128)(2,1)} %copy-done.3), custom_call_target="tpu_custom_call" | custom-call | tf_op jit(solution)/shard_map/sum_groups/pallas_call | solution.py:369
  (69 shorter events, 20.1 us)
Async XLA Ops:
  0.6 6.8 %collective-permute-start = (bf16[512,128]{1,0:T(8,128)(2,1)}, bf16[512,128]{1,0:T(8,128)(2,1)S(1)}, u32[]{:S(2)}, u32[]{:S(2)}) collective-permute-start(bf16[512,128]{1,0:T(8,128)(2,1)} %refs_2_.3), channel_id=1, source_target_pairs={{0,8},{8,16},{16,24},{24,0},{1,9},{9,17},{17,25},{25,1},{2,10},{10... | collective-permute-start | bytes 393224 | tf_op jit(solution)/shard_map/ppermute | solution.py:272
  2.3 6.5 %collective-permute-start.4 = (bf16[512,128]{1,0:T(8,128)(2,1)}, bf16[512,128]{1,0:T(8,128)(2,1)S(1)}, u32[]{:S(2)}, u32[]{:S(2)}) collective-permute-start(bf16[512,128]{1,0:T(8,128)(2,1)} %refs_6_.1), channel_id=1, source_target_pairs={{0,24},{8,0},{16,8},{24,16},{1,25},{9,1},{17,9},{25,17},{2,26},{10... | collective-permute-start | bytes 393224 | tf_op jit(solution)/shard_map/ppermute | solution.py:273
  3.9 14.7 %collective-permute-start.1 = (bf16[512,128]{1,0:T(8,128)(2,1)}, bf16[512,128]{1,0:T(8,128)(2,1)S(1)}, u32[]{:S(2)}, u32[]{:S(2)}) collective-permute-start(bf16[512,128]{1,0:T(8,128)(2,1)} %refs_2_.3), channel_id=1, source_target_pairs={{0,24},{8,0},{16,8},{24,16},{1,25},{9,1},{17,9},{25,17},{2,26},{10... | collective-permute-start | bytes 393224 | tf_op jit(solution)/shard_map/ppermute | solution.py:273
  5.7 12.9 %collective-permute-start.3 = (bf16[512,128]{1,0:T(8,128)(2,1)}, bf16[512,128]{1,0:T(8,128)(2,1)S(1)}, u32[]{:S(2)}, u32[]{:S(2)}) collective-permute-start(bf16[512,128]{1,0:T(8,128)(2,1)} %refs_6_.1), channel_id=1, source_target_pairs={{0,8},{8,16},{16,24},{24,0},{1,9},{9,17},{17,25},{25,1},{2,10},{10... | collective-permute-start | bytes 393224 | tf_op jit(solution)/shard_map/ppermute | solution.py:272
  7.4 20.3 %collective-permute-start.2 = (bf16[512,128]{1,0:T(8,128)(2,1)S(1)}, bf16[512,128]{1,0:T(8,128)(2,1)S(1)}, u32[]{:S(2)}, u32[]{:S(2)}) collective-permute-start(bf16[512,128]{1,0:T(8,128)(2,1)S(1)} %collective-permute-done.refs_2_.refs_3_), channel_id=1, source_target_pairs={{0,8},{8,16},{16,24},{24,0},{1,9},{9,17},{17,25},{25,1},{2,10},{10... | collective-permute-start | bytes 393224 | tf_op jit(solution)/shard_map/ppermute | solution.py:274
  8.8 18.9 %collective-permute-start.5 = (bf16[512,128]{1,0:T(8,128)(2,1)S(1)}, bf16[512,128]{1,0:T(8,128)(2,1)S(1)}, u32[]{:S(2)}, u32[]{:S(2)}) collective-permute-start(bf16[512,128]{1,0:T(8,128)(2,1)S(1)} %collective-permute-done.4.refs_5_.refs_8_), channel_id=1, source_target_pairs={{0,24},{8,0},{16,8},{24,16},{1,25},{9,1},{17,9},{25,17},{2,26},{10... | collective-permute-start | bytes 393224 | tf_op jit(solution)/shard_map/ppermute | solution.py:275
  35.2 6.2 %collective-permute-start.6 = (f32[16,512]{1,0:T(8,128)}, f32[16,512]{1,0:T(8,128)S(1)}, u32[]{:S(2)}, u32[]{:S(2)}) collective-permute-start(f32[16,512]{1,0:T(8,128)} %local_stats.5.refs_12_), channel_id=1, source_target_pairs={{0,32},{32,64},{64,96},{96,0},{1,33},{33,65},{65,97},{97,1},{2,34}... | collective-permute-start | bytes 98312 | tf_op jit(solution)/shard_map/ppermute | solution.py:256
  37.2 4.2 %collective-permute-start.7 = (f32[16,512]{1,0:T(8,128)}, f32[16,512]{1,0:T(8,128)S(1)}, u32[]{:S(2)}, u32[]{:S(2)}) collective-permute-start(f32[16,512]{1,0:T(8,128)} %local_stats.5.refs_12_), channel_id=1, source_target_pairs={{0,96},{32,0},{64,32},{96,64},{1,97},{33,1},{65,33},{97,65},{2,98}... | collective-permute-start | bytes 98312 | tf_op jit(solution)/shard_map/ppermute | solution.py:256
  39.3 5.6 %collective-permute-start.8 = (f32[16,512]{1,0:T(8,128)}, f32[16,512]{1,0:T(8,128)S(1)}, u32[]{:S(2)}, u32[]{:S(2)}) collective-permute-start(f32[16,512]{1,0:T(8,128)} %local_stats.5.refs_12_), channel_id=1, source_target_pairs={{0,64},{32,96},{64,0},{96,32},{1,65},{33,97},{65,1},{97,33},{2,66}... | collective-permute-start | bytes 98312 | tf_op jit(solution)/shard_map/ppermute | solution.py:256
  65.2 27.9 %copy-start.2 = (s32[7]{0:T(128)S(1)}, s32[7]{0:T(128)}, u32[]{:S(2)}) copy-start(s32[7]{0:T(128)} %pad_add_fusion.info) | copy-start | bytes 88
  65.2 12.4 %all-to-all-start = ((bf16[4,128,640]{2,1,0:T(8,128)(2,1)}), bf16[4,128,640]{2,1,0:T(8,128)(2,1)S(1)}, u32[]{:S(2)}, u32[]{:S(2)}) async-start(bf16[4,128,640]{2,1,0:T(8,128)(2,1)} %get-tuple-element.20), calls=%async_computation | async-start | bytes 1310720 | tf_op jit(solution)/shard_map/all_to_all | solution.py:348
  68.8 17.5 %collective-permute-start.12 = (bf16[320,640]{1,0:T(8,128)(2,1)S(1)}, bf16[320,640]{1,0:T(8,128)(2,1)S(1)}, u32[]{:S(2)}, u32[]{:S(2)}) collective-permute-start(bf16[320,640]{1,0:T(8,128)(2,1)S(1)} %copy-done.1), channel_id=1, source_target_pairs={{0,8},{8,16},{16,24},{24,0},{1,9},{9,17},{17,25},{25,1},{2,10},{10... | collective-permute-start | bytes 1228808 | tf_op jit(solution)/shard_map/ppermute | solution.py:256
  68.9 19.1 %collective-permute-start.13 = (bf16[320,640]{1,0:T(8,128)(2,1)S(1)}, bf16[320,640]{1,0:T(8,128)(2,1)S(1)}, u32[]{:S(2)}, u32[]{:S(2)}) collective-permute-start(bf16[320,640]{1,0:T(8,128)(2,1)S(1)} %copy-done.1), channel_id=1, source_target_pairs={{0,24},{8,0},{16,8},{24,16},{1,25},{9,1},{17,9},{25,17},{2,26},{10... | collective-permute-start | bytes 1228808 | tf_op jit(solution)/shard_map/ppermute | solution.py:256
  72.1 15.9 %collective-permute-start.14 = (bf16[320,640]{1,0:T(8,128)(2,1)S(1)}, bf16[320,640]{1,0:T(8,128)(2,1)S(1)}, u32[]{:S(2)}, u32[]{:S(2)}) collective-permute-start(bf16[320,640]{1,0:T(8,128)(2,1)S(1)} %copy-done.1), channel_id=1, source_target_pairs={{0,16},{8,24},{16,0},{24,8},{1,17},{9,25},{17,1},{25,9},{2,18},{10... | collective-permute-start | bytes 1228808 | tf_op jit(solution)/shard_map/ppermute | solution.py:256
  80.2 7.8 %collective-permute-start.10 = (bf16[128,640]{1,0:T(8,128)(2,1)}, bf16[128,640]{1,0:T(8,128)(2,1)S(1)}, u32[]{:S(2)}, u32[]{:S(2)}) collective-permute-start(bf16[128,640]{1,0:T(8,128)(2,1)} %sum_shards.1.refs_0_), channel_id=1, source_target_pairs={{0,96},{32,0},{64,32},{96,64},{1,97},{33,1},{65,33},{97,65},{2,98}... | collective-permute-start | bytes 491528 | tf_op jit(solution)/shard_map/ppermute | solution.py:256
  81.4 7.0 %collective-permute-start.11 = (bf16[128,640]{1,0:T(8,128)(2,1)}, bf16[128,640]{1,0:T(8,128)(2,1)S(1)}, u32[]{:S(2)}, u32[]{:S(2)}) collective-permute-start(bf16[128,640]{1,0:T(8,128)(2,1)} %sum_shards.1.refs_0_), channel_id=1, source_target_pairs={{0,64},{32,96},{64,0},{96,32},{1,65},{33,97},{65,1},{97,33},{2,66}... | collective-permute-start | bytes 491528 | tf_op jit(solution)/shard_map/ppermute | solution.py:256
  86.4 6.7 %collective-permute-start.9 = (bf16[128,640]{1,0:T(8,128)(2,1)}, bf16[128,640]{1,0:T(8,128)(2,1)S(1)}, u32[]{:S(2)}, u32[]{:S(2)}) collective-permute-start(bf16[128,640]{1,0:T(8,128)(2,1)} %sum_shards.1.refs_0_), channel_id=1, source_target_pairs={{0,32},{32,64},{64,96},{96,0},{1,33},{33,65},{65,97},{97,1},{2,34}... | collective-permute-start | bytes 491528 | tf_op jit(solution)/shard_map/ppermute | solution.py:256
  96.5 2.2 %collective-permute-start.15 = (bf16[4,640,128]{2,1,0:T(8,128)(2,1)S(1)}, bf16[4,640,128]{2,1,0:T(8,128)(2,1)S(1)}, u32[]{:S(2)}, u32[]{:S(2)}) collective-permute-start(bf16[4,640,128]{2,1,0:T(8,128)(2,1)S(1)} %get-tuple-element.23), channel_id=1, source_target_pairs={{0,1},{1,0},{2,3},{3,2},{4,5},{5,4},{6,7},{7,6},{8,9},{9,8},{10,11... | collective-permute-start | bytes 1966088 | tf_op jit(solution)/shard_map/ppermute | solution.py:365
  98.9 19.6 %copy-start.16 = (bf16[640,256]{1,0:T(8,128)(2,1)S(1)}, bf16[640,256]{1,0:T(8,128)(2,1)}, u32[]{:S(2)}) copy-start(bf16[640,256]{1,0:T(8,128)(2,1)} %get-tuple-element.28) | copy-start | bytes 983044
  98.9 21.6 %copy-start.14 = (bf16[640,256]{1,0:T(8,128)(2,1)S(1)}, bf16[640,256]{1,0:T(8,128)(2,1)}, u32[]{:S(2)}) copy-start(bf16[640,256]{1,0:T(8,128)(2,1)} %get-tuple-element.30) | copy-start | bytes 983044
  113.6 24.6 %all-to-all-start.2 = ((bf16[4,640,128]{2,1,0:T(8,128)(2,1)}), bf16[4,640,128]{2,1,0:T(8,128)(2,1)S(1)}, u32[]{:S(2)}, u32[]{:S(2)}) async-start(bf16[4,640,128]{2,1,0:T(8,128)(2,1)} %all_to_all.15), calls=%async_computation.2 | async-start | bytes 1310720 | tf_op jit(solution)/shard_map/all_to_all | solution.py:368
  118.4 10.6 %collective-permute-start.16 = (bf16[640,256]{1,0:T(8,128)(2,1)S(1)}, bf16[640,256]{1,0:T(8,128)(2,1)S(1)}, u32[]{:S(2)}, u32[]{:S(2)}) collective-permute-start(bf16[640,256]{1,0:T(8,128)(2,1)S(1)} %copy-done.16), channel_id=1, source_target_pairs={{0,24},{8,0},{16,8},{24,16},{1,25},{9,1},{17,9},{25,17},{2,26},{10... | collective-permute-start | bytes 983048 | tf_op jit(solution)/shard_map/ppermute | solution.py:346
  118.5 16.7 %collective-permute-start.17 = (bf16[640,256]{1,0:T(8,128)(2,1)S(1)}, bf16[640,256]{1,0:T(8,128)(2,1)S(1)}, u32[]{:S(2)}, u32[]{:S(2)}) collective-permute-start(bf16[640,256]{1,0:T(8,128)(2,1)S(1)} %copy-done.15), channel_id=1, source_target_pairs={{0,8},{8,16},{16,24},{24,0},{1,9},{9,17},{17,25},{25,1},{2,10},{10... | collective-permute-start | bytes 983048 | tf_op jit(solution)/shard_map/ppermute | solution.py:346
  120.5 14.6 %collective-permute-start.18 = (bf16[640,256]{1,0:T(8,128)(2,1)S(1)}, bf16[640,256]{1,0:T(8,128)(2,1)S(1)}, u32[]{:S(2)}, u32[]{:S(2)}) collective-permute-start(bf16[640,256]{1,0:T(8,128)(2,1)S(1)} %copy-done.14), channel_id=1, source_target_pairs={{0,16},{8,24},{16,0},{24,8},{1,17},{9,25},{17,1},{25,9},{2,18},{10... | collective-permute-start | bytes 983048 | tf_op jit(solution)/shard_map/ppermute | solution.py:346
  (17 other events, 64.7 us)

commit v3 on v2

v3 whole, which is shorter than its diff:
```python
import functools
import math

import jax
import jax.numpy as jnp
from jax import lax
from jax.experimental import pallas as pl
from jax.experimental.pallas import tpu as pltpu
from jax.sharding import Mesh, PartitionSpec as P

HQ = 40
KVH = 8
HD = 128
L = 512
GROUP = HQ // KVH
WIDTH = GROUP * HD
FACTOR = HD ** (-0.5)
LOG_FACTOR = FACTOR * math.log2(math.e)
STATS = 16
SIDE = 4
LOW = -1e30
BF16 = jnp.bfloat16
F32 = jnp.float32


def dot_nt(a, b):
    return lax.dot_general(a, b, (((1,), (1,)), ((), ())), preferred_element_type=F32)


def dot_nn(a, b):
    return lax.dot_general(a, b, (((1,), (0,)), ((), ())), preferred_element_type=F32)


def load_rows(ref):
    return ref[...].reshape(SIDE * HD, HD)


def load_valid(ref, info):
    pieces = []
    for response in range(SIDE):
        piece = ref[response]
        rows = lax.broadcasted_iota(jnp.int32, piece.shape, 0) + info[1] * HD
        pieces.append(jnp.where(rows < info[2 + response], piece, jnp.zeros_like(piece)))
    return jnp.concatenate(pieces, axis=0)


def load_own(ref, info, masked):
    piece = ref[info[0]]
    if not masked:
        return piece
    rows = lax.broadcasted_iota(jnp.int32, piece.shape, 0) + info[1] * HD
    return jnp.where(rows < info[2 + info[0]], piece, jnp.zeros_like(piece))


def own_lanes(row, info):
    pieces = [row[:, i * HD : (i + 1) * HD] for i in range(SIDE)]
    return sum(jnp.where(info[0] == i, piece, 0.0) for i, piece in enumerate(pieces))


def causal(info):
    keys = lax.broadcasted_iota(jnp.int32, (L, HD), 0)
    rows = lax.broadcasted_iota(jnp.int32, (L, HD), 1) + info[1] * HD
    return keys <= rows


def local_stats(scores, dprods):
    top = jnp.max(scores, axis=0, keepdims=True)
    weights = jnp.exp2(scores - top)
    total = jnp.sum(weights, axis=0, keepdims=True)
    mixed = jnp.sum(weights * dprods, axis=0, keepdims=True)
    return top, total, mixed


def merge(found):
    top = functools.reduce(jnp.maximum, [item[0] for item in found])
    scales = [jnp.exp2(item[0] - top) for item in found]
    total = sum(item[1] * scale for item, scale in zip(found, scales))
    mixed = sum(item[2] * scale for item, scale in zip(found, scales))
    return top, total, mixed


def stats_kernel(info, q_ref, g_ref, key_ref, value_ref, sk_ref, sv_ref, out_ref):
    head = pl.program_id(0)

    @pl.when(head == 0)
    def _():
        out_ref[...] = jnp.zeros_like(out_ref)

    q = load_rows(q_ref)
    g = load_valid(g_ref, info)
    found = [
        local_stats(dot_nt(key_ref[i], q) * LOG_FACTOR, dot_nt(value_ref[i], g)) for i in range(SIDE)
    ]
    q = load_own(q_ref, info, False)
    g = load_own(g_ref, info, True)
    scores = jnp.where(causal(info), dot_nt(sk_ref[...], q) * LOG_FACTOR, -jnp.inf)
    own = local_stats(scores, dot_nt(sv_ref[...], g))
    mine = lax.broadcasted_iota(jnp.int32, (1, SIDE * HD), 1) // HD == info[0]
    found.append(
        tuple(
            jnp.where(mine, jnp.concatenate([item] * SIDE, axis=1), other)
            for item, other in zip(own, (LOW, 0.0, 0.0))
        )
    )
    found = merge(found)
    for copy in range(SIDE):
        for kind in range(3):
            out_ref[copy, pl.ds(kind * GROUP + head, 1), :] = found[kind]


def score_grads(k, v, q, g, log_sum, delta, allowed=None):
    probs = jnp.exp2(dot_nt(k, q) * LOG_FACTOR - log_sum)
    if allowed is not None:
        probs = jnp.where(allowed, probs, 0.0)
    dscores = (probs * (dot_nt(v, g) - delta)).astype(BF16)
    return probs.astype(BF16), dscores


def grads_kernel(
    info, q_ref, g_ref, key_ref, value_ref, sk_ref, sv_ref, part_ref,
    dq_ref, dk_ref, dv_ref, dsk_ref, dsv_ref, send_ref,
    stat_ref, keyt_ref, skt_ref, dkey_ref, dvalue_ref, dself_key_ref, dself_value_ref,
):
    head = pl.program_id(0)

    @pl.when(head == 0)
    def _():
        parts = [
            tuple(part_ref[i, kind * GROUP : (kind + 1) * GROUP, :] for kind in range(3))
            for i in range(SIDE)
        ]
        top, total, mixed = merge(parts)
        stat_ref[:GROUP, :] = top + jnp.log2(total)
        stat_ref[GROUP : 2 * GROUP, :] = mixed / total
        for i in range(SIDE):
            keyt_ref[i] = key_ref[i].T
        skt_ref[...] = sk_ref[...].T
        dkey_ref[...] = jnp.zeros_like(dkey_ref)
        dvalue_ref[...] = jnp.zeros_like(dvalue_ref)
        dself_key_ref[...] = jnp.zeros_like(dself_key_ref)
        dself_value_ref[...] = jnp.zeros_like(dself_value_ref)

    log_sum = stat_ref[pl.ds(head, 1), :]
    delta = stat_ref[pl.ds(GROUP + head, 1), :]
    q = load_rows(q_ref)
    g = load_valid(g_ref, info)
    dq = jnp.zeros((HD, SIDE * HD), F32)
    for i in range(SIDE):
        probs, dscores = score_grads(key_ref[i], value_ref[i], q, g, log_sum, delta)
        dvalue_ref[i] += dot_nn(probs, g)
        dkey_ref[i] += dot_nn(dscores, q)
        dq = dq + dot_nn(keyt_ref[i], dscores)

    q = load_own(q_ref, info, False)
    g = load_own(g_ref, info, True)
    probs, dscores = score_grads(
        sk_ref[...], sv_ref[...], q, g, own_lanes(log_sum, info), own_lanes(delta, info), causal(info)
    )
    dself_value_ref[...] += dot_nn(probs, g)
    dself_key_ref[...] += dot_nn(dscores, q)
    own = dot_nn(skt_ref[...], dscores)
    for response in range(SIDE):
        piece = dq[:, response * HD : (response + 1) * HD]
        piece = piece + jnp.where(response == info[0], own, 0.0)
        dq_ref[response] = (piece * FACTOR).T.astype(BF16)

    @pl.when(head == GROUP - 1)
    def _():
        mine = info[1]
        slots = pl.ds(pl.multiple_of(mine * HD, HD), HD)
        dk_ref[...] = dkey_ref[mine] * FACTOR
        dv_ref[...] = dvalue_ref[mine]
        dsk_ref[...] = dself_key_ref[slots, :] * FACTOR
        dsv_ref[...] = dself_value_ref[slots, :]
        for i in range(SIDE):
            slots = slice(i * HD, (i + 1) * HD)
            send_ref[i, :L, :HD] = (dkey_ref[i] * FACTOR).astype(BF16)
            send_ref[i, :L, HD:] = dvalue_ref[i].astype(BF16)
            send_ref[i, L:, :HD] = (dself_key_ref[slots, :] * FACTOR).astype(BF16)
            send_ref[i, L:, HD:] = dself_value_ref[slots, :].astype(BF16)
        send_ref[mine] = jnp.zeros(send_ref.shape[1:], BF16)


def finish_kernel(dk_ref, dv_ref, dsk_ref, dsv_ref, back_ref, dk_out, dv_out, dsk_out, dsv_out):
    def total(own_ref, rows, columns):
        return own_ref[...] + sum(back_ref[i, rows, columns].astype(F32) for i in range(SIDE))

    doc, slots = slice(0, L), slice(L, L + HD)
    keys, values = slice(0, HD), slice(HD, 2 * HD)
    dk_out[...] = total(dk_ref, doc, keys)
    dv_out[...] = total(dv_ref, doc, values)
    dsk_out[...] = total(dsk_ref, slots, keys)
    dsv_out[...] = total(dsv_ref, slots, values)


def sum_turn_kernel(parts_ref, out_ref):
    total = parts_ref[0].astype(F32)
    for part in range(1, parts_ref.shape[0]):
        total = total + parts_ref[part].astype(F32)
    out_ref[...] = total.T.astype(BF16)


def project_kernel(info, part_ref, weight_ref, theirs_ref, mine_ref, rows_ref):
    step = pl.program_id(0)

    @pl.when(step == 0)
    def _():
        rows_ref[...] = sum(part_ref[i].astype(F32) for i in range(SIDE)).astype(BF16)

    terms = dot_nt(weight_ref[...], rows_ref[...]).astype(BF16)

    @pl.when(step < SIDE)
    def _():
        theirs_ref[0] = terms

    @pl.when(step >= SIDE)
    def _():
        mine_ref[0] = terms


def params(megabytes=56):
    return pltpu.CompilerParams(vmem_limit_bytes=megabytes * 1024 * 1024)


def body(queries, doc_keys, doc_values, self_keys, self_values, out_grads, lengths, query_weight):
    doc_rows = doc_keys.shape[0]
    info = jnp.concatenate(
        [
            lax.axis_index("z").astype(jnp.int32)[None],
            lax.axis_index("y").astype(jnp.int32)[None],
            lengths.astype(jnp.int32),
            lax.axis_index("core").astype(jnp.int32)[None],
        ]
    )
    q_four = queries.reshape(SIDE, L, WIDTH)
    g_four = out_grads.reshape(SIDE, L, WIDTH)

    weight = lax.all_gather(query_weight, ("z", "y"), axis=0, tiled=True)
    pairs = jnp.concatenate([doc_keys, doc_values], axis=1)
    pairs = jnp.broadcast_to(pairs[None], (SIDE, doc_rows, 2 * HD))
    pairs = lax.all_to_all(pairs, "y", 0, 0, tiled=True)

    rows_spec = pl.BlockSpec((SIDE, HD, HD), lambda h, info: (0, info[1], h))
    keys_spec = pl.BlockSpec((SIDE, doc_rows, HD), lambda h, info: (0, 0, 0))
    values_spec = pl.BlockSpec((SIDE, doc_rows, HD), lambda h, info: (0, 0, 1))
    response_spec = pl.BlockSpec((L, HD), lambda h, info: (info[0], 0))
    stat_spec = pl.BlockSpec((SIDE, STATS, SIDE * HD), lambda h, info: (0, 0, 0))
    in_specs = [rows_spec, rows_spec, keys_spec, values_spec, response_spec, response_spec]
    operands = (info, q_four, g_four, pairs, pairs, self_keys, self_values)
    elements = GROUP * SIDE * HD * doc_rows * SIDE

    stats = pl.pallas_call(
        stats_kernel,
        grid_spec=pltpu.PrefetchScalarGridSpec(
            num_scalar_prefetch=1, grid=(GROUP,), in_specs=in_specs, out_specs=stat_spec
        ),
        out_shape=jax.ShapeDtypeStruct((SIDE, STATS, SIDE * HD), F32),
        compiler_params=params(),
        cost_estimate=pl.CostEstimate(
            flops=4 * elements * HD, bytes_accessed=2**22, transcendentals=elements
        ),
        name="local_stats",
    )(*operands)
    parts = lax.all_to_all(stats, "z", 0, 0, tiled=True)

    fixed = lambda *shape: pl.BlockSpec(shape, lambda h, info: (0,) * len(shape))
    dq, dk, dv, dsk, dsv, sends = pl.pallas_call(
        grads_kernel,
        grid_spec=pltpu.PrefetchScalarGridSpec(
            num_scalar_prefetch=1,
            grid=(GROUP,),
            in_specs=in_specs + [stat_spec],
            out_specs=[
                pl.BlockSpec((SIDE, HD, HD), lambda h, info: (0, 0, h)),
                fixed(doc_rows, HD), fixed(doc_rows, HD), fixed(HD, HD), fixed(HD, HD),
                fixed(SIDE, doc_rows + HD, 2 * HD),
            ],
            scratch_shapes=[
                pltpu.VMEM((STATS, SIDE * HD), F32),
                pltpu.VMEM((SIDE, HD, doc_rows), BF16),
                pltpu.VMEM((HD, L), BF16),
                pltpu.VMEM((SIDE, doc_rows, HD), F32),
                pltpu.VMEM((SIDE, doc_rows, HD), F32),
                pltpu.VMEM((L, HD), F32),
                pltpu.VMEM((L, HD), F32),
            ],
        ),
        out_shape=[jax.ShapeDtypeStruct((SIDE, HD, WIDTH), BF16)]
        + [jax.ShapeDtypeStruct((doc_rows, HD), F32)] * 2
        + [jax.ShapeDtypeStruct((HD, HD), F32)] * 2
        + [jax.ShapeDtypeStruct((SIDE, doc_rows + HD, 2 * HD), BF16)],
        compiler_params=params(),
        cost_estimate=pl.CostEstimate(
            flops=10 * elements * HD, bytes_accessed=2**23, transcendentals=elements
        ),
        name="local_grads",
    )(*operands, parts)

    dq_parts = lax.all_to_all(dq, "z", 0, 0, tiled=True)
    back = lax.all_to_all(sends, "y", 0, 0, tiled=True)
    columns = 2 * query_weight.shape[0]

    def weight_block(i, info):
        core = info[2 + SIDE]
        return 2 * lax.rem(i, SIDE) + jnp.where(i < SIDE, 1 - core, core), 0

    theirs, mine = pl.pallas_call(
        project_kernel,
        grid_spec=pltpu.PrefetchScalarGridSpec(
            num_scalar_prefetch=1,
            grid=(2 * SIDE,),
            in_specs=[fixed(SIDE, HD, WIDTH), pl.BlockSpec((columns, WIDTH), weight_block)],
            out_specs=[
                pl.BlockSpec((1, columns, HD), lambda i, info: (jnp.minimum(i, SIDE - 1), 0, 0)),
                pl.BlockSpec((1, columns, HD), lambda i, info: (jnp.maximum(i - SIDE, 0), 0, 0)),
            ],
            scratch_shapes=[pltpu.VMEM((HD, WIDTH), BF16)],
        ),
        out_shape=[jax.ShapeDtypeStruct((SIDE, columns, HD), BF16)] * 2,
        compiler_params=params(),
        name="project",
    )(info, dq_parts, weight)
    theirs = lax.ppermute(theirs, "core", [(0, 1), (1, 0)])
    terms = (mine.astype(F32) + theirs.astype(F32)).astype(BF16)
    terms = lax.all_to_all(terms, "x", 0, 0, tiled=True)
    input_grads = pl.pallas_call(
        sum_turn_kernel,
        out_shape=jax.ShapeDtypeStruct((HD, columns), BF16),
        name="sum_groups",
    )(terms)
    dk, dv, dsk, dsv = pl.pallas_call(
        finish_kernel,
        out_shape=[jax.ShapeDtypeStruct((doc_rows, HD), F32)] * 2
        + [jax.ShapeDtypeStruct((HD, HD), F32)] * 2,
        name="sum_key_values",
    )(dk, dv, dsk, dsv, back)
    return input_grads, dk, dv, dsk, dsv


def solution(mesh):
    grid = Mesh(mesh.devices.reshape(SIDE, SIDE, SIDE, 2), ("z", "y", "x", "core"))
    seq, head = ("z", "y"), ("x", "core")
    in_specs = (
        P(None, head),
        P(seq, head),
        P(seq, head),
        P(None, head),
        P(None, head),
        P(None, head),
        P(),
        P(seq, head),
    )
    return jax.shard_map(
        body, mesh=grid, in_specs=in_specs, out_specs=(P(seq, head),) * 5, check_vma=False
    )
```

time: 142 us -> 136 us (0.958)
  starting transfers between devices: 33 us -> 13 us
  between operations: 0.81 us -> 14.1 us
  blocking collectives: 14.7 us -> 26.1 us
  waiting for transfers between devices: 35.4 us -> 28.4 us
  local copies, waits for them, and re-layouts: 6.64 us -> 2.92 us
  Pallas kernels: 49 us -> 45.9 us
  other arithmetic: 1.48 us -> 3.69 us
    ppermute x18 -> x0, waiting for transfers between devices: 27.8 us -> none  [the longest x3 14.6 us: body(): lax.ppermute(a, 'y', ring(step))]
    ppermute x18 -> x0, starting transfers between devices: 24.5 us -> none  [the longest x9 13.5 us: spread(): return [lax.ppermute(array, axis, ring(step)) for step in (1, 3, 2)]]
    all_to_all x1 -> x2, waiting for transfers between devices: 5.43 us -> 18.1 us  [the longest x1 18.1 us: body(): pairs = lax.all_to_all(pairs, 'y', 0, 0, tiled=True)]
    all_to_all x1 -> x2, blocking collectives: 14.7 us -> 26.1 us  [the longest x1 13 us: body(): parts = lax.all_to_all(stats, 'z', 0, 0, tiled=True)]
    all_to_all x1, waiting for transfers between devices: 0.01 us -> 7.28 us  [body(): terms = lax.all_to_all(terms, 'x', 0, 0, tiled=True)]
    unnamed x40 -> x8, local copies, waits for them, and re-layouts: 6.64 us -> 1.89 us
    all_to_all x1 -> x2, starting transfers between devices: 3.63 us -> 8.13 us  [the longest x1 4.59 us: body(): pairs = lax.all_to_all(pairs, 'y', 0, 0, tiled=True)]
    pallas_call x5 -> x2, Pallas kernels: 25.1 us -> 21.9 us  [the longest x1 13.1 us: body(): pl.pallas_call(stats_kernel, grid_spec=pltpu.PrefetchScalarGridSpec(num_s...]
  transfers between devices with their start and end apart: 21 -> 5, of which waited for: 11 -> 3; matrix products, arithmetic and copies ran while one was open for 1% -> 4% of each run, Pallas kernels for 13% -> 33%
where the time goes in v3:
time: 136 us; the launch traced here: 134 us
  Pallas kernels  45.9 us (34%)
  waiting for transfers between devices  28.4 us (21%)
  blocking collectives  26.1 us (19%)
  between operations  14.1 us (10%)
  starting transfers between devices  13 us (10%)
  other arithmetic  3.69 us (3%)
  local copies, waits for them, and re-layouts  2.92 us (2%)
    pallas_call x1, Pallas kernels, body(): pl.pallas_call(grads_kernel, grid_spec=pltpu.PrefetchScalarGridSpec(num_s...  19.7 us
    all_to_all x1, waiting for transfers between devices, body(): pairs = lax.all_to_all(pairs, 'y', 0, 0, tiled=True)  18.1 us
    pallas_call x1, Pallas kernels, body(): pl.pallas_call(stats_kernel, grid_spec=pltpu.PrefetchScalarGridSpec(num_s...  13.1 us
    all_to_all x1, blocking collectives, body(): parts = lax.all_to_all(stats, 'z', 0, 0, tiled=True)  13 us
    all_to_all x1, blocking collectives, body(): dq_parts = lax.all_to_all(dq, 'z', 0, 0, tiled=True)  13 us
    pallas_call x1, Pallas kernels, body(): pl.pallas_call(project_kernel, grid_spec=pltpu.PrefetchScalarGridSpec(num...  8.79 us
    all_to_all x1, waiting for transfers between devices, body(): terms = lax.all_to_all(terms, 'x', 0, 0, tiled=True)  7.28 us
    all_to_all x1, starting transfers between devices, body(): terms = lax.all_to_all(terms, 'x', 0, 0, tiled=True)  4.83 us
  transfers between devices with their start and end apart: 5, of which 3 were waited for; matrix products, arithmetic and copies ran while one was open for 4% of the time, Pallas kernels for 33%

profile of v3, /device:TPU:2, one launch (start us, length us, event | category | flops | bytes accessed | tf_op | source)
XLA Modules:
  0.0 134.1 jit_solution(12513788552069881743)
XLA Ops:
  7.2 0.0 all-gather.2.cloned.1.call-start
  7.2 0.7 all-gather.2.cloned.1.call-update
  7.9 1.0 pad_maximum_fusion
  8.9 1.0 broadcast_in_dim.18
  9.9 4.6 %all-to-all-start = ((bf16[4,512,256]{2,1,0:T(8,128)(2,1)}), bf16[4,512,256]{2,1,0:T(8,128)(2,1)S(1)}, u32[]{:S(2)}, u32[]{:S(2)}) async-start(bf16[4,512,256]{2,1,0:T(8,128)(2,1)} %broadcast_in_dim.18), calls=%async_computation | async-start | bytes 2097152 | tf_op jit(solution)/shard_map/all_to_all | solution.py:241
  14.5 0.6 pad_add_fusion.info
  15.1 18.1 %all-to-all-done.key_ref.value_ref = bf16[4,512,256]{2,1,0:T(8,128)(2,1)S(1)} async-done(((bf16[4,512,256]{2,1,0:T(8,128)(2,1)}), bf16[4,512,256]{2,1,0:T(8,128)(2,1)S(1)}, u32[]{:S(2)}, u32[]{:S(2)}) %all-to-all-start) | async-done | bytes 1048608 | tf_op jit(solution)/shard_map/all_to_all | solution.py:241
  33.2 1.0 copy-done.2
  34.3 13.1 %local_stats.1 = f32[4,16,512]{2,1,0:T(8,128)} custom-call(s32[7]{0:T(128)} %pad_add_fusion.info, bf16[4,512,640]{2,1,0:T(8,128)(2,1)} %bitcast.5, bf16[4,512,640]{2,1,0:T(8,128)(2,1)} %bitcast.7, bf16[4,512,256]{2,1,0:T(8,128)(2,1)} %copy-done.2, bf16[4,512,256]{2,1,0:T(8,128)(2,1)} %copy-done.2, bf16[2048,128]{1,0:T(8,128)(2,1)} %sk_ref.3, ...), custom_call_target="tpu_custom_call" | custom-call | flops 2684354560 | bytes 4194304 | tf_op jit(solution)/shard_map/local_stats/pallas_call | solution.py:252
  47.4 13.0 %all_to_all.25.part_ref = f32[4,16,512]{2,1,0:T(8,128)} all-to-all(f32[4,16,512]{2,1,0:T(8,128)} %local_stats.1), channel_id=1, replica_groups=mesh['z'=4,'y'=4,'x'=4,'core'=2] {'z'}, dimensions={0} | all-to-all | bytes 262144 | tf_op jit(solution)/shard_map/all_to_all | solution.py:264
  60.4 19.7 %local_grads.1 = (bf16[4,128,640]{2,1,0:T(8,128)(2,1)}, f32[512,128]{1,0:T(8,128)}, f32[512,128]{1,0:T(8,128)}, f32[128,128]{1,0:T(8,128)}, f32[128,128]{1,0:T(8,128)}, /*index=5*/bf16[4,640,256]{2,1,0:T(8,128)(2,1)}) custom-call(s32[7]{0:T(128)} %pad_add_fusion.info, bf16[4,512,640]{2,1,0:T(8,128)(2,1)} %bitcast.6, bf16[4,512,640]{2,1,0:T(8,128)(2,1)} %bitcast.8, ...), custom_call_target="tpu_custom_call" | custom-call | flops 6710886400 | bytes 8388608 | tf_op jit(solution)/shard_map/local_grads/pallas_call | solution.py:267
  80.1 13.0 %all_to_all.26.part_ref = bf16[4,128,640]{2,1,0:T(8,128)(2,1)} all-to-all(bf16[4,128,640]{2,1,0:T(8,128)(2,1)} %get-tuple-element.17), channel_id=1, replica_groups=mesh['z'=4,'y'=4,'x'=4,'core'=2] {'z'}, dimensions={0} | all-to-all | bytes 1310720 | tf_op jit(solution)/shard_map/all_to_all | solution.py:299
  93.1 3.5 %all-to-all-start.4 = ((bf16[4,640,256]{2,1,0:T(8,128)(2,1)}), bf16[4,640,256]{2,1,0:T(8,128)(2,1)S(1)}, u32[]{:S(2)}, u32[]{:S(2)}) async-start(bf16[4,640,256]{2,1,0:T(8,128)(2,1)} %get-tuple-element.24), calls=%async_computation.4 | async-start | bytes 2621440 | tf_op jit(solution)/shard_map/all_to_all | solution.py:300
  96.7 0.0 all-gather.2.cloned.1.call-done.weight_ref
  96.7 8.8 %project.1 = (bf16[4,640,128]{2,1,0:T(8,128)(2,1)}, bf16[4,640,128]{2,1,0:T(8,128)(2,1)}) custom-call(s32[7]{0:T(128)} %pad_add_fusion.info, bf16[4,128,640]{2,1,0:T(8,128)(2,1)} %all_to_all.26.part_ref, bf16[5120,640]{1,0:T(8,128)(2,1)} %all-gather.2.cloned.1.call-done.weight_ref), custom_call_target="tpu_custom_call" | custom-call | tf_op jit(solution)/shard_map/project/pallas_call | solution.py:307
  105.5 0.0 collective-permute-start
  105.5 2.3 %collective-permute-done = bf16[4,640,128]{2,1,0:T(8,128)(2,1)S(1)} collective-permute-done((bf16[4,640,128]{2,1,0:T(8,128)(2,1)}, bf16[4,640,128]{2,1,0:T(8,128)(2,1)S(1)}, u32[]{:S(2)}, u32[]{:S(2)}) %collective-permute-start) | collective-permute-done | bytes 655392 | tf_op jit(solution)/shard_map/ppermute | solution.py:323
  107.8 2.1 %add_convert_fusion = bf16[4,640,128]{2,1,0:T(8,128)(2,1)} fusion(bf16[4,640,128]{2,1,0:T(8,128)(2,1)S(1)} %collective-permute-done, bf16[4,640,128]{2,1,0:T(8,128)(2,1)} %get-tuple-element.18), kind=kLoop, calls=%fused_computation | loop fusion | flops 1310720 | bytes 1966080 | tf_op jit(solution)/shard_map/convert_element_type | solution.py:324
  109.9 0.0 all-to-all-done.4.back_ref
  109.9 4.8 %all-to-all-start.3 = ((bf16[4,640,128]{2,1,0:T(8,128)(2,1)}), bf16[4,640,128]{2,1,0:T(8,128)(2,1)S(1)}, u32[]{:S(2)}, u32[]{:S(2)}) async-start(bf16[4,640,128]{2,1,0:T(8,128)(2,1)} %add_convert_fusion), calls=%async_computation.3 | async-start | bytes 1310720 | tf_op jit(solution)/shard_map/all_to_all | solution.py:325
  114.7 2.4 %sum_key_values.1 = (f32[512,128]{1,0:T(8,128)}, f32[512,128]{1,0:T(8,128)}, f32[128,128]{1,0:T(8,128)}, f32[128,128]{1,0:T(8,128)}) custom-call(f32[512,128]{1,0:T(8,128)} %get-tuple-element.20.dk_ref, f32[512,128]{1,0:T(8,128)} %get-tuple-element.21.dv_ref, f32[128,128]{1,0:T(8,128)} %get-tuple-element.22.dsk_ref, f32[128,128]{1,0:T(8,128)} %get-tuple-element.23.dsv_ref, ...), custom_call_target="tpu_custom_call" | custom-call | tf_op jit(solution)/shard_map/sum_key_values/pallas_call | solution.py:331
  117.2 7.3 %all-to-all-done.3.parts_ref = bf16[4,640,128]{2,1,0:T(8,128)(2,1)S(1)} async-done(((bf16[4,640,128]{2,1,0:T(8,128)(2,1)}), bf16[4,640,128]{2,1,0:T(8,128)(2,1)S(1)}, u32[]{:S(2)}, u32[]{:S(2)}) %all-to-all-start.3) | async-done | bytes 655392 | tf_op jit(solution)/shard_map/all_to_all | solution.py:325
  124.5 0.8 copy-done.1
  125.3 1.9 %sum_groups.1 = bf16[128,640]{1,0:T(8,128)(2,1)} custom-call(bf16[4,640,128]{2,1,0:T(8,128)(2,1)} %copy-done.1), custom_call_target="tpu_custom_call" | custom-call | tf_op jit(solution)/shard_map/sum_groups/pallas_call | solution.py:326
  (6 shorter events, 0.0 us)
Async XLA Ops:
  7.2 89.5 %all-gather.2.cloned.1.call-start = ((), (), s32[]{:S(2)}) async-start(), calls=%async_computation.5 | async-start | bytes 6963200 | tf_op jit(solution)/shard_map/all_gather | solution.py:238
  9.9 4.6 %copy-start.3 = (s32[4]{0:T(128)S(1)}, s32[4]{0:T(128)}, u32[]{:S(2)}) copy-start(s32[4]{0:T(128)} %param.14) | copy-start | bytes 52
  9.9 23.3 %all-to-all-start = ((bf16[4,512,256]{2,1,0:T(8,128)(2,1)}), bf16[4,512,256]{2,1,0:T(8,128)(2,1)S(1)}, u32[]{:S(2)}, u32[]{:S(2)}) async-start(bf16[4,512,256]{2,1,0:T(8,128)(2,1)} %broadcast_in_dim.18), calls=%async_computation | async-start | bytes 2097152 | tf_op jit(solution)/shard_map/all_to_all | solution.py:241
  33.2 1.0 copy-start.2
  93.1 16.8 %all-to-all-start.4 = ((bf16[4,640,256]{2,1,0:T(8,128)(2,1)}), bf16[4,640,256]{2,1,0:T(8,128)(2,1)S(1)}, u32[]{:S(2)}, u32[]{:S(2)}) async-start(bf16[4,640,256]{2,1,0:T(8,128)(2,1)} %get-tuple-element.24), calls=%async_computation.4 | async-start | bytes 2621440 | tf_op jit(solution)/shard_map/all_to_all | solution.py:300
  105.5 2.3 %collective-permute-start = (bf16[4,640,128]{2,1,0:T(8,128)(2,1)}, bf16[4,640,128]{2,1,0:T(8,128)(2,1)S(1)}, u32[]{:S(2)}, u32[]{:S(2)}) collective-permute-start(bf16[4,640,128]{2,1,0:T(8,128)(2,1)} %get-tuple-element.19), channel_id=1, source_target_pairs={{0,1},{1,0},{2,3},{3,2},{4,5},{5,4},{6,7},{7,6},{8,9},{9,8},{10,11... | collective-permute-start | bytes 1966088 | tf_op jit(solution)/shard_map/ppermute | solution.py:323
  109.9 4.8 %copy-start = (bf16[4,640,256]{2,1,0:T(8,128)(2,1)}, bf16[4,640,256]{2,1,0:T(8,128)(2,1)S(1)}, u32[]{:S(2)}) copy-start(bf16[4,640,256]{2,1,0:T(8,128)(2,1)S(1)} %all-to-all-done.4.back_ref) | copy-start | bytes 3932164
  109.9 14.6 %all-to-all-start.3 = ((bf16[4,640,128]{2,1,0:T(8,128)(2,1)}), bf16[4,640,128]{2,1,0:T(8,128)(2,1)S(1)}, u32[]{:S(2)}, u32[]{:S(2)}) async-start(bf16[4,640,128]{2,1,0:T(8,128)(2,1)} %add_convert_fusion), calls=%async_computation.3 | async-start | bytes 1310720 | tf_op jit(solution)/shard_map/all_to_all | solution.py:325
  124.5 0.8 copy-start.1
Sparse Core Ops, SparseCore 0:
  10.1 68.7 all-gather.1

commit v4 on v3

v4 whole, which is shorter than its diff:
```python
import functools
import math

import jax
import jax.numpy as jnp
from jax import lax
from jax.experimental import pallas as pl
from jax.experimental.pallas import tpu as pltpu
from jax.sharding import Mesh, PartitionSpec as P

HQ = 40
KVH = 8
HD = 128
L = 512
GROUP = HQ // KVH
WIDTH = GROUP * HD
FACTOR = HD ** (-0.5)
LOG_FACTOR = FACTOR * math.log2(math.e)
STATS = 16
SIDE = 4
LOW = -1e30
BF16 = jnp.bfloat16
F32 = jnp.float32


def dot_nt(a, b):
    return lax.dot_general(a, b, (((1,), (1,)), ((), ())), preferred_element_type=F32)


def dot_nn(a, b):
    return lax.dot_general(a, b, (((1,), (0,)), ((), ())), preferred_element_type=F32)


def head_lanes(head):
    return pl.ds(pl.multiple_of(head * HD, HD), HD)


def load_head(ref, head):
    return ref[:, :, head_lanes(head)].reshape(SIDE * HD, HD)


def load_own(ref, info):
    own = ref[info[0]]
    return jnp.concatenate([own[:, h * HD : (h + 1) * HD] for h in range(GROUP)], axis=0)


def own_lanes(row, info):
    pieces = [row[:, i * HD : (i + 1) * HD] for i in range(SIDE)]
    return sum(jnp.where(info[0] == i, piece, 0.0) for i, piece in enumerate(pieces))


def response_rows(info):
    return pl.ds(pl.multiple_of(info[0] * L, L), L)


def causal(info):
    keys = lax.broadcasted_iota(jnp.int32, (L, HD), 0)
    rows = lax.broadcasted_iota(jnp.int32, (L, HD), 1) + info[1] * HD
    return jnp.concatenate([keys <= rows] * GROUP, axis=1)


def local_stats(scores, dprods):
    top = jnp.max(scores, axis=0, keepdims=True)
    weights = jnp.exp2(scores - top)
    total = jnp.sum(weights, axis=0, keepdims=True)
    mixed = jnp.sum(weights * dprods, axis=0, keepdims=True)
    return top, total, mixed


def merge(found):
    top = functools.reduce(jnp.maximum, [item[0] for item in found])
    scales = [jnp.exp2(item[0] - top) for item in found]
    total = sum(item[1] * scale for item, scale in zip(found, scales))
    mixed = sum(item[2] * scale for item, scale in zip(found, scales))
    return top, total, mixed


def block_stats(q, g, keys, values):
    return local_stats(dot_nt(keys, q) * LOG_FACTOR, dot_nt(values, g))


def put_stats(ref, head, found):
    for kind in range(3):
        ref[pl.ds(kind * GROUP + head, 1), :] = found[kind]


def get_stats(ref, head):
    return tuple(ref[pl.ds(kind * GROUP + head, 1), :] for kind in range(3))


def own_stats_kernel(info, q_ref, g_ref, key_ref, value_ref, sk_ref, sv_ref, out_ref):
    out_ref[...] = jnp.zeros_like(out_ref)
    scores = dot_nt(sk_ref[response_rows(info), :], load_own(q_ref, info)) * LOG_FACTOR
    scores = jnp.where(causal(info), scores, -jnp.inf)
    own = local_stats(scores, dot_nt(sv_ref[response_rows(info), :], load_own(g_ref, info)))
    mine = lax.broadcasted_iota(jnp.int32, (1, SIDE * HD), 1) // HD == info[0]
    for head in range(GROUP):
        wide = [jnp.concatenate([item[:, head * HD : (head + 1) * HD]] * SIDE, axis=1) for item in own]
        put_stats(out_ref, head, [jnp.where(mine, a, b) for a, b in zip(wide, (LOW, 0.0, 0.0))])

    @pl.loop(0, GROUP)
    def _(head):
        found = block_stats(load_head(q_ref, head), load_head(g_ref, head), key_ref[...], value_ref[...])
        put_stats(out_ref, head, merge([found, get_stats(out_ref, head)]))


def rest_stats_kernel(info, q_ref, g_ref, pair_ref, former_ref, out_ref):
    out_ref[...] = jnp.zeros_like(out_ref)

    @pl.loop(0, GROUP)
    def _(head):
        q, g = load_head(q_ref, head), load_head(g_ref, head)
        found = [get_stats(former_ref, head)]
        for step in range(1, SIDE):
            i = lax.rem(info[1] + step, SIDE)
            found.append(block_stats(q, g, pair_ref[i, :, :HD], pair_ref[i, :, HD:]))
        found = merge(found)
        for copy in range(SIDE):
            put_stats(out_ref.at[copy], head, found)


def score_grads(k, v, q, g, log_sum, delta, allowed=None):
    probs = jnp.exp2(dot_nt(k, q) * LOG_FACTOR - log_sum)
    if allowed is not None:
        probs = jnp.where(allowed, probs, 0.0)
    dscores = (probs * (dot_nt(v, g) - delta)).astype(BF16)
    return probs.astype(BF16), dscores


def grads_kernel(
    info, q_ref, g_ref, pair_ref, sk_ref, sv_ref, part_ref,
    dq_ref, dk_ref, dv_ref, dsk_ref, dsv_ref, send_ref,
    stat_ref, keyt_ref, dkey_ref, dvalue_ref, dself_key_ref, dself_value_ref, dself_query_ref,
):
    parts = [
        tuple(part_ref[i, kind * GROUP : (kind + 1) * GROUP, :] for kind in range(3)) for i in range(SIDE)
    ]
    top, total, mixed = merge(parts)
    stat_ref[:GROUP, :] = top + jnp.log2(total)
    stat_ref[GROUP : 2 * GROUP, :] = mixed / total
    for i in range(SIDE):
        keyt_ref[i] = pair_ref[i, :, :HD].T
    dkey_ref[...] = jnp.zeros_like(dkey_ref)
    dvalue_ref[...] = jnp.zeros_like(dvalue_ref)

    q, g = load_own(q_ref, info), load_own(g_ref, info)
    keys = sk_ref[response_rows(info), :]
    log_sum, delta = (
        jnp.concatenate([own_lanes(stat_ref[first + h : first + h + 1, :], info) for h in range(GROUP)], axis=1)
        for first in (0, GROUP)
    )
    probs, dscores = score_grads(
        keys, sv_ref[response_rows(info), :], q, g, log_sum, delta, causal(info)
    )
    dself_value_ref[...] = dot_nn(probs, g)
    dself_key_ref[...] = dot_nn(dscores, q)
    dself_query_ref[...] = dot_nn(keys.T, dscores)

    @pl.loop(0, GROUP)
    def _(head):
        log_sum = stat_ref[pl.ds(head, 1), :]
        delta = stat_ref[pl.ds(GROUP + head, 1), :]
        q, g = load_head(q_ref, head), load_head(g_ref, head)
        dq = jnp.zeros((HD, SIDE * HD), F32)
        for i in range(SIDE):
            probs, dscores = score_grads(pair_ref[i, :, :HD], pair_ref[i, :, HD:], q, g, log_sum, delta)
            dvalue_ref[i] += dot_nn(probs, g)
            dkey_ref[i] += dot_nn(dscores, q)
            dq = dq + dot_nn(keyt_ref[i], dscores)
        own = dself_query_ref[:, head_lanes(head)]
        for response in range(SIDE):
            piece = dq[:, response * HD : (response + 1) * HD]
            piece = piece + jnp.where(response == info[0], own, 0.0)
            dq_ref[response, :, head_lanes(head)] = (piece * FACTOR).T.astype(BF16)

    mine = info[1]
    slots = pl.ds(pl.multiple_of(mine * HD, HD), HD)
    dk_ref[...] = dkey_ref[mine] * FACTOR
    dv_ref[...] = dvalue_ref[mine]
    dsk_ref[...] = dself_key_ref[slots, :] * FACTOR
    dsv_ref[...] = dself_value_ref[slots, :]
    for i in range(SIDE):
        slots = slice(i * HD, (i + 1) * HD)
        send_ref[i, :L, :HD] = (dkey_ref[i] * FACTOR).astype(BF16)
        send_ref[i, :L, HD:] = dvalue_ref[i].astype(BF16)
        send_ref[i, L:, :HD] = (dself_key_ref[slots, :] * FACTOR).astype(BF16)
        send_ref[i, L:, HD:] = dself_value_ref[slots, :].astype(BF16)
    send_ref[mine] = jnp.zeros(send_ref.shape[1:], BF16)


def finish_kernel(dk_ref, dv_ref, dsk_ref, dsv_ref, back_ref, dk_out, dv_out, dsk_out, dsv_out):
    def total(own_ref, rows, columns):
        return own_ref[...] + sum(back_ref[i, rows, columns].astype(F32) for i in range(SIDE))

    doc, slots = slice(0, L), slice(L, L + HD)
    keys, values = slice(0, HD), slice(HD, 2 * HD)
    dk_out[...] = total(dk_ref, doc, keys)
    dv_out[...] = total(dv_ref, doc, values)
    dsk_out[...] = total(dsk_ref, slots, keys)
    dsv_out[...] = total(dsv_ref, slots, values)


def sum_turn_kernel(parts_ref, out_ref):
    total = parts_ref[0].astype(F32)
    for part in range(1, parts_ref.shape[0]):
        total = total + parts_ref[part].astype(F32)
    out_ref[...] = total.T.astype(BF16)


def project_blocks(weight_hbm, buffer, sems, core, rows, put):
    depth = buffer.shape[1]

    def fetch(i):
        at = pl.ds(pl.multiple_of((2 * i + core) * depth, depth), depth)
        return pltpu.make_async_copy(weight_hbm.at[at], buffer.at[i], sems.at[i])

    for i in range(SIDE):
        fetch(i).start()
    rows = rows()
    for i in range(SIDE):
        fetch(i).wait()
        put(i, dot_nt(buffer[i], rows))


def project_theirs_kernel(info, part_ref, weight_hbm, out_ref, rows_ref, buffer, sems):
    def rows():
        rows_ref[...] = sum(part_ref[i].astype(F32) for i in range(SIDE)).astype(BF16)
        return rows_ref[...]

    def put(i, terms):
        out_ref[i] = terms.astype(BF16)

    project_blocks(weight_hbm, buffer, sems, 1 - info[2], rows, put)


def project_mine_kernel(info, rows_ref, theirs_ref, weight_hbm, out_ref, buffer, sems):
    def put(i, terms):
        out_ref[i] = (terms + theirs_ref[i].astype(F32)).astype(BF16)

    project_blocks(weight_hbm, buffer, sems, info[2], lambda: rows_ref[...], put)


def params(megabytes):
    return pltpu.CompilerParams(vmem_limit_bytes=megabytes * 1024 * 1024)


def body(queries, doc_keys, doc_values, self_keys, self_values, out_grads, lengths, query_weight):
    doc_rows = doc_keys.shape[0]
    place_y = lax.axis_index("y").astype(jnp.int32)
    info = jnp.stack([lax.axis_index("z").astype(jnp.int32), place_y, lax.axis_index("core").astype(jnp.int32)])
    weight = lax.all_gather(query_weight, ("z", "y"), axis=0, tiled=True)
    pairs = jnp.concatenate([doc_keys, doc_values], axis=1)
    pairs = jnp.broadcast_to(pairs[None], (SIDE, doc_rows, 2 * HD))
    pairs = lax.all_to_all(pairs, "y", 0, 0, tiled=True)

    def own_rows(array):
        return lax.dynamic_slice_in_dim(array.reshape(SIDE, L, WIDTH), place_y * HD, HD, 1)

    valid = (jnp.arange(HD, dtype=jnp.int32) + place_y * HD)[None, :] < lengths[:, None]
    q_own = own_rows(queries)
    g_own = own_rows(out_grads) * valid[..., None].astype(out_grads.dtype)

    smem = pl.BlockSpec(memory_space=pltpu.SMEM)
    vmem = pl.BlockSpec(memory_space=pltpu.VMEM)
    anywhere = pl.BlockSpec(memory_space=pl.ANY)
    elements = GROUP * SIDE * HD * doc_rows

    def cost(products, blocks):
        return pl.CostEstimate(
            flops=2 * products * blocks * elements * HD,
            bytes_accessed=2**21,
            transcendentals=blocks * elements,
        )

    stats = pl.pallas_call(
        own_stats_kernel,
        in_specs=[smem] + [vmem] * 6,
        out_specs=vmem,
        out_shape=jax.ShapeDtypeStruct((STATS, SIDE * HD), F32),
        compiler_params=params(20),
        cost_estimate=cost(2, 1),
        name="own_stats",
    )(info, q_own, g_own, doc_keys, doc_values, self_keys, self_values)
    stats = pl.pallas_call(
        rest_stats_kernel,
        in_specs=[smem] + [vmem] * 4,
        out_specs=vmem,
        out_shape=jax.ShapeDtypeStruct((SIDE, STATS, SIDE * HD), F32),
        compiler_params=params(20),
        cost_estimate=cost(2, 3),
        name="rest_stats",
    )(info, q_own, g_own, pairs, stats)
    parts = lax.all_to_all(stats, "z", 0, 0, tiled=True)

    dq, dk, dv, dsk, dsv, sends = pl.pallas_call(
        grads_kernel,
        in_specs=[smem] + [vmem] * 6,
        out_specs=[vmem] * 6,
        scratch_shapes=[
            pltpu.VMEM((STATS, SIDE * HD), F32),
            pltpu.VMEM((SIDE, HD, doc_rows), BF16),
            pltpu.VMEM((SIDE, doc_rows, HD), F32),
            pltpu.VMEM((SIDE, doc_rows, HD), F32),
            pltpu.VMEM((L, HD), F32),
            pltpu.VMEM((L, HD), F32),
            pltpu.VMEM((HD, WIDTH), F32),
        ],
        out_shape=[jax.ShapeDtypeStruct((SIDE, HD, WIDTH), BF16)]
        + [jax.ShapeDtypeStruct((doc_rows, HD), F32)] * 2
        + [jax.ShapeDtypeStruct((HD, HD), F32)] * 2
        + [jax.ShapeDtypeStruct((SIDE, doc_rows + HD, 2 * HD), BF16)],
        compiler_params=params(28),
        cost_estimate=cost(5, SIDE),
        name="local_grads",
    )(info, q_own, g_own, pairs, self_keys, self_values, parts)

    dq_parts = lax.all_to_all(dq, "z", 0, 0, tiled=True)
    back = lax.all_to_all(sends, "y", 0, 0, tiled=True)
    columns = 2 * query_weight.shape[0]
    terms_shape = jax.ShapeDtypeStruct((SIDE, columns, HD), BF16)
    scratch = [pltpu.VMEM((SIDE, columns, WIDTH), BF16), pltpu.SemaphoreType.DMA((SIDE,))]
    project_cost = pl.CostEstimate(
        flops=SIDE * columns * WIDTH * HD * 2, bytes_accessed=2**22, transcendentals=0
    )
    theirs, rows = pl.pallas_call(
        project_theirs_kernel,
        in_specs=[smem, vmem, anywhere],
        out_specs=[vmem] * 2,
        out_shape=[terms_shape, jax.ShapeDtypeStruct((HD, WIDTH), BF16)],
        scratch_shapes=scratch,
        compiler_params=params(24),
        cost_estimate=project_cost,
        name="project_theirs",
    )(info, dq_parts, weight)
    theirs = lax.ppermute(theirs, "core", [(0, 1), (1, 0)])
    terms = pl.pallas_call(
        project_mine_kernel,
        in_specs=[smem, vmem, vmem, anywhere],
        out_specs=vmem,
        out_shape=terms_shape,
        scratch_shapes=scratch,
        compiler_params=params(24),
        cost_estimate=project_cost,
        name="project_mine",
    )(info, rows, theirs, weight)
    terms = lax.all_to_all(terms, "x", 0, 0, tiled=True)
    input_grads = pl.pallas_call(
        sum_turn_kernel,
        out_shape=jax.ShapeDtypeStruct((HD, columns), BF16),
        name="sum_groups",
    )(terms)
    dk, dv, dsk, dsv = pl.pallas_call(
        finish_kernel,
        out_shape=[jax.ShapeDtypeStruct((doc_rows, HD), F32)] * 2
        + [jax.ShapeDtypeStruct((HD, HD), F32)] * 2,
        name="sum_key_values",
    )(dk, dv, dsk, dsv, back)
    return input_grads, dk, dv, dsk, dsv


def solution(mesh):
    grid = Mesh(mesh.devices.reshape(SIDE, SIDE, SIDE, 2), ("z", "y", "x", "core"))
    seq, head = ("z", "y"), ("x", "core")
    in_specs = (
        P(None, head),
        P(seq, head),
        P(seq, head),
        P(None, head),
        P(None, head),
        P(None, head),
        P(),
        P(seq, head),
    )
    return jax.shard_map(
        body, mesh=grid, in_specs=in_specs, out_specs=(P(seq, head),) * 5, check_vma=False
    )
```

time: 136 us -> 128 us (0.941)
  Pallas kernels: 45.9 us -> 38.8 us
  waiting for transfers between devices: 28.4 us -> 23.7 us
  local copies, waits for them, and re-layouts: 2.92 us -> 5.83 us
  blocking collectives: 26.1 us -> 27.6 us
    pallas_call x3 -> x5, Pallas kernels: 41.6 us -> 34.5 us  [the longest x1 17.1 us: body(): pl.pallas_call(grads_kernel, in_specs=[smem] + [vmem] * 6, out_specs=[vme...]
    all_to_all x1, waiting for transfers between devices: 18.1 us -> 12.1 us  [body(): pairs = lax.all_to_all(pairs, 'y', 0, 0, tiled=True)]
    all_to_all x1, waiting for transfers between devices: 0.01 us -> 3.91 us  [body(): back = lax.all_to_all(sends, 'y', 0, 0, tiled=True)]
    unnamed x8 -> x28, local copies, waits for them, and re-layouts: 1.89 us -> 4.79 us
    all_to_all x1, blocking collectives: 13 us -> 15.5 us  [body(): dq_parts = lax.all_to_all(dq, 'z', 0, 0, tiled=True)]
    all_to_all x1, waiting for transfers between devices: 7.28 us -> 4.88 us  [body(): terms = lax.all_to_all(terms, 'x', 0, 0, tiled=True)]
    convert_element_type x1, other arithmetic: 2.1 us -> 0.07 us  [body(): g_own = own_rows(out_grads) * valid[..., None].astype(out_grads.dtype)]
    mul x0 -> x1, other arithmetic: none -> 1.48 us  [body(): g_own = own_rows(out_grads) * valid[..., None].astype(out_grads.dtype)]
  transfers between devices with their start and end apart: 5 -> 5, of which waited for: 3 -> 4; matrix products, arithmetic and copies ran while one was open for 4% -> 3% of each run, Pallas kernels for 33% -> 29%
where the time goes in v4:
time: 128 us; the launch traced here: 126 us
  Pallas kernels  38.8 us (30%)
  blocking collectives  27.6 us (22%)
  waiting for transfers between devices  23.7 us (19%)
  between operations  14.1 us (11%)
  starting transfers between devices  13.5 us (11%)
  local copies, waits for them, and re-layouts  5.83 us (5%)
  other arithmetic  2.63 us (2%)
    pallas_call x1, Pallas kernels, body(): pl.pallas_call(grads_kernel, in_specs=[smem] + [vmem] * 6, out_specs=[vme...  17.1 us
    all_to_all x1, blocking collectives, body(): dq_parts = lax.all_to_all(dq, 'z', 0, 0, tiled=True)  15.5 us
    all_to_all x1, waiting for transfers between devices, body(): pairs = lax.all_to_all(pairs, 'y', 0, 0, tiled=True)  12.1 us
    all_to_all x1, blocking collectives, body(): parts = lax.all_to_all(stats, 'z', 0, 0, tiled=True)  12.1 us
    pallas_call x1, Pallas kernels, body(): pl.pallas_call(rest_stats_kernel, in_specs=[smem] + [vmem] * 4, out_specs...  6.56 us
    all_to_all x1, waiting for transfers between devices, body(): terms = lax.all_to_all(terms, 'x', 0, 0, tiled=True)  4.88 us
    all_to_all x1, starting transfers between devices, body(): terms = lax.all_to_all(terms, 'x', 0, 0, tiled=True)  4.83 us
    unnamed x28, local copies, waits for them, and re-layouts  4.79 us
  transfers between devices with their start and end apart: 5, of which 4 were waited for; matrix products, arithmetic and copies ran while one was open for 3% of the time, Pallas kernels for 29%

profile of v4, /device:TPU:2, one launch (start us, length us, event | category | flops | bytes accessed | tf_op | source)
XLA Modules:
  0.0 126.1 jit_solution(16686758894813933530)
XLA Ops:
  7.2 0.7 all-gather.2.cloned.1.call-update
  7.9 1.0 pad_maximum_fusion
  8.9 1.0 broadcast_in_dim.2
  10.0 4.6 %all-to-all-start = ((bf16[4,512,256]{2,1,0:T(8,128)(2,1)}), bf16[4,512,256]{2,1,0:T(8,128)(2,1)S(1)}, u32[]{:S(2)}, u32[]{:S(2)}) async-start(bf16[4,512,256]{2,1,0:T(8,128)(2,1)} %broadcast_in_dim.2), calls=%async_computation | async-start | bytes 2097152 | tf_op jit(solution)/shard_map/all_to_all | solution.py:254
  14.7 1.5 %dynamic-slice_multiply_fusion = (bf16[4,128,640]{2,1,0:T(8,128)(2,1)S(1)}, bf16[4,128,640]{2,1,0:T(8,128)(2,1)S(1)}) fusion(bf16[4,512,640]{2,1,0:T(8,128)(2,1)} %bitcast.5, s32[]{:T(128)S(6)} %select_n.4, bf16[4,128]{1,0:T(4,128)(2,1)S(1)} %compare_convert_fusion, bf16[4,512,640]{2,1,0:T(8,128)(2,1)} %bitcast.6), kind=kLoop, calls=%fused_computation | loop fusion | flops 1310720 | bytes 2622468 | tf_op jit(solution)/shard_map/mul | solution.py:261
  16.2 1.0 copy-done.5
  17.3 3.9 %own_stats.1.former_ref = f32[16,512]{1,0:T(8,128)S(1)} custom-call(s32[3]{0:T(128)S(1)} %pad_add_fusion.info, bf16[4,128,640]{2,1,0:T(8,128)(2,1)S(1)} %get-tuple-element.30.q_ref, bf16[4,128,640]{2,1,0:T(8,128)(2,1)S(1)} %get-tuple-element.29.g_ref, bf16[512,128]{1,0:T(8,128)(2,1)S(1)} %copy-done.3, bf16[512,128]{1,0:T(8,128)(2,1)S(1)} %copy-done.2, ...), custom_call_target="tpu_custom_call" | custom-call | flops 671088640 | bytes 2097152 | tf_op jit(solution)/shard_map/own_stats/pallas_call | solution.py:275
  21.2 12.1 %all-to-all-done.pair_ref = bf16[4,512,256]{2,1,0:T(8,128)(2,1)S(1)} async-done(((bf16[4,512,256]{2,1,0:T(8,128)(2,1)}), bf16[4,512,256]{2,1,0:T(8,128)(2,1)S(1)}, u32[]{:S(2)}, u32[]{:S(2)}) %all-to-all-start) | async-done | bytes 1048608 | tf_op jit(solution)/shard_map/all_to_all | solution.py:254
  33.3 6.6 %rest_stats.1 = f32[4,16,512]{2,1,0:T(8,128)S(1)} custom-call(s32[3]{0:T(128)S(1)} %pad_add_fusion.info, bf16[4,128,640]{2,1,0:T(8,128)(2,1)S(1)} %get-tuple-element.30.q_ref, bf16[4,128,640]{2,1,0:T(8,128)(2,1)S(1)} %get-tuple-element.29.g_ref, bf16[4,512,256]{2,1,0:T(8,128)(2,1)S(1)} %all-to-all-done.pair_ref, f32[16,512]{1,0:T(8,128)S(1)} %own_stats.1.former_ref), custom_call_target="tpu_custom_call" | custom-call | flops 2013265920 | bytes 2097152 | tf_op jit(solution)/shard_map/rest_stats/pallas_call | solution.py:284
  39.9 12.1 %all_to_all.25.part_ref = f32[4,16,512]{2,1,0:T(8,128)S(1)} all-to-all(f32[4,16,512]{2,1,0:T(8,128)S(1)} %rest_stats.1), channel_id=1, replica_groups=mesh['z'=4,'y'=4,'x'=4,'core'=2] {'z'}, dimensions={0} | all-to-all | bytes 262144 | tf_op jit(solution)/shard_map/all_to_all | solution.py:293
  51.9 17.1 %local_grads.1 = (bf16[4,128,640]{2,1,0:T(8,128)(2,1)S(1)}, f32[512,128]{1,0:T(8,128)S(1)}, f32[512,128]{1,0:T(8,128)S(1)}, f32[128,128]{1,0:T(8,128)S(1)}, f32[...) custom-call(s32[3]{0:T(128)S(1)} %pad_add_fusion.info, bf16[4,128,640]{2,1,0:T(8,128)(2,1)S(1)} %get-tuple-element.30.q_ref, ...), custom_call_target="tpu_custom_call" | custom-call | flops 6710886400 | bytes 2097152 | tf_op jit(solution)/shard_map/local_grads/pallas_call | solution.py:295
  69.1 15.5 %all_to_all.26.part_ref = bf16[4,128,640]{2,1,0:T(8,128)(2,1)S(1)} all-to-all(bf16[4,128,640]{2,1,0:T(8,128)(2,1)S(1)} %get-tuple-element.17), channel_id=1, replica_groups=mesh['z'=4,'y'=4,'x'=4,'core'=2] {'z'}, dimensions={0} | all-to-all | bytes 1310720 | tf_op jit(solution)/shard_map/all_to_all | solution.py:317
  84.6 3.9 %all-to-all-start.4 = ((bf16[4,640,256]{2,1,0:T(8,128)(2,1)}), bf16[4,640,256]{2,1,0:T(8,128)(2,1)S(1)}, u32[]{:S(2)}, u32[]{:S(2)}) async-start(bf16[4,640,256]{2,1,0:T(8,128)(2,1)} %get-tuple-element.24), calls=%async_computation.4 | async-start | bytes 2621440 | tf_op jit(solution)/shard_map/all_to_all | solution.py:318
  88.5 2.9 %copy-done = bf16[5120,640]{1,0:T(8,128)(2,1)S(1)} copy-done((bf16[5120,640]{1,0:T(8,128)(2,1)S(1)}, bf16[5120,640]{1,0:T(8,128)(2,1)}, u32[]{:S(2)}) %copy-start) | copy-done | bytes 6553624
  91.4 3.1 %project_theirs.1 = (bf16[4,640,128]{2,1,0:T(8,128)(2,1)S(1)}, bf16[128,640]{1,0:T(8,128)(2,1)S(1)}) custom-call(s32[3]{0:T(128)S(1)} %pad_add_fusion.info, bf16[4,128,640]{2,1,0:T(8,128)(2,1)S(1)} %all_to_all.26.part_ref, bf16[5120,640]{1,0:T(8,128)(2,1)S(1)} %copy-done), custom_call_target="tpu_custom_call" | custom-call | flops 419430400 | bytes 4194304 | tf_op jit(solution)/shard_map/project_theirs/pallas_call | solution.py:325
  94.4 0.1 collective-permute-start
  94.5 2.1 %collective-permute-done.theirs_ref = bf16[4,640,128]{2,1,0:T(8,128)(2,1)S(1)} collective-permute-done((bf16[4,640,128]{2,1,0:T(8,128)(2,1)S(1)}, bf16[4,640,128]{2,1,0:T(8,128)(2,1)S(1)}, u32[]{:S(2)}, u32[]{:S(2)}) %collective-permute-start) | collective-permute-done | bytes 655392 | tf_op jit(solution)/shard_map/ppermute | solution.py:335
  96.6 3.8 %project_mine.1 = bf16[4,640,128]{2,1,0:T(8,128)(2,1)} custom-call(s32[3]{0:T(128)S(1)} %pad_add_fusion.info, bf16[128,640]{1,0:T(8,128)(2,1)S(1)} %get-tuple-element.18.rows_ref, bf16[4,640,128]{2,1,0:T(8,128)(2,1)S(1)} %collective-permute-done.theirs_ref, bf16[5120,640]{1,0:T(8,128)(2,1)S(1)} %copy-done.1), custom_call_target="tpu_custom_call" | custom-call | flops 419430400 | bytes 4194304 | tf_op jit(solution)/shard_map/project_mine/pallas_call | solution.py:336
  100.4 3.9 %all-to-all-done.4.back_ref = bf16[4,640,256]{2,1,0:T(8,128)(2,1)S(1)} async-done(((bf16[4,640,256]{2,1,0:T(8,128)(2,1)}), bf16[4,640,256]{2,1,0:T(8,128)(2,1)S(1)}, u32[]{:S(2)}, u32[]{:S(2)}) %all-to-all-start.4) | async-done | bytes 1310752 | tf_op jit(solution)/shard_map/all_to_all | solution.py:318
  104.4 4.8 %all-to-all-start.3 = ((bf16[4,640,128]{2,1,0:T(8,128)(2,1)}), bf16[4,640,128]{2,1,0:T(8,128)(2,1)S(1)}, u32[]{:S(2)}, u32[]{:S(2)}) async-start(bf16[4,640,128]{2,1,0:T(8,128)(2,1)} %project_mine.1), calls=%async_computation.3 | async-start | bytes 1310720 | tf_op jit(solution)/shard_map/all_to_all | solution.py:346
  109.2 2.4 %sum_key_values.1 = (f32[512,128]{1,0:T(8,128)}, f32[512,128]{1,0:T(8,128)}, f32[128,128]{1,0:T(8,128)}, f32[128,128]{1,0:T(8,128)}) custom-call(f32[512,128]{1,0:T(8,128)} %copy-done.7, f32[512,128]{1,0:T(8,128)} %copy-done.8, f32[128,128]{1,0:T(8,128)} %copy-done.9, f32[128,128]{1,0:T(8,128)} %copy-done.10, bf16[4,640,256]{2,1,0:T(8,128)(2,1)} %copy-done.11), custom_call_target="tpu_custom_call" | custom-call | tf_op jit(solution)/shard_map/sum_key_values/pallas_call | solution.py:352
  111.6 4.9 %all-to-all-done.3.parts_ref = bf16[4,640,128]{2,1,0:T(8,128)(2,1)S(1)} async-done(((bf16[4,640,128]{2,1,0:T(8,128)(2,1)}), bf16[4,640,128]{2,1,0:T(8,128)(2,1)S(1)}, u32[]{:S(2)}, u32[]{:S(2)}) %all-to-all-start.3) | async-done | bytes 655392 | tf_op jit(solution)/shard_map/all_to_all | solution.py:346
  116.5 0.8 copy-done.12
  117.4 1.9 %sum_groups.1 = bf16[128,640]{1,0:T(8,128)(2,1)} custom-call(bf16[4,640,128]{2,1,0:T(8,128)(2,1)} %copy-done.12), custom_call_target="tpu_custom_call" | custom-call | tf_op jit(solution)/shard_map/sum_groups/pallas_call | solution.py:347
  (30 shorter events, 0.2 us)
Async XLA Ops:
  7.2 7.5 %copy-start.13 = (s32[4]{0:T(128)S(1)}, s32[4]{0:T(128)}, u32[]{:S(2)}) copy-start(s32[4]{0:T(128)} %param.14) | copy-start | bytes 52
  7.2 81.3 %all-gather.2.cloned.1.call-start = ((), (), s32[]{:S(2)}) async-start(), calls=%async_computation.5 | async-start | bytes 6963200 | tf_op jit(solution)/shard_map/all_gather | solution.py:251
  10.0 6.2 %copy-start.2 = (bf16[512,128]{1,0:T(8,128)(2,1)S(1)}, bf16[512,128]{1,0:T(8,128)(2,1)}, u32[]{:S(2)}) copy-start(bf16[512,128]{1,0:T(8,128)(2,1)} %value_ref.1) | copy-start | bytes 393220
  10.0 6.3 %copy-start.3 = (bf16[512,128]{1,0:T(8,128)(2,1)S(1)}, bf16[512,128]{1,0:T(8,128)(2,1)}, u32[]{:S(2)}) copy-start(bf16[512,128]{1,0:T(8,128)(2,1)} %key_ref.1) | copy-start | bytes 393220
  10.0 6.3 %copy-start.4 = (bf16[2048,128]{1,0:T(8,128)(2,1)S(1)}, bf16[2048,128]{1,0:T(8,128)(2,1)}, u32[]{:S(2)}) copy-start(bf16[2048,128]{1,0:T(8,128)(2,1)} %sk_ref.3) | copy-start | bytes 1572868
  10.0 23.3 %all-to-all-start = ((bf16[4,512,256]{2,1,0:T(8,128)(2,1)}), bf16[4,512,256]{2,1,0:T(8,128)(2,1)S(1)}, u32[]{:S(2)}, u32[]{:S(2)}) async-start(bf16[4,512,256]{2,1,0:T(8,128)(2,1)} %broadcast_in_dim.2), calls=%async_computation | async-start | bytes 2097152 | tf_op jit(solution)/shard_map/all_to_all | solution.py:254
  16.2 1.0 copy-start.5
  33.3 18.7 %copy-start.6 = (bf16[2048,128]{1,0:T(8,128)(2,1)S(1)}, bf16[2048,128]{1,0:T(8,128)(2,1)}, u32[]{:S(2)}) copy-start(bf16[2048,128]{1,0:T(8,128)(2,1)} %sv_ref.3) | copy-start | bytes 1572868
  69.1 15.5 %copy-start.7 = (f32[512,128]{1,0:T(8,128)}, f32[512,128]{1,0:T(8,128)S(1)}, u32[]{:S(2)}) copy-start(f32[512,128]{1,0:T(8,128)S(1)} %get-tuple-element.20.dk_ref) | copy-start | bytes 786436
  69.1 15.5 %copy-start.8 = (f32[512,128]{1,0:T(8,128)}, f32[512,128]{1,0:T(8,128)S(1)}, u32[]{:S(2)}) copy-start(f32[512,128]{1,0:T(8,128)S(1)} %get-tuple-element.21.dv_ref) | copy-start | bytes 786436
  69.1 15.5 %copy-start.9 = (f32[128,128]{1,0:T(8,128)}, f32[128,128]{1,0:T(8,128)S(1)}, u32[]{:S(2)}) copy-start(f32[128,128]{1,0:T(8,128)S(1)} %get-tuple-element.22.dsk_ref) | copy-start | bytes 196612
  69.1 15.5 %copy-start.10 = (f32[128,128]{1,0:T(8,128)}, f32[128,128]{1,0:T(8,128)S(1)}, u32[]{:S(2)}) copy-start(f32[128,128]{1,0:T(8,128)S(1)} %get-tuple-element.23.dsv_ref) | copy-start | bytes 196612
  84.6 19.8 %all-to-all-start.4 = ((bf16[4,640,256]{2,1,0:T(8,128)(2,1)}), bf16[4,640,256]{2,1,0:T(8,128)(2,1)S(1)}, u32[]{:S(2)}, u32[]{:S(2)}) async-start(bf16[4,640,256]{2,1,0:T(8,128)(2,1)} %get-tuple-element.24), calls=%async_computation.4 | async-start | bytes 2621440 | tf_op jit(solution)/shard_map/all_to_all | solution.py:318
  88.5 2.9 %copy-start = (bf16[5120,640]{1,0:T(8,128)(2,1)S(1)}, bf16[5120,640]{1,0:T(8,128)(2,1)}, u32[]{:S(2)}) copy-start(bf16[5120,640]{1,0:T(8,128)(2,1)} %all-gather.2.cloned.1.call-done.weight_hbm) | copy-start | bytes 19660804
  91.4 5.3 %copy-start.1 = (bf16[5120,640]{1,0:T(8,128)(2,1)S(1)}, bf16[5120,640]{1,0:T(8,128)(2,1)}, u32[]{:S(2)}) copy-start(bf16[5120,640]{1,0:T(8,128)(2,1)} %all-gather.2.cloned.1.call-done.weight_hbm) | copy-start | bytes 19660804
  94.4 2.2 %collective-permute-start = (bf16[4,640,128]{2,1,0:T(8,128)(2,1)S(1)}, bf16[4,640,128]{2,1,0:T(8,128)(2,1)S(1)}, u32[]{:S(2)}, u32[]{:S(2)}) collective-permute-start(bf16[4,640,128]{2,1,0:T(8,128)(2,1)S(1)} %get-tuple-element.19), channel_id=1, source_target_pairs={{0,1},{1,0},{2,3},{3,2},{4,5},{5,4},{6,7},{7,6},{8,9},{9,8},{10,11... | collective-permute-start | bytes 1966088 | tf_op jit(solution)/shard_map/ppermute | solution.py:335
  104.4 4.8 %copy-start.11 = (bf16[4,640,256]{2,1,0:T(8,128)(2,1)}, bf16[4,640,256]{2,1,0:T(8,128)(2,1)S(1)}, u32[]{:S(2)}) copy-start(bf16[4,640,256]{2,1,0:T(8,128)(2,1)S(1)} %all-to-all-done.4.back_ref) | copy-start | bytes 3932164
  104.4 12.2 %all-to-all-start.3 = ((bf16[4,640,128]{2,1,0:T(8,128)(2,1)}), bf16[4,640,128]{2,1,0:T(8,128)(2,1)S(1)}, u32[]{:S(2)}, u32[]{:S(2)}) async-start(bf16[4,640,128]{2,1,0:T(8,128)(2,1)} %project_mine.1), calls=%async_computation.3 | async-start | bytes 1310720 | tf_op jit(solution)/shard_map/all_to_all | solution.py:346
  116.5 0.8 copy-start.12
Sparse Core Ops, SparseCore 0:
  10.1 74.3 all-gather.1

commit v5 on v4

v5 whole, which is shorter than its diff:
```python
import functools
import math

import jax
import jax.numpy as jnp
from jax import lax
from jax.experimental import pallas as pl
from jax.experimental.pallas import tpu as pltpu
from jax.sharding import Mesh, PartitionSpec as P

HQ = 40
KVH = 8
HD = 128
L = 512
GROUP = HQ // KVH
WIDTH = GROUP * HD
FACTOR = HD ** (-0.5)
LOG_FACTOR = FACTOR * math.log2(math.e)
STATS = 16
SIDE = 4
LOW = -1e30
PLACES = (1, 3, 2)
Z = ("z_high", "z_low")
BF16 = jnp.bfloat16
F32 = jnp.float32


def dot_nt(a, b):
    return lax.dot_general(a, b, (((1,), (1,)), ((), ())), preferred_element_type=F32)


def dot_nn(a, b):
    return lax.dot_general(a, b, (((1,), (0,)), ((), ())), preferred_element_type=F32)


def head_lanes(head):
    return pl.ds(pl.multiple_of(head * HD, HD), HD)


def load_head(ref, head):
    return ref[:, :, head_lanes(head)].reshape(SIDE * HD, HD)


def load_own(ref, info):
    own = ref[info[0]]
    return jnp.concatenate([own[:, h * HD : (h + 1) * HD] for h in range(GROUP)], axis=0)


def own_lanes(row, info):
    pieces = [row[:, i * HD : (i + 1) * HD] for i in range(SIDE)]
    return sum(jnp.where(info[0] == i, piece, 0.0) for i, piece in enumerate(pieces))


def response_rows(info):
    return pl.ds(pl.multiple_of(info[0] * L, L), L)


def causal(info):
    keys = lax.broadcasted_iota(jnp.int32, (L, HD), 0)
    rows = lax.broadcasted_iota(jnp.int32, (L, HD), 1) + info[1] * HD
    return jnp.concatenate([keys <= rows] * GROUP, axis=1)


def local_stats(scores, dprods):
    top = jnp.max(scores, axis=0, keepdims=True)
    weights = jnp.exp2(scores - top)
    total = jnp.sum(weights, axis=0, keepdims=True)
    mixed = jnp.sum(weights * dprods, axis=0, keepdims=True)
    return top, total, mixed


def merge(found):
    top = functools.reduce(jnp.maximum, [item[0] for item in found])
    scales = [jnp.exp2(item[0] - top) for item in found]
    total = sum(item[1] * scale for item, scale in zip(found, scales))
    mixed = sum(item[2] * scale for item, scale in zip(found, scales))
    return top, total, mixed


def block_stats(q, g, keys, values):
    return local_stats(dot_nt(keys, q) * LOG_FACTOR, dot_nt(values, g))


def put_stats(ref, head, found):
    for kind in range(3):
        ref[pl.ds(kind * GROUP + head, 1), :] = found[kind]


def get_stats(ref, head):
    return tuple(ref[pl.ds(kind * GROUP + head, 1), :] for kind in range(3))


def own_stats_kernel(info, q_ref, g_ref, pair_ref, sk_ref, sv_ref, out_ref):
    out_ref[...] = jnp.zeros_like(out_ref)
    scores = dot_nt(sk_ref[response_rows(info), :], load_own(q_ref, info)) * LOG_FACTOR
    scores = jnp.where(causal(info), scores, -jnp.inf)
    own = local_stats(scores, dot_nt(sv_ref[response_rows(info), :], load_own(g_ref, info)))
    mine = lax.broadcasted_iota(jnp.int32, (1, SIDE * HD), 1) // HD == info[0]
    for head in range(GROUP):
        wide = [jnp.concatenate([item[:, head * HD : (head + 1) * HD]] * SIDE, axis=1) for item in own]
        put_stats(out_ref, head, [jnp.where(mine, a, b) for a, b in zip(wide, (LOW, 0.0, 0.0))])

    @pl.loop(0, GROUP)
    def _(head):
        found = block_stats(load_head(q_ref, head), load_head(g_ref, head), pair_ref[0], pair_ref[1])
        put_stats(out_ref, head, merge([found, get_stats(out_ref, head)]))


def rest_stats_kernel(info, q_ref, g_ref, p1_ref, p2_ref, p3_ref, former_ref, out_ref):
    out_ref[...] = jnp.zeros_like(out_ref)

    @pl.loop(0, GROUP)
    def _(head):
        q, g = load_head(q_ref, head), load_head(g_ref, head)
        found = [get_stats(former_ref, head)]
        for ref in (p1_ref, p2_ref, p3_ref):
            found.append(block_stats(q, g, ref[0], ref[1]))
        found = merge(found)
        for copy in range(SIDE):
            put_stats(out_ref.at[copy], head, found)


def score_grads(k, v, q, g, log_sum, delta, allowed=None):
    probs = jnp.exp2(dot_nt(k, q) * LOG_FACTOR - log_sum)
    if allowed is not None:
        probs = jnp.where(allowed, probs, 0.0)
    dscores = (probs * (dot_nt(v, g) - delta)).astype(BF16)
    return probs.astype(BF16), dscores


def grads_kernel(
    info, q_ref, g_ref, p0_ref, p1_ref, p2_ref, p3_ref, sk_ref, sv_ref, part_ref,
    dq0_ref, dq1_ref, dq2_ref, dq3_ref, own_ref, send1_ref, send2_ref, send3_ref,
    stat_ref, keyt_ref, dkey_ref, dvalue_ref, dself_key_ref, dself_value_ref, dself_query_ref, piece_ref,
):
    pair_refs = (p0_ref, p1_ref, p2_ref, p3_ref)
    parts = [
        tuple(part_ref[i, kind * GROUP : (kind + 1) * GROUP, :] for kind in range(3)) for i in range(SIDE)
    ]
    top, total, mixed = merge(parts)
    stat_ref[:GROUP, :] = top + jnp.log2(total)
    stat_ref[GROUP : 2 * GROUP, :] = mixed / total
    for i in range(SIDE):
        keyt_ref[i] = pair_refs[i][0].T
    dkey_ref[...] = jnp.zeros_like(dkey_ref)
    dvalue_ref[...] = jnp.zeros_like(dvalue_ref)

    q, g = load_own(q_ref, info), load_own(g_ref, info)
    keys = sk_ref[response_rows(info), :]
    log_sum, delta = (
        jnp.concatenate([own_lanes(stat_ref[first + h : first + h + 1, :], info) for h in range(GROUP)], axis=1)
        for first in (0, GROUP)
    )
    probs, dscores = score_grads(
        keys, sv_ref[response_rows(info), :], q, g, log_sum, delta, causal(info)
    )
    dself_value_ref[...] = dot_nn(probs, g)
    dself_key_ref[...] = dot_nn(dscores, q)
    dself_query_ref[...] = dot_nn(keys.T, dscores)

    @pl.loop(0, GROUP)
    def _(head):
        log_sum = stat_ref[pl.ds(head, 1), :]
        delta = stat_ref[pl.ds(GROUP + head, 1), :]
        q, g = load_head(q_ref, head), load_head(g_ref, head)
        dq = jnp.zeros((HD, SIDE * HD), F32)
        for i in range(SIDE):
            probs, dscores = score_grads(pair_refs[i][0], pair_refs[i][1], q, g, log_sum, delta)
            dvalue_ref[i] += dot_nn(probs, g)
            dkey_ref[i] += dot_nn(dscores, q)
            dq = dq + dot_nn(keyt_ref[i], dscores)
        own = dself_query_ref[:, head_lanes(head)]
        for response in range(SIDE):
            piece = dq[:, response * HD : (response + 1) * HD]
            piece = piece + jnp.where(response == info[0], own, 0.0)
            piece_ref[response] = (piece * FACTOR).T.astype(BF16)
        for step, out_ref in zip((0,) + PLACES, (dq0_ref, dq1_ref, dq2_ref, dq3_ref)):
            response = lax.rem(info[0] + step, SIDE)
            out_ref[0, :, head_lanes(head)] = piece_ref[response]
            out_ref[1, :, head_lanes(head)] = piece_ref[response ^ 1]

    for i, step, ref in zip(range(SIDE), (0,) + PLACES, (own_ref, send1_ref, send2_ref, send3_ref)):
        source = lax.rem(info[1] + SIDE - step, SIDE)
        slots = pl.ds(pl.multiple_of(source * HD, HD), HD)
        ref[:L, :HD] = (dkey_ref[i] * FACTOR).astype(ref.dtype)
        ref[:L, HD:] = dvalue_ref[i].astype(ref.dtype)
        ref[L:, :HD] = (dself_key_ref[slots, :] * FACTOR).astype(ref.dtype)
        ref[L:, HD:] = dself_value_ref[slots, :].astype(ref.dtype)


def finish_kernel(own_ref, b1_ref, b2_ref, b3_ref, dk_ref, dv_ref, dsk_ref, dsv_ref):
    total = own_ref[...] + sum(ref[...].astype(F32) for ref in (b1_ref, b2_ref, b3_ref))
    dk_ref[...] = total[:L, :HD]
    dv_ref[...] = total[:L, HD:]
    dsk_ref[...] = total[L:, :HD]
    dsv_ref[...] = total[L:, HD:]


def sum_turn_kernel(parts_ref, out_ref):
    total = parts_ref[0].astype(F32)
    for part in range(1, parts_ref.shape[0]):
        total = total + parts_ref[part].astype(F32)
    out_ref[...] = total.T.astype(BF16)


def project_blocks(info, weight_refs, core, rows, put):
    depth = weight_refs[0].shape[1]
    for step, weight_ref in zip((0,) + PLACES, weight_refs):
        source = lax.rem(info[1] + SIDE - step, SIDE)
        at = pl.ds(pl.multiple_of(lax.rem(source, 2) * depth, depth), depth)

        @pl.when(lax.div(source, 2) == core)
        def _():
            for block in range(2):
                terms = dot_nt(weight_ref[block], rows)
                for part in range(2):
                    put(part, block, at, terms[:, part * HD : (part + 1) * HD])


def project_theirs_kernel(
    info, d0_ref, d1_ref, d2_ref, d3_ref, w0_ref, w1_ref, w2_ref, w3_ref, out_ref, rows_ref
):
    for part in range(2):
        total = sum(ref[part].astype(F32) for ref in (d0_ref, d1_ref, d2_ref, d3_ref))
        rows_ref[part * HD : (part + 1) * HD, :] = total.astype(BF16)

    def put(part, block, at, terms):
        out_ref[part, block, at, :] = terms.astype(BF16)

    project_blocks(info, (w0_ref, w1_ref, w2_ref, w3_ref), 1 - info[2], rows_ref[...], put)


def project_mine_kernel(
    info, rows_ref, theirs_ref, w0_ref, w1_ref, w2_ref, w3_ref, out_ref
):
    columns = (info[0], SIDE - 1 - info[0])

    def put(part, block, at, terms):
        terms = terms + theirs_ref[part, block, at, :].astype(F32)
        out_ref[columns[block] ^ part, at, :] = terms.astype(BF16)

    project_blocks(info, (w0_ref, w1_ref, w2_ref, w3_ref), info[2], rows_ref[...], put)


def ring(step):
    return [(i, (i + step) % SIDE) for i in range(SIDE)]


def spread(array, axis):
    return [lax.ppermute(array, axis, ring(step)) for step in PLACES]


def body(queries, doc_keys, doc_values, self_keys, self_values, out_grads, lengths, query_weight):
    doc_rows = doc_keys.shape[0]
    place_y = lax.axis_index("y").astype(jnp.int32)
    info = jnp.stack([lax.axis_index(Z).astype(jnp.int32), place_y, lax.axis_index("core").astype(jnp.int32)])
    pair = jnp.stack([doc_keys, doc_values])
    pairs = [pair] + spread(pair, "y")
    other = lax.ppermute(query_weight, Z, [(i, SIDE - 1 - i) for i in range(SIDE)])

    def own_rows(array):
        return lax.dynamic_slice_in_dim(array.reshape(SIDE, L, WIDTH), place_y * HD, HD, 1)

    valid = (jnp.arange(HD, dtype=jnp.int32) + place_y * HD)[None, :] < lengths[:, None]
    q_own = own_rows(queries)
    g_own = own_rows(out_grads) * valid[..., None].astype(out_grads.dtype)

    smem = pl.BlockSpec(memory_space=pltpu.SMEM)
    vmem = pl.BlockSpec(memory_space=pltpu.VMEM)

    def call(kernel, shapes, operands, name, megabytes=8, scratch=()):
        return pl.pallas_call(
            kernel,
            in_specs=[smem if a is info else vmem for a in operands],
            out_specs=jax.tree.map(lambda _: vmem, shapes),
            out_shape=shapes,
            scratch_shapes=scratch,
            compiler_params=pltpu.CompilerParams(vmem_limit_bytes=megabytes * 1024 * 1024),
            name=name,
        )(*operands)

    shape = jax.ShapeDtypeStruct
    stats = call(
        own_stats_kernel,
        shape((STATS, SIDE * HD), F32),
        (info, q_own, g_own, pair, self_keys, self_values),
        "own_stats",
    )
    weight = jnp.stack([query_weight, other])
    weight, stats, *pairs = lax.optimization_barrier((weight, stats, *pairs))
    weights = [weight] + spread(weight, "y")
    stats = call(
        rest_stats_kernel,
        shape((SIDE, STATS, SIDE * HD), F32),
        (info, q_own, g_own, *pairs[1:], stats),
        "rest_stats",
    )
    parts = lax.all_to_all(stats, Z, 0, 0, tiled=True)

    grad_shape = shape((2, HD, WIDTH), BF16)
    back_shape = shape((doc_rows + HD, 2 * HD), BF16)
    found = call(
        grads_kernel,
        [grad_shape] * SIDE + [shape(back_shape.shape, F32)] + [back_shape] * 3,
        (info, q_own, g_own, *pairs, self_keys, self_values, parts),
        "local_grads",
        megabytes=14,
        scratch=[
            pltpu.VMEM((STATS, SIDE * HD), F32),
            pltpu.VMEM((SIDE, HD, doc_rows), BF16),
            pltpu.VMEM((SIDE, doc_rows, HD), F32),
            pltpu.VMEM((SIDE, doc_rows, HD), F32),
            pltpu.VMEM((L, HD), F32),
            pltpu.VMEM((L, HD), F32),
            pltpu.VMEM((HD, WIDTH), F32),
            pltpu.VMEM((SIDE, HD, HD), BF16),
        ],
    )
    found, weights = lax.optimization_barrier((found, weights))
    dq, dq_sends, own, sends = found[0], found[1:SIDE], found[SIDE], found[SIDE + 1 :]
    dq_parts = [lax.ppermute(a, Z, ring(step)) for step, a in zip(PLACES, dq_sends)]
    backs = [lax.ppermute(a, "y", ring(SIDE - step)) for step, a in zip(PLACES, sends)]
    dq_parts, backs = lax.optimization_barrier((dq_parts, backs))
    columns = 2 * query_weight.shape[0]
    theirs, rows = call(
        project_theirs_kernel,
        [shape((2, 2, columns, HD), BF16), shape((2 * HD, WIDTH), BF16)],
        (info, dq, *dq_parts, *weights),
        "project_theirs",
    )
    theirs = lax.ppermute(theirs, "core", [(0, 1), (1, 0)])
    terms = call(
        project_mine_kernel,
        shape((SIDE, columns, HD), BF16),
        (info, rows, theirs, *weights),
        "project_mine",
    )
    terms = lax.all_to_all(terms, "x", 0, 0, tiled=True)
    input_grads = call(sum_turn_kernel, shape((HD, columns), BF16), (terms,), "sum_groups")
    moves = []
    for z in range(SIDE):
        for x in range(SIDE):
            stays = x in (z, SIDE - 1 - z)
            moves.append((z * SIDE + x, z * SIDE + x if stays else (z ^ 1) * SIDE + (x ^ 1)))
    input_grads = lax.ppermute(input_grads, Z + ("x",), moves)
    grads = call(
        finish_kernel,
        [shape((doc_rows, HD), F32)] * 2 + [shape((HD, HD), F32)] * 2,
        (own, *backs),
        "sum_key_values",
    )
    return (input_grads, *grads)


def solution(mesh):
    names = ("z_high", "z_low", "y", "x", "core")
    grid = Mesh(mesh.devices.reshape(2, 2, SIDE, SIDE, 2), names)
    seq, head = names[:3], names[3:]
    in_specs = (
        P(None, head),
        P(seq, head),
        P(seq, head),
        P(None, head),
        P(None, head),
        P(None, head),
        P(),
        P(seq, head),
    )
    return jax.shard_map(
        body, mesh=grid, in_specs=in_specs, out_specs=(P(seq, head),) * 5, check_vma=False
    )
```

time: 128 us -> 110 us (0.86)
  between operations: 14.1 us -> 0.78 us
  starting transfers between devices: 13.5 us -> 24.7 us
  Pallas kernels: 38.8 us -> 30.9 us
  local copies, waits for them, and re-layouts: 5.83 us -> 0.68 us
  blocking collectives: 27.6 us -> 24.4 us
  other arithmetic: 2.63 us -> 4.45 us
    ppermute x0 -> x14, starting transfers between devices: none -> 24.7 us  [the longest x6 9.07 us: spread(): return [lax.ppermute(array, axis, ring(step)) for step in PLACES]]
    ppermute x0 -> x14, waiting for transfers between devices: none -> 21.3 us  [the longest x3 7.73 us: body(): lax.ppermute(a, 'y', ring(SIDE - step))]
    all_to_all x3 -> x0, waiting for transfers between devices: 20.9 us -> none  [the longest x1 12.1 us: body(): pairs = lax.all_to_all(pairs, 'y', 0, 0, tiled=True)]
    all_to_all x3 -> x0, starting transfers between devices: 13.3 us -> none  [the longest x1 4.83 us: body(): terms = lax.all_to_all(terms, 'x', 0, 0, tiled=True)]
    pallas_call x7, Pallas kernels: 38.8 us -> 30.9 us  [call(): pl.pallas_call(kernel, in_specs=[smem if a is info else vmem for a in ope...]
    unnamed x28 -> x7, local copies, waits for them, and re-layouts: 4.79 us -> 0.68 us
    all_to_all x2, blocking collectives: 27.6 us -> 24.4 us  [the longest x1 14.4 us: body(): terms = lax.all_to_all(terms, 'x', 0, 0, tiled=True)]
    another operation x1 -> x3, other arithmetic: 0.08 us -> 2.25 us  [the longest x1 1.09 us: body(): weight = jnp.stack([query_weight, other])]
  transfers between devices with their start and end apart: 5 -> 15, of which waited for: 4 -> 7; matrix products, arithmetic and copies ran while one was open for 3% -> 3% of each run, Pallas kernels for 29% -> 25%
where the time goes in v5:
time: 110 us; the launch traced here: 109 us
  Pallas kernels  30.9 us (28%)
  starting transfers between devices  24.7 us (22%)
  blocking collectives  24.4 us (22%)
  waiting for transfers between devices  23.4 us (21%)
  other arithmetic  4.45 us (4%)
    pallas_call x7, Pallas kernels, call(): pl.pallas_call(kernel, in_specs=[smem if a is info else vmem for a in ope...  30.9 us
    all_to_all x1, blocking collectives, body(): terms = lax.all_to_all(terms, 'x', 0, 0, tiled=True)  14.4 us
    all_to_all x1, blocking collectives, body(): parts = lax.all_to_all(stats, Z, 0, 0, tiled=True)  10 us
    ppermute x6, starting transfers between devices, spread(): return [lax.ppermute(array, axis, ring(step)) for step in PLACES]  9.07 us
    ppermute x3, waiting for transfers between devices, body(): lax.ppermute(a, 'y', ring(SIDE - step))  7.73 us
    ppermute x3, waiting for transfers between devices, body(): lax.ppermute(a, Z, ring(step))  5.45 us
    ppermute x1, waiting for transfers between devices, body(): input_grads = lax.ppermute(input_grads, Z + ('x',), moves)  4.52 us
    ppermute x3, starting transfers between devices, body(): lax.ppermute(a, 'y', ring(SIDE - step))  4.45 us
  transfers between devices with their start and end apart: 15, of which 7 were waited for; matrix products, arithmetic and copies ran while one was open for 3% of the time, Pallas kernels for 25%

profile of v5, /device:TPU:2, one launch (start us, length us, event | category | flops | bytes accessed | tf_op | source)
XLA Modules:
  0.0 109.3 jit_solution(10202756910717937750)
XLA Ops:
  1.7 1.6 %collective-permute-start.1 = (bf16[2,512,128]{2,1,0:T(8,128)(2,1)S(1)}, bf16[2,512,128]{2,1,0:T(8,128)(2,1)S(1)}, u32[]{:S(2)}, u32[]{:S(2)}) collective-permute-start(bf16[2,512,128]{2,1,0:T(8,128)(2,1)S(1)} %pad_maximum_fusion.1.pair_ref.p0_ref), channel_id=1, source_target_pairs={{0,8},{8,16},{16,24},{24,0},{1,9},{9,17},{17,25},{25,1},{2,10},{10... | collective-permute-start | bytes 786440 | tf_op jit(solution)/shard_map/ppermute | solution.py:250
  3.4 1.7 %collective-permute-start.2 = (bf16[2,512,128]{2,1,0:T(8,128)(2,1)S(1)}, bf16[2,512,128]{2,1,0:T(8,128)(2,1)S(1)}, u32[]{:S(2)}, u32[]{:S(2)}) collective-permute-start(bf16[2,512,128]{2,1,0:T(8,128)(2,1)S(1)} %pad_maximum_fusion.1.pair_ref.p0_ref), channel_id=1, source_target_pairs={{0,24},{8,0},{16,8},{24,16},{1,25},{9,1},{17,9},{25,17},{2,26},{10... | collective-permute-start | bytes 786440 | tf_op jit(solution)/shard_map/ppermute | solution.py:250
  5.0 2.0 %collective-permute-start.3 = (bf16[2,512,128]{2,1,0:T(8,128)(2,1)S(1)}, bf16[2,512,128]{2,1,0:T(8,128)(2,1)S(1)}, u32[]{:S(2)}, u32[]{:S(2)}) collective-permute-start(bf16[2,512,128]{2,1,0:T(8,128)(2,1)S(1)} %pad_maximum_fusion.1.pair_ref.p0_ref), channel_id=1, source_target_pairs={{0,16},{8,24},{16,0},{24,8},{1,17},{9,25},{17,1},{25,9},{2,18},{10... | collective-permute-start | bytes 786440 | tf_op jit(solution)/shard_map/ppermute | solution.py:250
  7.0 4.0 %collective-permute-start = (bf16[320,640]{1,0:T(8,128)(2,1)}, bf16[320,640]{1,0:T(8,128)(2,1)}, u32[]{:S(2)}, u32[]{:S(2)}) collective-permute-start(bf16[320,640]{1,0:T(8,128)(2,1)} %param.15), channel_id=1, source_target_pairs={{0,96},{32,64},{64,32},{96,0},{1,97},{33,65},{65,33},{97,1},{2,98}... | collective-permute-start | bytes 1228808 | tf_op jit(solution)/shard_map/ppermute | solution.py:259
  11.8 1.5 %dynamic-slice_multiply_fusion = (bf16[4,128,640]{2,1,0:T(8,128)(2,1)S(1)}, bf16[4,128,640]{2,1,0:T(8,128)(2,1)S(1)}) fusion(bf16[4,512,640]{2,1,0:T(8,128)(2,1)} %bitcast.10, s32[]{:T(128)S(6)} %select_n.4, bf16[4,128]{1,0:T(4,128)(2,1)S(1)} %compare_convert_fusion, bf16[4,512,640]{2,1,0:T(8,128)(2,1)} %bitcast.11), kind=kLoop, calls=%fused_computation.1 | loop fusion | flops 1310720 | bytes 2622468 | tf_op jit(solution)/shard_map/mul | solution.py:266
  13.4 3.9 %own_stats.1.former_ref = f32[16,512]{1,0:T(8,128)S(1)} custom-call(s32[3]{0:T(128)S(1)} %pad_add_fusion.info, bf16[4,128,640]{2,1,0:T(8,128)(2,1)S(1)} %get-tuple-element.82.q_ref, bf16[4,128,640]{2,1,0:T(8,128)(2,1)S(1)} %get-tuple-element.81.g_ref, bf16[2,512,128]{2,1,0:T(8,128)(2,1)S(1)} %pad_maximum_fusion.1.pair_ref.p0_ref, ...), custom_call_target="tpu_custom_call" | custom-call | tf_op jit(solution)/shard_map/own_stats/pallas_call | solution.py:272
  17.3 2.7 %collective-permute-done = bf16[320,640]{1,0:T(8,128)(2,1)} collective-permute-done((bf16[320,640]{1,0:T(8,128)(2,1)}, bf16[320,640]{1,0:T(8,128)(2,1)}, u32[]{:S(2)}, u32[]{:S(2)}) %collective-permute-start) | collective-permute-done | bytes 409632 | tf_op jit(solution)/shard_map/ppermute | solution.py:259
  21.9 2.6 %collective-permute-start.5 = (bf16[2,320,640]{2,1,0:T(8,128)(2,1)S(1)}, bf16[2,320,640]{2,1,0:T(8,128)(2,1)S(1)}, u32[]{:S(2)}, u32[]{:S(2)}) collective-permute-start(bf16[2,320,640]{2,1,0:T(8,128)(2,1)S(1)} %pad_maximum_fusion.w0_ref), channel_id=1, source_target_pairs={{0,24},{8,0},{16,8},{24,16},{1,25},{9,1},{17,9},{25,17},{2,26},{10... | collective-permute-start | bytes 2457608 | tf_op jit(solution)/shard_map/ppermute | solution.py:250
  24.9 6.5 %rest_stats.1 = f32[4,16,512]{2,1,0:T(8,128)S(1)} custom-call(s32[3]{0:T(128)S(1)} %pad_add_fusion.info, bf16[4,128,640]{2,1,0:T(8,128)(2,1)S(1)} %get-tuple-element.82.q_ref, bf16[4,128,640]{2,1,0:T(8,128)(2,1)S(1)} %get-tuple-element.81.g_ref, bf16[2,512,128]{2,1,0:T(8,128)(2,1)S(1)} %collective-permute-done.1.p1_ref, ...), custom_call_target="tpu_custom_call" | custom-call | tf_op jit(solution)/shard_map/rest_stats/pallas_call | solution.py:272
  31.4 10.0 %all_to_all.10.part_ref = f32[4,16,512]{2,1,0:T(8,128)S(1)} all-to-all(f32[4,16,512]{2,1,0:T(8,128)S(1)} %rest_stats.1), channel_id=1, replica_groups=mesh['z_high'=2,'z_low'=2,'y'=4,'x'=4,'core'=2] {'z_high','z_low'}, dimensions={0} | all-to-all | bytes 262144 | tf_op jit(solution)/shard_map/all_to_all | solution.py:298
  41.4 16.2 %local_grads.1 = (bf16[2,128,640]{2,1,0:T(8,128)(2,1)S(1)}, bf16[2,128,640]{2,1,0:T(8,128)(2,1)S(1)}, bf16[2,128,640]{2,1,0:T(8,128)(2,1)S(1)}, bf16[2,128,640]{...) custom-call(s32[3]{0:T(128)S(1)} %pad_add_fusion.info, ...), custom_call_target="tpu_custom_call" | custom-call | tf_op jit(solution)/shard_map/local_grads/pallas_call | solution.py:272
  58.5 3.0 %collective-permute-start.10 = (bf16[640,256]{1,0:T(8,128)(2,1)S(1)}, bf16[640,256]{1,0:T(8,128)(2,1)S(1)}, u32[]{:S(2)}, u32[]{:S(2)}) collective-permute-start(bf16[640,256]{1,0:T(8,128)(2,1)S(1)} %get-tuple-element.61), channel_id=1, source_target_pairs={{0,24},{8,0},{16,8},{24,16},{1,25},{9,1},{17,9},{25,17},{2,26},{10... | collective-permute-start | bytes 983048 | tf_op jit(solution)/shard_map/ppermute | solution.py:322
  61.5 1.5 %collective-permute-start.12 = (bf16[640,256]{1,0:T(8,128)(2,1)S(1)}, bf16[640,256]{1,0:T(8,128)(2,1)S(1)}, u32[]{:S(2)}, u32[]{:S(2)}) collective-permute-start(bf16[640,256]{1,0:T(8,128)(2,1)S(1)} %get-tuple-element.63), channel_id=1, source_target_pairs={{0,16},{8,24},{16,0},{24,8},{1,17},{9,25},{17,1},{25,9},{2,18},{10... | collective-permute-start | bytes 983048 | tf_op jit(solution)/shard_map/ppermute | solution.py:322
  63.4 2.7 %collective-permute-start.8 = (bf16[2,128,640]{2,1,0:T(8,128)(2,1)S(1)}, bf16[2,128,640]{2,1,0:T(8,128)(2,1)S(1)}, u32[]{:S(2)}, u32[]{:S(2)}) collective-permute-start(bf16[2,128,640]{2,1,0:T(8,128)(2,1)S(1)} %get-tuple-element.59), channel_id=1, source_target_pairs={{0,96},{32,0},{64,32},{96,64},{1,97},{33,1},{65,33},{97,65},{2,98}... | collective-permute-start | bytes 983048 | tf_op jit(solution)/shard_map/ppermute | solution.py:321
  66.2 5.8 %collective-permute-done.10.b1_ref = bf16[640,256]{1,0:T(8,128)(2,1)S(1)} collective-permute-done((bf16[640,256]{1,0:T(8,128)(2,1)S(1)}, bf16[640,256]{1,0:T(8,128)(2,1)S(1)}, u32[]{:S(2)}, u32[]{:S(2)}) %collective-permute-start.10) | collective-permute-done | bytes 327712 | tf_op jit(solution)/shard_map/ppermute | solution.py:322
  72.0 1.2 %collective-permute-start.9 = (bf16[2,128,640]{2,1,0:T(8,128)(2,1)S(1)}, bf16[2,128,640]{2,1,0:T(8,128)(2,1)S(1)}, u32[]{:S(2)}, u32[]{:S(2)}) collective-permute-start(bf16[2,128,640]{2,1,0:T(8,128)(2,1)S(1)} %get-tuple-element.60), channel_id=1, source_target_pairs={{0,64},{32,96},{64,0},{96,32},{1,65},{33,97},{65,1},{97,33},{2,66}... | collective-permute-start | bytes 983048 | tf_op jit(solution)/shard_map/ppermute | solution.py:321
  73.2 1.9 %collective-permute-done.11.b2_ref = bf16[640,256]{1,0:T(8,128)(2,1)S(1)} collective-permute-done((bf16[640,256]{1,0:T(8,128)(2,1)S(1)}, bf16[640,256]{1,0:T(8,128)(2,1)S(1)}, u32[]{:S(2)}, u32[]{:S(2)}) %collective-permute-start.11) | collective-permute-done | bytes 327712 | tf_op jit(solution)/shard_map/ppermute | solution.py:322
  75.1 5.4 %collective-permute-done.9.d3_ref = bf16[2,128,640]{2,1,0:T(8,128)(2,1)S(1)} collective-permute-done((bf16[2,128,640]{2,1,0:T(8,128)(2,1)S(1)}, bf16[2,128,640]{2,1,0:T(8,128)(2,1)S(1)}, u32[]{:S(2)}, u32[]{:S(2)}) %collective-permute-start.9) | collective-permute-done | bytes 327712 | tf_op jit(solution)/shard_map/ppermute | solution.py:321
  80.5 1.7 %project_theirs.1 = (bf16[2,2,640,128]{3,2,1,0:T(8,128)(2,1)S(1)}, bf16[256,640]{1,0:T(8,128)(2,1)S(1)}) custom-call(s32[3]{0:T(128)S(1)} %pad_add_fusion.info, bf16[2,128,640]{2,1,0:T(8,128)(2,1)S(1)} %get-tuple-element.57.d0_ref, bf16[2,128,640]{2,1,0:T(8,128)(2,1)S(1)} %collective-permute-done.7.d1_ref, ...), custom_call_target="tpu_custom_call" | custom-call | tf_op jit(solution)/shard_map/project_theirs/pallas_call | solution.py:272
  82.4 2.1 %collective-permute-done.13.theirs_ref = bf16[2,2,640,128]{3,2,1,0:T(8,128)(2,1)S(1)} collective-permute-done((bf16[2,2,640,128]{3,2,1,0:T(8,128)(2,1)S(1)}, bf16[2,2,640,128]{3,2,1,0:T(8,128)(2,1)S(1)}, u32[]{:S(2)}, u32[]{:S(2)}) %collective-permute-start.13) | collective-permute-done | bytes 655392 | tf_op jit(solution)/shard_map/ppermute | solution.py:331
  84.5 1.5 %project_mine.1 = bf16[4,640,128]{2,1,0:T(8,128)(2,1)S(1)} custom-call(s32[3]{0:T(128)S(1)} %pad_add_fusion.info, bf16[256,640]{1,0:T(8,128)(2,1)S(1)} %get-tuple-element.71.rows_ref, bf16[2,2,640,128]{3,2,1,0:T(8,128)(2,1)S(1)} %collective-permute-done.13.theirs_ref, bf16[2,320,640]{2,1,0:T(8,128)(2,1)S(1)} %pad_maximum_fusion.w0_ref, ...), custom_call_target="tpu_custom_call" | custom-call | tf_op jit(solution)/shard_map/project_mine/pallas_call | solution.py:272
  86.0 14.4 %all_to_all.11.parts_ref = bf16[4,640,128]{2,1,0:T(8,128)(2,1)S(1)} all-to-all(bf16[4,640,128]{2,1,0:T(8,128)(2,1)S(1)} %project_mine.1), channel_id=1, replica_groups=mesh['z_high'=2,'z_low'=2,'y'=4,'x'=4,'core'=2] {'x'}, dimensions={0} | all-to-all | bytes 1310720 | tf_op jit(solution)/shard_map/all_to_all | solution.py:338
  100.5 2.7 %collective-permute-start.14 = (bf16[128,640]{1,0:T(8,128)(2,1)S(1)}, bf16[128,640]{1,0:T(8,128)(2,1)S(1)}, u32[]{:S(2)}, u32[]{:S(2)}) collective-permute-start(bf16[128,640]{1,0:T(8,128)(2,1)S(1)} %sum_groups.1), channel_id=1, source_target_pairs={{0,0},{2,32},{4,38},{6,6},{32,2},{34,34},{36,36},{38,4},{64,98},{6... | collective-permute-start | bytes 491528 | tf_op jit(solution)/shard_map/ppermute | solution.py:345
  104.1 4.5 %collective-permute-done.14 = bf16[128,640]{1,0:T(8,128)(2,1)S(1)} collective-permute-done((bf16[128,640]{1,0:T(8,128)(2,1)S(1)}, bf16[128,640]{1,0:T(8,128)(2,1)S(1)}, u32[]{:S(2)}, u32[]{:S(2)}) %collective-permute-start.14) | collective-permute-done | bytes 163872 | tf_op jit(solution)/shard_map/ppermute | solution.py:345
  (28 shorter events, 7.4 us)
Async XLA Ops:
  0.6 12.7 %copy-start = (bf16[2048,128]{1,0:T(8,128)(2,1)S(1)}, bf16[2048,128]{1,0:T(8,128)(2,1)}, u32[]{:S(2)}) copy-start(bf16[2048,128]{1,0:T(8,128)(2,1)} %sk_ref.3) | copy-start | bytes 1572868
  0.6 12.7 %copy-start.1 = (bf16[2048,128]{1,0:T(8,128)(2,1)S(1)}, bf16[2048,128]{1,0:T(8,128)(2,1)}, u32[]{:S(2)}) copy-start(bf16[2048,128]{1,0:T(8,128)(2,1)} %sv_ref.3) | copy-start | bytes 1572868
  1.7 19.4 %collective-permute-start.1 = (bf16[2,512,128]{2,1,0:T(8,128)(2,1)S(1)}, bf16[2,512,128]{2,1,0:T(8,128)(2,1)S(1)}, u32[]{:S(2)}, u32[]{:S(2)}) collective-permute-start(bf16[2,512,128]{2,1,0:T(8,128)(2,1)S(1)} %pad_maximum_fusion.1.pair_ref.p0_ref), channel_id=1, source_target_pairs={{0,8},{8,16},{16,24},{24,0},{1,9},{9,17},{17,25},{25,1},{2,10},{10... | collective-permute-start | bytes 786440 | tf_op jit(solution)/shard_map/ppermute | solution.py:250
  3.4 17.7 %collective-permute-start.2 = (bf16[2,512,128]{2,1,0:T(8,128)(2,1)S(1)}, bf16[2,512,128]{2,1,0:T(8,128)(2,1)S(1)}, u32[]{:S(2)}, u32[]{:S(2)}) collective-permute-start(bf16[2,512,128]{2,1,0:T(8,128)(2,1)S(1)} %pad_maximum_fusion.1.pair_ref.p0_ref), channel_id=1, source_target_pairs={{0,24},{8,0},{16,8},{24,16},{1,25},{9,1},{17,9},{25,17},{2,26},{10... | collective-permute-start | bytes 786440 | tf_op jit(solution)/shard_map/ppermute | solution.py:250
  5.0 16.1 %collective-permute-start.3 = (bf16[2,512,128]{2,1,0:T(8,128)(2,1)S(1)}, bf16[2,512,128]{2,1,0:T(8,128)(2,1)S(1)}, u32[]{:S(2)}, u32[]{:S(2)}) collective-permute-start(bf16[2,512,128]{2,1,0:T(8,128)(2,1)S(1)} %pad_maximum_fusion.1.pair_ref.p0_ref), channel_id=1, source_target_pairs={{0,16},{8,24},{16,0},{24,8},{1,17},{9,25},{17,1},{25,9},{2,18},{10... | collective-permute-start | bytes 786440 | tf_op jit(solution)/shard_map/ppermute | solution.py:250
  7.0 13.0 %collective-permute-start = (bf16[320,640]{1,0:T(8,128)(2,1)}, bf16[320,640]{1,0:T(8,128)(2,1)}, u32[]{:S(2)}, u32[]{:S(2)}) collective-permute-start(bf16[320,640]{1,0:T(8,128)(2,1)} %param.15), channel_id=1, source_target_pairs={{0,96},{32,64},{64,32},{96,0},{1,97},{33,65},{65,33},{97,1},{2,98}... | collective-permute-start | bytes 1228808 | tf_op jit(solution)/shard_map/ppermute | solution.py:259
  13.3 6.7 %copy-start.2 = (bf16[320,640]{1,0:T(8,128)(2,1)S(1)}, bf16[320,640]{1,0:T(8,128)(2,1)}, u32[]{:S(2)}) copy-start(bf16[320,640]{1,0:T(8,128)(2,1)} %param.15) | copy-start | bytes 1228804
  21.1 37.3 %collective-permute-start.4 = (bf16[2,320,640]{2,1,0:T(8,128)(2,1)S(1)}, bf16[2,320,640]{2,1,0:T(8,128)(2,1)S(1)}, u32[]{:S(2)}, u32[]{:S(2)}) collective-permute-start(bf16[2,320,640]{2,1,0:T(8,128)(2,1)S(1)} %pad_maximum_fusion.w0_ref), channel_id=1, source_target_pairs={{0,8},{8,16},{16,24},{24,0},{1,9},{9,17},{17,25},{25,1},{2,10},{10... | collective-permute-start | bytes 2457608 | tf_op jit(solution)/shard_map/ppermute | solution.py:250
  21.9 36.6 %collective-permute-start.5 = (bf16[2,320,640]{2,1,0:T(8,128)(2,1)S(1)}, bf16[2,320,640]{2,1,0:T(8,128)(2,1)S(1)}, u32[]{:S(2)}, u32[]{:S(2)}) collective-permute-start(bf16[2,320,640]{2,1,0:T(8,128)(2,1)S(1)} %pad_maximum_fusion.w0_ref), channel_id=1, source_target_pairs={{0,24},{8,0},{16,8},{24,16},{1,25},{9,1},{17,9},{25,17},{2,26},{10... | collective-permute-start | bytes 2457608 | tf_op jit(solution)/shard_map/ppermute | solution.py:250
  24.4 34.0 %collective-permute-start.6 = (bf16[2,320,640]{2,1,0:T(8,128)(2,1)S(1)}, bf16[2,320,640]{2,1,0:T(8,128)(2,1)S(1)}, u32[]{:S(2)}, u32[]{:S(2)}) collective-permute-start(bf16[2,320,640]{2,1,0:T(8,128)(2,1)S(1)} %pad_maximum_fusion.w0_ref), channel_id=1, source_target_pairs={{0,16},{8,24},{16,0},{24,8},{1,17},{9,25},{17,1},{25,9},{2,18},{10... | collective-permute-start | bytes 2457608 | tf_op jit(solution)/shard_map/ppermute | solution.py:250
  58.5 13.5 %collective-permute-start.10 = (bf16[640,256]{1,0:T(8,128)(2,1)S(1)}, bf16[640,256]{1,0:T(8,128)(2,1)S(1)}, u32[]{:S(2)}, u32[]{:S(2)}) collective-permute-start(bf16[640,256]{1,0:T(8,128)(2,1)S(1)} %get-tuple-element.61), channel_id=1, source_target_pairs={{0,24},{8,0},{16,8},{24,16},{1,25},{9,1},{17,9},{25,17},{2,26},{10... | collective-permute-start | bytes 983048 | tf_op jit(solution)/shard_map/ppermute | solution.py:322
  61.4 13.6 %collective-permute-start.11 = (bf16[640,256]{1,0:T(8,128)(2,1)S(1)}, bf16[640,256]{1,0:T(8,128)(2,1)S(1)}, u32[]{:S(2)}, u32[]{:S(2)}) collective-permute-start(bf16[640,256]{1,0:T(8,128)(2,1)S(1)} %get-tuple-element.62), channel_id=1, source_target_pairs={{0,8},{8,16},{16,24},{24,0},{1,9},{9,17},{17,25},{25,1},{2,10},{10... | collective-permute-start | bytes 983048 | tf_op jit(solution)/shard_map/ppermute | solution.py:322
  61.5 13.6 %collective-permute-start.12 = (bf16[640,256]{1,0:T(8,128)(2,1)S(1)}, bf16[640,256]{1,0:T(8,128)(2,1)S(1)}, u32[]{:S(2)}, u32[]{:S(2)}) collective-permute-start(bf16[640,256]{1,0:T(8,128)(2,1)S(1)} %get-tuple-element.63), channel_id=1, source_target_pairs={{0,16},{8,24},{16,0},{24,8},{1,17},{9,25},{17,1},{25,9},{2,18},{10... | collective-permute-start | bytes 983048 | tf_op jit(solution)/shard_map/ppermute | solution.py:322
  62.9 12.2 %collective-permute-start.7 = (bf16[2,128,640]{2,1,0:T(8,128)(2,1)S(1)}, bf16[2,128,640]{2,1,0:T(8,128)(2,1)S(1)}, u32[]{:S(2)}, u32[]{:S(2)}) collective-permute-start(bf16[2,128,640]{2,1,0:T(8,128)(2,1)S(1)} %get-tuple-element.58), channel_id=1, source_target_pairs={{0,32},{32,64},{64,96},{96,0},{1,33},{33,65},{65,97},{97,1},{2,34}... | collective-permute-start | bytes 983048 | tf_op jit(solution)/shard_map/ppermute | solution.py:321
  63.4 11.7 %collective-permute-start.8 = (bf16[2,128,640]{2,1,0:T(8,128)(2,1)S(1)}, bf16[2,128,640]{2,1,0:T(8,128)(2,1)S(1)}, u32[]{:S(2)}, u32[]{:S(2)}) collective-permute-start(bf16[2,128,640]{2,1,0:T(8,128)(2,1)S(1)} %get-tuple-element.59), channel_id=1, source_target_pairs={{0,96},{32,0},{64,32},{96,64},{1,97},{33,1},{65,33},{97,65},{2,98}... | collective-permute-start | bytes 983048 | tf_op jit(solution)/shard_map/ppermute | solution.py:321
  72.0 8.6 %collective-permute-start.9 = (bf16[2,128,640]{2,1,0:T(8,128)(2,1)S(1)}, bf16[2,128,640]{2,1,0:T(8,128)(2,1)S(1)}, u32[]{:S(2)}, u32[]{:S(2)}) collective-permute-start(bf16[2,128,640]{2,1,0:T(8,128)(2,1)S(1)} %get-tuple-element.60), channel_id=1, source_target_pairs={{0,64},{32,96},{64,0},{96,32},{1,65},{33,97},{65,1},{97,33},{2,66}... | collective-permute-start | bytes 983048 | tf_op jit(solution)/shard_map/ppermute | solution.py:321
  82.3 2.2 %collective-permute-start.13 = (bf16[2,2,640,128]{3,2,1,0:T(8,128)(2,1)S(1)}, bf16[2,2,640,128]{3,2,1,0:T(8,128)(2,1)S(1)}, u32[]{:S(2)}, u32[]{:S(2)}) collective-permute-start(bf16[2,2,640,128]{3,2,1,0:T(8,128)(2,1)S(1)} %get-tuple-element.72), channel_id=1, source_target_pairs={{0,1},{1,0},{2,3},{3,2},{4,5},{5,4},{6,7},{7,6},{8,9},{9,8},{10,11... | collective-permute-start | bytes 1966088 | tf_op jit(solution)/shard_map/ppermute | solution.py:331
  100.5 8.1 %collective-permute-start.14 = (bf16[128,640]{1,0:T(8,128)(2,1)S(1)}, bf16[128,640]{1,0:T(8,128)(2,1)S(1)}, u32[]{:S(2)}, u32[]{:S(2)}) collective-permute-start(bf16[128,640]{1,0:T(8,128)(2,1)S(1)} %sum_groups.1), channel_id=1, source_target_pairs={{0,0},{2,32},{4,38},{6,6},{32,2},{34,34},{36,36},{38,4},{64,98},{6... | collective-permute-start | bytes 491528 | tf_op jit(solution)/shard_map/ppermute | solution.py:345

commit v6 on v5

--- a/solution.py
+++ b/solution.py
@@ -316,11 +316,11 @@
             pltpu.VMEM((SIDE, HD, HD), BF16),
         ],
     )
-    found, weights = lax.optimization_barrier((found, weights))
     dq, dq_sends, own, sends = found[0], found[1:SIDE], found[SIDE], found[SIDE + 1 :]
     dq_parts = [lax.ppermute(a, Z, ring(step)) for step, a in zip(PLACES, dq_sends)]
+    weights, sends = lax.optimization_barrier((weights, sends))
     backs = [lax.ppermute(a, "y", ring(SIDE - step)) for step, a in zip(PLACES, sends)]
-    dq_parts, backs = lax.optimization_barrier((dq_parts, backs))
+    dq_parts, backs[:2] = lax.optimization_barrier((dq_parts, backs[:2]))
     columns = 2 * query_weight.shape[0]
     theirs, rows = call(
         project_theirs_kernel,

time: 110 us -> 102 us (0.927)
  blocking collectives: 24.4 us -> 10 us
  starting transfers between devices: 24.7 us -> 29.9 us
    all_to_all x1 -> x0, blocking collectives: 14.4 us -> none  [body(): terms = lax.all_to_all(terms, 'x', 0, 0, tiled=True)]
    ppermute x3, waiting for transfers between devices: 7.73 us -> 0.01 us  [body(): lax.ppermute(a, 'y', ring(SIDE - step))]
    all_to_all x0 -> x1, waiting for transfers between devices: none -> 6.81 us  [body(): terms = lax.all_to_all(terms, 'x', 0, 0, tiled=True)]
    all_to_all x0 -> x1, starting transfers between devices: none -> 4.82 us  [body(): terms = lax.all_to_all(terms, 'x', 0, 0, tiled=True)]
    ppermute x3, waiting for transfers between devices: 5.45 us -> 8.44 us  [body(): lax.ppermute(a, Z, ring(step))]
    ppermute x3, starting transfers between devices: 4.44 us -> 3.24 us  [body(): lax.ppermute(a, Z, ring(step))]
  transfers between devices with their start and end apart: 15 -> 16, of which waited for: 7 -> 5; matrix products, arithmetic and copies ran while one was open for 3% -> 3% of each run, Pallas kernels for 25% -> 27%
where the time goes in v6:
time: 102 us
  Pallas kernels  31.8 us (31%)
  starting transfers between devices  29.9 us (29%)
  waiting for transfers between devices  23.6 us (23%)
  blocking collectives  10 us (10%)
  other arithmetic  4.45 us (4%)
  local copies, waits for them, and re-layouts  1.53 us (2%)
    pallas_call x7, Pallas kernels, call(): pl.pallas_call(kernel, in_specs=[smem if a is info else vmem for a in ope...  31.8 us
    all_to_all x1, blocking collectives, body(): parts = lax.all_to_all(stats, Z, 0, 0, tiled=True)  10 us
    ppermute x6, starting transfers between devices, spread(): return [lax.ppermute(array, axis, ring(step)) for step in PLACES]  9.07 us
    ppermute x3, waiting for transfers between devices, body(): lax.ppermute(a, Z, ring(step))  8.44 us
    all_to_all x1, waiting for transfers between devices, body(): terms = lax.all_to_all(terms, 'x', 0, 0, tiled=True)  6.81 us
    ppermute x3, starting transfers between devices, body(): lax.ppermute(a, 'y', ring(SIDE - step))  5.01 us
    all_to_all x1, starting transfers between devices, body(): terms = lax.all_to_all(terms, 'x', 0, 0, tiled=True)  4.82 us
    ppermute x1, starting transfers between devices, body(): lax.ppermute(query_weight, Z, [(i, SIDE - 1 - i) for i in range(SIDE)])  4.04 us
  transfers between devices with their start and end apart: 16, of which 5 were waited for; matrix products, arithmetic and copies ran while one was open for 3% of the time, Pallas kernels for 27%

profile of v6, /device:TPU:2, one launch (start us, length us, event | category | flops | bytes accessed | tf_op | source)
XLA Modules:
  0.0 102.1 jit_solution(5667059502593150056)
XLA Ops:
  0.7 1.1 %pad_maximum_fusion.1.pair_ref.p0_ref = bf16[2,512,128]{2,1,0:T(8,128)(2,1)S(1)} fusion(bf16[1,512,128]{2,1,0:T(8,128)(2,1)} %bitcast.12, bf16[1,512,128]{2,1,0:T(8,128)(2,1)} %bitcast.13), kind=kLoop, calls=%fused_computation.2 | loop fusion | flops 131072 | bytes 524288 | tf_op jit(solution)/shard_map/stack | solution.py:257
  1.7 1.6 %collective-permute-start.1 = (bf16[2,512,128]{2,1,0:T(8,128)(2,1)S(1)}, bf16[2,512,128]{2,1,0:T(8,128)(2,1)S(1)}, u32[]{:S(2)}, u32[]{:S(2)}) collective-permute-start(bf16[2,512,128]{2,1,0:T(8,128)(2,1)S(1)} %pad_maximum_fusion.1.pair_ref.p0_ref), channel_id=1, source_target_pairs={{0,8},{8,16},{16,24},{24,0},{1,9},{9,17},{17,25},{25,1},{2,10},{10... | collective-permute-start | bytes 786440 | tf_op jit(solution)/shard_map/ppermute | solution.py:250
  3.4 1.7 %collective-permute-start.2 = (bf16[2,512,128]{2,1,0:T(8,128)(2,1)S(1)}, bf16[2,512,128]{2,1,0:T(8,128)(2,1)S(1)}, u32[]{:S(2)}, u32[]{:S(2)}) collective-permute-start(bf16[2,512,128]{2,1,0:T(8,128)(2,1)S(1)} %pad_maximum_fusion.1.pair_ref.p0_ref), channel_id=1, source_target_pairs={{0,24},{8,0},{16,8},{24,16},{1,25},{9,1},{17,9},{25,17},{2,26},{10... | collective-permute-start | bytes 786440 | tf_op jit(solution)/shard_map/ppermute | solution.py:250
  5.0 2.0 %collective-permute-start.3 = (bf16[2,512,128]{2,1,0:T(8,128)(2,1)S(1)}, bf16[2,512,128]{2,1,0:T(8,128)(2,1)S(1)}, u32[]{:S(2)}, u32[]{:S(2)}) collective-permute-start(bf16[2,512,128]{2,1,0:T(8,128)(2,1)S(1)} %pad_maximum_fusion.1.pair_ref.p0_ref), channel_id=1, source_target_pairs={{0,16},{8,24},{16,0},{24,8},{1,17},{9,25},{17,1},{25,9},{2,18},{10... | collective-permute-start | bytes 786440 | tf_op jit(solution)/shard_map/ppermute | solution.py:250
  7.0 4.0 %collective-permute-start = (bf16[320,640]{1,0:T(8,128)(2,1)}, bf16[320,640]{1,0:T(8,128)(2,1)}, u32[]{:S(2)}, u32[]{:S(2)}) collective-permute-start(bf16[320,640]{1,0:T(8,128)(2,1)} %param.15), channel_id=1, source_target_pairs={{0,96},{32,64},{64,32},{96,0},{1,97},{33,65},{65,33},{97,1},{2,98}... | collective-permute-start | bytes 1228808 | tf_op jit(solution)/shard_map/ppermute | solution.py:259
  11.8 1.5 %dynamic-slice_multiply_fusion = (bf16[4,128,640]{2,1,0:T(8,128)(2,1)S(1)}, bf16[4,128,640]{2,1,0:T(8,128)(2,1)S(1)}) fusion(bf16[4,512,640]{2,1,0:T(8,128)(2,1)} %bitcast.10, s32[]{:T(128)S(6)} %select_n.4, bf16[4,128]{1,0:T(4,128)(2,1)S(1)} %compare_convert_fusion, bf16[4,512,640]{2,1,0:T(8,128)(2,1)} %bitcast.11), kind=kLoop, calls=%fused_computation.1 | loop fusion | flops 1310720 | bytes 2622468 | tf_op jit(solution)/shard_map/mul | solution.py:266
  13.4 3.9 %own_stats.1.former_ref = f32[16,512]{1,0:T(8,128)S(1)} custom-call(s32[3]{0:T(128)S(1)} %pad_add_fusion.info, bf16[4,128,640]{2,1,0:T(8,128)(2,1)S(1)} %get-tuple-element.70.q_ref, bf16[4,128,640]{2,1,0:T(8,128)(2,1)S(1)} %get-tuple-element.69.g_ref, bf16[2,512,128]{2,1,0:T(8,128)(2,1)S(1)} %pad_maximum_fusion.1.pair_ref.p0_ref, ...), custom_call_target="tpu_custom_call" | custom-call | tf_op jit(solution)/shard_map/own_stats/pallas_call | solution.py:272
  17.3 2.7 %collective-permute-done = bf16[320,640]{1,0:T(8,128)(2,1)} collective-permute-done((bf16[320,640]{1,0:T(8,128)(2,1)}, bf16[320,640]{1,0:T(8,128)(2,1)}, u32[]{:S(2)}, u32[]{:S(2)}) %collective-permute-start) | collective-permute-done | bytes 409632 | tf_op jit(solution)/shard_map/ppermute | solution.py:259
  20.0 1.1 %pad_maximum_fusion.w0_ref = bf16[2,320,640]{2,1,0:T(8,128)(2,1)S(1)} fusion(bf16[1,320,640]{2,1,0:T(8,128)(2,1)} %bitcast.6, bf16[1,320,640]{2,1,0:T(8,128)(2,1)S(1)} %bitcast.9), kind=kLoop, calls=%fused_computation | loop fusion | flops 409600 | bytes 1638400 | tf_op jit(solution)/shard_map/stack | solution.py:289
  21.9 2.6 %collective-permute-start.8 = (bf16[2,320,640]{2,1,0:T(8,128)(2,1)S(1)}, bf16[2,320,640]{2,1,0:T(8,128)(2,1)S(1)}, u32[]{:S(2)}, u32[]{:S(2)}) collective-permute-start(bf16[2,320,640]{2,1,0:T(8,128)(2,1)S(1)} %pad_maximum_fusion.w0_ref), channel_id=1, source_target_pairs={{0,24},{8,0},{16,8},{24,16},{1,25},{9,1},{17,9},{25,17},{2,26},{10... | collective-permute-start | bytes 2457608 | tf_op jit(solution)/shard_map/ppermute | solution.py:250
  24.9 6.5 %rest_stats.1 = f32[4,16,512]{2,1,0:T(8,128)S(1)} custom-call(s32[3]{0:T(128)S(1)} %pad_add_fusion.info, bf16[4,128,640]{2,1,0:T(8,128)(2,1)S(1)} %get-tuple-element.70.q_ref, bf16[4,128,640]{2,1,0:T(8,128)(2,1)S(1)} %get-tuple-element.69.g_ref, bf16[2,512,128]{2,1,0:T(8,128)(2,1)S(1)} %collective-permute-done.1.p1_ref, ...), custom_call_target="tpu_custom_call" | custom-call | tf_op jit(solution)/shard_map/rest_stats/pallas_call | solution.py:272
  31.4 10.0 %all_to_all.10.part_ref = f32[4,16,512]{2,1,0:T(8,128)S(1)} all-to-all(f32[4,16,512]{2,1,0:T(8,128)S(1)} %rest_stats.1), channel_id=1, replica_groups=mesh['z_high'=2,'z_low'=2,'y'=4,'x'=4,'core'=2] {'z_high','z_low'}, dimensions={0} | all-to-all | bytes 262144 | tf_op jit(solution)/shard_map/all_to_all | solution.py:298
  41.4 16.2 %local_grads.1 = (bf16[2,128,640]{2,1,0:T(8,128)(2,1)S(1)}, bf16[2,128,640]{2,1,0:T(8,128)(2,1)S(1)}, bf16[2,128,640]{2,1,0:T(8,128)(2,1)S(1)}, bf16[2,128,640]{...) custom-call(s32[3]{0:T(128)S(1)} %pad_add_fusion.info, ...), custom_call_target="tpu_custom_call" | custom-call | tf_op jit(solution)/shard_map/local_grads/pallas_call | solution.py:272
  59.1 2.6 %collective-permute-start.5 = (bf16[2,128,640]{2,1,0:T(8,128)(2,1)S(1)}, bf16[2,128,640]{2,1,0:T(8,128)(2,1)S(1)}, u32[]{:S(2)}, u32[]{:S(2)}) collective-permute-start(bf16[2,128,640]{2,1,0:T(8,128)(2,1)S(1)} %get-tuple-element.44), channel_id=1, source_target_pairs={{0,96},{32,0},{64,32},{96,64},{1,97},{33,1},{65,33},{97,65},{2,98}... | collective-permute-start | bytes 983048 | tf_op jit(solution)/shard_map/ppermute | solution.py:320
  61.7 1.7 %collective-permute-start.10 = (bf16[640,256]{1,0:T(8,128)(2,1)S(1)}, bf16[640,256]{1,0:T(8,128)(2,1)S(1)}, u32[]{:S(2)}, u32[]{:S(2)}) collective-permute-start(bf16[640,256]{1,0:T(8,128)(2,1)S(1)} %get-tuple-element.50), channel_id=1, source_target_pairs={{0,24},{8,0},{16,8},{24,16},{1,25},{9,1},{17,9},{25,17},{2,26},{10... | collective-permute-start | bytes 983048 | tf_op jit(solution)/shard_map/ppermute | solution.py:322
  63.8 8.4 %collective-permute-done.4.d1_ref = bf16[2,128,640]{2,1,0:T(8,128)(2,1)S(1)} collective-permute-done((bf16[2,128,640]{2,1,0:T(8,128)(2,1)S(1)}, bf16[2,128,640]{2,1,0:T(8,128)(2,1)S(1)}, u32[]{:S(2)}, u32[]{:S(2)}) %collective-permute-start.4) | collective-permute-done | bytes 327712 | tf_op jit(solution)/shard_map/ppermute | solution.py:320
  72.3 1.7 %project_theirs.1 = (bf16[2,2,640,128]{3,2,1,0:T(8,128)(2,1)S(1)}, bf16[256,640]{1,0:T(8,128)(2,1)S(1)}) custom-call(s32[3]{0:T(128)S(1)} %pad_add_fusion.info, bf16[2,128,640]{2,1,0:T(8,128)(2,1)S(1)} %get-tuple-element.42.d0_ref, bf16[2,128,640]{2,1,0:T(8,128)(2,1)S(1)} %collective-permute-done.4.d1_ref, ...), custom_call_target="tpu_custom_call" | custom-call | tf_op jit(solution)/shard_map/project_theirs/pallas_call | solution.py:272
  74.1 2.1 %collective-permute-done.12.theirs_ref = bf16[2,2,640,128]{3,2,1,0:T(8,128)(2,1)S(1)} collective-permute-done((bf16[2,2,640,128]{3,2,1,0:T(8,128)(2,1)S(1)}, bf16[2,2,640,128]{3,2,1,0:T(8,128)(2,1)S(1)}, u32[]{:S(2)}, u32[]{:S(2)}) %collective-permute-start.12) | collective-permute-done | bytes 655392 | tf_op jit(solution)/shard_map/ppermute | solution.py:331
  76.2 2.4 %project_mine.1 = bf16[4,640,128]{2,1,0:T(8,128)(2,1)} custom-call(s32[3]{0:T(128)S(1)} %pad_add_fusion.info, bf16[256,640]{1,0:T(8,128)(2,1)S(1)} %get-tuple-element.59.rows_ref, bf16[2,2,640,128]{3,2,1,0:T(8,128)(2,1)S(1)} %collective-permute-done.12.theirs_ref, bf16[2,320,640]{2,1,0:T(8,128)(2,1)S(1)} %pad_maximum_fusion.w0_ref, ...), custom_call_target="tpu_custom_call" | custom-call | tf_op jit(solution)/shard_map/project_mine/pallas_call | solution.py:272
  78.6 4.8 %all-to-all-start.1 = ((bf16[4,640,128]{2,1,0:T(8,128)(2,1)}), bf16[4,640,128]{2,1,0:T(8,128)(2,1)S(1)}, u32[]{:S(2)}, u32[]{:S(2)}) async-start(bf16[4,640,128]{2,1,0:T(8,128)(2,1)} %project_mine.1), calls=%async_computation.1 | async-start | bytes 1310720 | tf_op jit(solution)/shard_map/all_to_all | solution.py:338
  83.4 2.9 %collective-permute-start.14 = (bf16[640,256]{1,0:T(8,128)(2,1)S(1)}, bf16[640,256]{1,0:T(8,128)(2,1)S(1)}, u32[]{:S(2)}, u32[]{:S(2)}) collective-permute-start(bf16[640,256]{1,0:T(8,128)(2,1)S(1)} %copy-done.5), channel_id=1, source_target_pairs={{0,16},{8,24},{16,0},{24,8},{1,17},{9,25},{17,1},{25,9},{2,18},{10... | collective-permute-start | bytes 983048 | tf_op jit(solution)/shard_map/ppermute | solution.py:322
  86.4 6.8 %all-to-all-done.1.parts_ref = bf16[4,640,128]{2,1,0:T(8,128)(2,1)S(1)} async-done(((bf16[4,640,128]{2,1,0:T(8,128)(2,1)}), bf16[4,640,128]{2,1,0:T(8,128)(2,1)S(1)}, u32[]{:S(2)}, u32[]{:S(2)}) %all-to-all-start.1) | async-done | bytes 655392 | tf_op jit(solution)/shard_map/all_to_all | solution.py:338
  93.3 3.7 %collective-permute-start.13 = (bf16[128,640]{1,0:T(8,128)(2,1)S(1)}, bf16[128,640]{1,0:T(8,128)(2,1)S(1)}, u32[]{:S(2)}, u32[]{:S(2)}) collective-permute-start(bf16[128,640]{1,0:T(8,128)(2,1)S(1)} %sum_groups.1), channel_id=1, source_target_pairs={{0,0},{2,32},{4,38},{6,6},{32,2},{34,34},{36,36},{38,4},{64,98},{6... | collective-permute-start | bytes 491528 | tf_op jit(solution)/shard_map/ppermute | solution.py:345
  97.9 3.5 %collective-permute-done.13 = bf16[128,640]{1,0:T(8,128)(2,1)S(1)} collective-permute-done((bf16[128,640]{1,0:T(8,128)(2,1)S(1)}, bf16[128,640]{1,0:T(8,128)(2,1)S(1)}, u32[]{:S(2)}, u32[]{:S(2)}) %collective-permute-start.13) | collective-permute-done | bytes 163872 | tf_op jit(solution)/shard_map/ppermute | solution.py:345
  (37 shorter events, 5.7 us)
Async XLA Ops:
  0.6 12.7 %copy-start = (bf16[2048,128]{1,0:T(8,128)(2,1)S(1)}, bf16[2048,128]{1,0:T(8,128)(2,1)}, u32[]{:S(2)}) copy-start(bf16[2048,128]{1,0:T(8,128)(2,1)} %sk_ref.3) | copy-start | bytes 1572868
  0.6 12.7 %copy-start.1 = (bf16[2048,128]{1,0:T(8,128)(2,1)S(1)}, bf16[2048,128]{1,0:T(8,128)(2,1)}, u32[]{:S(2)}) copy-start(bf16[2048,128]{1,0:T(8,128)(2,1)} %sv_ref.3) | copy-start | bytes 1572868
  1.7 19.4 %collective-permute-start.1 = (bf16[2,512,128]{2,1,0:T(8,128)(2,1)S(1)}, bf16[2,512,128]{2,1,0:T(8,128)(2,1)S(1)}, u32[]{:S(2)}, u32[]{:S(2)}) collective-permute-start(bf16[2,512,128]{2,1,0:T(8,128)(2,1)S(1)} %pad_maximum_fusion.1.pair_ref.p0_ref), channel_id=1, source_target_pairs={{0,8},{8,16},{16,24},{24,0},{1,9},{9,17},{17,25},{25,1},{2,10},{10... | collective-permute-start | bytes 786440 | tf_op jit(solution)/shard_map/ppermute | solution.py:250
  3.4 17.7 %collective-permute-start.2 = (bf16[2,512,128]{2,1,0:T(8,128)(2,1)S(1)}, bf16[2,512,128]{2,1,0:T(8,128)(2,1)S(1)}, u32[]{:S(2)}, u32[]{:S(2)}) collective-permute-start(bf16[2,512,128]{2,1,0:T(8,128)(2,1)S(1)} %pad_maximum_fusion.1.pair_ref.p0_ref), channel_id=1, source_target_pairs={{0,24},{8,0},{16,8},{24,16},{1,25},{9,1},{17,9},{25,17},{2,26},{10... | collective-permute-start | bytes 786440 | tf_op jit(solution)/shard_map/ppermute | solution.py:250
  5.0 16.1 %collective-permute-start.3 = (bf16[2,512,128]{2,1,0:T(8,128)(2,1)S(1)}, bf16[2,512,128]{2,1,0:T(8,128)(2,1)S(1)}, u32[]{:S(2)}, u32[]{:S(2)}) collective-permute-start(bf16[2,512,128]{2,1,0:T(8,128)(2,1)S(1)} %pad_maximum_fusion.1.pair_ref.p0_ref), channel_id=1, source_target_pairs={{0,16},{8,24},{16,0},{24,8},{1,17},{9,25},{17,1},{25,9},{2,18},{10... | collective-permute-start | bytes 786440 | tf_op jit(solution)/shard_map/ppermute | solution.py:250
  7.0 13.0 %collective-permute-start = (bf16[320,640]{1,0:T(8,128)(2,1)}, bf16[320,640]{1,0:T(8,128)(2,1)}, u32[]{:S(2)}, u32[]{:S(2)}) collective-permute-start(bf16[320,640]{1,0:T(8,128)(2,1)} %param.15), channel_id=1, source_target_pairs={{0,96},{32,64},{64,32},{96,0},{1,97},{33,65},{65,33},{97,1},{2,98}... | collective-permute-start | bytes 1228808 | tf_op jit(solution)/shard_map/ppermute | solution.py:259
  13.3 6.7 %copy-start.6 = (bf16[320,640]{1,0:T(8,128)(2,1)S(1)}, bf16[320,640]{1,0:T(8,128)(2,1)}, u32[]{:S(2)}) copy-start(bf16[320,640]{1,0:T(8,128)(2,1)} %param.15) | copy-start | bytes 1228804
  21.1 40.6 %collective-permute-start.7 = (bf16[2,320,640]{2,1,0:T(8,128)(2,1)S(1)}, bf16[2,320,640]{2,1,0:T(8,128)(2,1)S(1)}, u32[]{:S(2)}, u32[]{:S(2)}) collective-permute-start(bf16[2,320,640]{2,1,0:T(8,128)(2,1)S(1)} %pad_maximum_fusion.w0_ref), channel_id=1, source_target_pairs={{0,8},{8,16},{16,24},{24,0},{1,9},{9,17},{17,25},{25,1},{2,10},{10... | collective-permute-start | bytes 2457608 | tf_op jit(solution)/shard_map/ppermute | solution.py:250
  21.9 39.8 %collective-permute-start.8 = (bf16[2,320,640]{2,1,0:T(8,128)(2,1)S(1)}, bf16[2,320,640]{2,1,0:T(8,128)(2,1)S(1)}, u32[]{:S(2)}, u32[]{:S(2)}) collective-permute-start(bf16[2,320,640]{2,1,0:T(8,128)(2,1)S(1)} %pad_maximum_fusion.w0_ref), channel_id=1, source_target_pairs={{0,24},{8,0},{16,8},{24,16},{1,25},{9,1},{17,9},{25,17},{2,26},{10... | collective-permute-start | bytes 2457608 | tf_op jit(solution)/shard_map/ppermute | solution.py:250
  24.4 37.3 %collective-permute-start.9 = (bf16[2,320,640]{2,1,0:T(8,128)(2,1)S(1)}, bf16[2,320,640]{2,1,0:T(8,128)(2,1)S(1)}, u32[]{:S(2)}, u32[]{:S(2)}) collective-permute-start(bf16[2,320,640]{2,1,0:T(8,128)(2,1)S(1)} %pad_maximum_fusion.w0_ref), channel_id=1, source_target_pairs={{0,16},{8,24},{16,0},{24,8},{1,17},{9,25},{17,1},{25,9},{2,18},{10... | collective-permute-start | bytes 2457608 | tf_op jit(solution)/shard_map/ppermute | solution.py:250
  57.6 0.8 copy-start.2
  58.5 17.7 %copy-start.4 = (bf16[640,256]{1,0:T(8,128)(2,1)}, bf16[640,256]{1,0:T(8,128)(2,1)S(1)}, u32[]{:S(2)}) copy-start(bf16[640,256]{1,0:T(8,128)(2,1)S(1)} %get-tuple-element.64) | copy-start | bytes 983044
  58.5 13.8 %collective-permute-start.4 = (bf16[2,128,640]{2,1,0:T(8,128)(2,1)S(1)}, bf16[2,128,640]{2,1,0:T(8,128)(2,1)S(1)}, u32[]{:S(2)}, u32[]{:S(2)}) collective-permute-start(bf16[2,128,640]{2,1,0:T(8,128)(2,1)S(1)} %get-tuple-element.43), channel_id=1, source_target_pairs={{0,32},{32,64},{64,96},{96,0},{1,33},{33,65},{65,97},{97,1},{2,34}... | collective-permute-start | bytes 983048 | tf_op jit(solution)/shard_map/ppermute | solution.py:320
  59.1 13.2 %collective-permute-start.5 = (bf16[2,128,640]{2,1,0:T(8,128)(2,1)S(1)}, bf16[2,128,640]{2,1,0:T(8,128)(2,1)S(1)}, u32[]{:S(2)}, u32[]{:S(2)}) collective-permute-start(bf16[2,128,640]{2,1,0:T(8,128)(2,1)S(1)} %get-tuple-element.44), channel_id=1, source_target_pairs={{0,96},{32,0},{64,32},{96,64},{1,97},{33,1},{65,33},{97,65},{2,98}... | collective-permute-start | bytes 983048 | tf_op jit(solution)/shard_map/ppermute | solution.py:320
  61.7 10.6 %collective-permute-start.6 = (bf16[2,128,640]{2,1,0:T(8,128)(2,1)S(1)}, bf16[2,128,640]{2,1,0:T(8,128)(2,1)S(1)}, u32[]{:S(2)}, u32[]{:S(2)}) collective-permute-start(bf16[2,128,640]{2,1,0:T(8,128)(2,1)S(1)} %get-tuple-element.45), channel_id=1, source_target_pairs={{0,64},{32,96},{64,0},{96,32},{1,65},{33,97},{65,1},{97,33},{2,66}... | collective-permute-start | bytes 983048 | tf_op jit(solution)/shard_map/ppermute | solution.py:320
  61.7 10.5 %collective-permute-start.10 = (bf16[640,256]{1,0:T(8,128)(2,1)S(1)}, bf16[640,256]{1,0:T(8,128)(2,1)S(1)}, u32[]{:S(2)}, u32[]{:S(2)}) collective-permute-start(bf16[640,256]{1,0:T(8,128)(2,1)S(1)} %get-tuple-element.50), channel_id=1, source_target_pairs={{0,24},{8,0},{16,8},{24,16},{1,25},{9,1},{17,9},{25,17},{2,26},{10... | collective-permute-start | bytes 983048 | tf_op jit(solution)/shard_map/ppermute | solution.py:322
  63.5 8.8 %collective-permute-start.11 = (bf16[640,256]{1,0:T(8,128)(2,1)S(1)}, bf16[640,256]{1,0:T(8,128)(2,1)S(1)}, u32[]{:S(2)}, u32[]{:S(2)}) collective-permute-start(bf16[640,256]{1,0:T(8,128)(2,1)S(1)} %get-tuple-element.51), channel_id=1, source_target_pairs={{0,8},{8,16},{16,24},{24,0},{1,9},{9,17},{17,25},{25,1},{2,10},{10... | collective-permute-start | bytes 983048 | tf_op jit(solution)/shard_map/ppermute | solution.py:322
  74.0 2.2 %collective-permute-start.12 = (bf16[2,2,640,128]{3,2,1,0:T(8,128)(2,1)S(1)}, bf16[2,2,640,128]{3,2,1,0:T(8,128)(2,1)S(1)}, u32[]{:S(2)}, u32[]{:S(2)}) collective-permute-start(bf16[2,2,640,128]{3,2,1,0:T(8,128)(2,1)S(1)} %get-tuple-element.60), channel_id=1, source_target_pairs={{0,1},{1,0},{2,3},{3,2},{4,5},{5,4},{6,7},{7,6},{8,9},{9,8},{10,11... | collective-permute-start | bytes 1966088 | tf_op jit(solution)/shard_map/ppermute | solution.py:331
  76.2 7.2 %copy-start.5 = (bf16[640,256]{1,0:T(8,128)(2,1)S(1)}, bf16[640,256]{1,0:T(8,128)(2,1)}, u32[]{:S(2)}) copy-start(bf16[640,256]{1,0:T(8,128)(2,1)} %copy-done.4) | copy-start | bytes 983044
  76.2 20.8 %copy-start.3 = (f32[640,256]{1,0:T(8,128)S(1)}, f32[640,256]{1,0:T(8,128)}, u32[]{:S(2)}) copy-start(f32[640,256]{1,0:T(8,128)} %copy-done.2) | copy-start | bytes 1966084
  78.6 14.6 %all-to-all-start.1 = ((bf16[4,640,128]{2,1,0:T(8,128)(2,1)}), bf16[4,640,128]{2,1,0:T(8,128)(2,1)S(1)}, u32[]{:S(2)}, u32[]{:S(2)}) async-start(bf16[4,640,128]{2,1,0:T(8,128)(2,1)} %project_mine.1), calls=%async_computation.1 | async-start | bytes 1310720 | tf_op jit(solution)/shard_map/all_to_all | solution.py:338
  83.4 13.6 %collective-permute-start.14 = (bf16[640,256]{1,0:T(8,128)(2,1)S(1)}, bf16[640,256]{1,0:T(8,128)(2,1)S(1)}, u32[]{:S(2)}, u32[]{:S(2)}) collective-permute-start(bf16[640,256]{1,0:T(8,128)(2,1)S(1)} %copy-done.5), channel_id=1, source_target_pairs={{0,16},{8,24},{16,0},{24,8},{1,17},{9,25},{17,1},{25,9},{2,18},{10... | collective-permute-start | bytes 983048 | tf_op jit(solution)/shard_map/ppermute | solution.py:322
  93.3 8.1 %collective-permute-start.13 = (bf16[128,640]{1,0:T(8,128)(2,1)S(1)}, bf16[128,640]{1,0:T(8,128)(2,1)S(1)}, u32[]{:S(2)}, u32[]{:S(2)}) collective-permute-start(bf16[128,640]{1,0:T(8,128)(2,1)S(1)} %sum_groups.1), channel_id=1, source_target_pairs={{0,0},{2,32},{4,38},{6,6},{32,2},{34,34},{36,36},{38,4},{64,98},{6... | collective-permute-start | bytes 491528 | tf_op jit(solution)/shard_map/ppermute | solution.py:345

commit v7 on v6

--- a/solution.py
+++ b/solution.py
@@ -19,6 +19,7 @@
 STATS = 16
 SIDE = 4
 LOW = -1e30
+HIGH = 1e30
 PLACES = (1, 3, 2)
 Z = ("z_high", "z_low")
 BF16 = jnp.bfloat16
@@ -100,24 +101,43 @@
         wide = [jnp.concatenate([item[:, head * HD : (head + 1) * HD]] * SIDE, axis=1) for item in own]
         put_stats(out_ref, head, [jnp.where(mine, a, b) for a, b in zip(wide, (LOW, 0.0, 0.0))])
 
-    @pl.loop(0, GROUP)
+    @pl.loop(0, GROUP, unroll=True)
     def _(head):
         found = block_stats(load_head(q_ref, head), load_head(g_ref, head), pair_ref[0], pair_ref[1])
         put_stats(out_ref, head, merge([found, get_stats(out_ref, head)]))
 
 
-def rest_stats_kernel(info, q_ref, g_ref, p1_ref, p2_ref, p3_ref, former_ref, out_ref):
+def rest_stats_kernel(info, q_ref, g_ref, *refs):
+    pair_refs, former_ref, out_ref = refs[:-2], refs[-2], refs[-1]
+    wide = len(out_ref.shape) > 2
+
+    def put(head, found):
+        for copy in range(SIDE if wide else 1):
+            put_stats(out_ref.at[copy] if wide else out_ref, head, found)
+
     out_ref[...] = jnp.zeros_like(out_ref)
 
-    @pl.loop(0, GROUP)
+    @pl.loop(0, GROUP, unroll=True)
     def _(head):
         q, g = load_head(q_ref, head), load_head(g_ref, head)
-        found = [get_stats(former_ref, head)]
-        for ref in (p1_ref, p2_ref, p3_ref):
-            found.append(block_stats(q, g, ref[0], ref[1]))
-        found = merge(found)
-        for copy in range(SIDE):
-            put_stats(out_ref.at[copy], head, found)
+        top, total, mixed = get_stats(former_ref, head)
+        for ref in pair_refs:
+            weights = jnp.exp2(dot_nt(ref[0], q) * LOG_FACTOR - top)
+            total = total + jnp.sum(weights, axis=0, keepdims=True)
+            mixed = mixed + jnp.sum(weights * dot_nt(ref[1], g), axis=0, keepdims=True)
+        put(head, (top, total, mixed))
+
+    sums = (out_ref.at[0] if wide else out_ref)[GROUP : 2 * GROUP, :]
+
+    @pl.when(jnp.logical_not(jnp.max(sums) < HIGH))
+    def _():
+        @pl.loop(0, GROUP)
+        def _(head):
+            q, g = load_head(q_ref, head), load_head(g_ref, head)
+            found = [get_stats(former_ref, head)]
+            for ref in pair_refs:
+                found.append(block_stats(q, g, ref[0], ref[1]))
+            put(head, merge(found))
 
 
 def score_grads(k, v, q, g, log_sum, delta, allowed=None):
@@ -158,7 +178,7 @@
     dself_key_ref[...] = dot_nn(dscores, q)
     dself_query_ref[...] = dot_nn(keys.T, dscores)
 
-    @pl.loop(0, GROUP)
+    @pl.loop(0, GROUP, unroll=True)
     def _(head):
         log_sum = stat_ref[pl.ds(head, 1), :]
         delta = stat_ref[pl.ds(GROUP + head, 1), :]
@@ -196,10 +216,8 @@
     dsv_ref[...] = total[L:, HD:]
 
 
-def sum_turn_kernel(parts_ref, out_ref):
-    total = parts_ref[0].astype(F32)
-    for part in range(1, parts_ref.shape[0]):
-        total = total + parts_ref[part].astype(F32)
+def sum_turn_kernel(a_ref, b_ref, c_ref, d_ref, out_ref):
+    total = sum(ref[...].astype(F32) for ref in (a_ref, b_ref, c_ref, d_ref))
     out_ref[...] = total.T.astype(BF16)
 
 
@@ -231,7 +249,7 @@
 
 
 def project_mine_kernel(
-    info, rows_ref, theirs_ref, w0_ref, w1_ref, w2_ref, w3_ref, out_ref
+    info, rows_ref, theirs_ref, w0_ref, w1_ref, w2_ref, w3_ref, o0_ref, o1_ref, o2_ref, o3_ref, out_ref
 ):
     columns = (info[0], SIDE - 1 - info[0])
 
@@ -240,6 +258,8 @@
         out_ref[columns[block] ^ part, at, :] = terms.astype(BF16)
 
     project_blocks(info, (w0_ref, w1_ref, w2_ref, w3_ref), info[2], rows_ref[...], put)
+    for step, ref in zip((0,) + PLACES, (o0_ref, o1_ref, o2_ref, o3_ref)):
+        ref[...] = out_ref[lax.rem(info[3] + step, SIDE)]
 
 
 def ring(step):
@@ -253,7 +273,7 @@
 def body(queries, doc_keys, doc_values, self_keys, self_values, out_grads, lengths, query_weight):
     doc_rows = doc_keys.shape[0]
     place_y = lax.axis_index("y").astype(jnp.int32)
-    info = jnp.stack([lax.axis_index(Z).astype(jnp.int32), place_y, lax.axis_index("core").astype(jnp.int32)])
+    info = jnp.stack([lax.axis_index(Z).astype(jnp.int32), place_y, lax.axis_index("core").astype(jnp.int32), lax.axis_index("x").astype(jnp.int32)])
     pair = jnp.stack([doc_keys, doc_values])
     pairs = [pair] + spread(pair, "y")
     other = lax.ppermute(query_weight, Z, [(i, SIDE - 1 - i) for i in range(SIDE)])
@@ -329,14 +349,15 @@
         "project_theirs",
     )
     theirs = lax.ppermute(theirs, "core", [(0, 1), (1, 0)])
-    terms = call(
+    term, *terms = call(
         project_mine_kernel,
-        shape((SIDE, columns, HD), BF16),
+        [shape((columns, HD), BF16)] * SIDE,
         (info, rows, theirs, *weights),
         "project_mine",
-    )
-    terms = lax.all_to_all(terms, "x", 0, 0, tiled=True)
-    input_grads = call(sum_turn_kernel, shape((HD, columns), BF16), (terms,), "sum_groups")
+        scratch=[pltpu.VMEM((SIDE, columns, HD), BF16)],
+    )
+    terms = [lax.ppermute(a, "x", ring(step)) for step, a in zip(PLACES, terms)]
+    input_grads = call(sum_turn_kernel, shape((HD, columns), BF16), (term, *terms), "sum_groups")
     moves = []
     for z in range(SIDE):
         for x in range(SIDE):

time: 102 us -> 96.1 us (0.942)
  Pallas kernels: 31.8 us -> 26.8 us
  starting transfers between devices: 29.9 us -> 28.5 us
  waiting for transfers between devices: 23.6 us -> 24.7 us
    ppermute x0 -> x3, waiting for transfers between devices: none -> 7.46 us  [body(): terms = [lax.ppermute(a, 'x', ring(step)) for step, a in zip(PLACES, terms)]]
    all_to_all x1 -> x0, waiting for transfers between devices: 6.81 us -> none  [body(): terms = lax.all_to_all(terms, 'x', 0, 0, tiled=True)]
    pallas_call x7, Pallas kernels: 31.8 us -> 26.8 us  [call(): pl.pallas_call(kernel, in_specs=[smem if a is info else vmem for a in ope...]
    all_to_all x1 -> x0, starting transfers between devices: 4.82 us -> none  [body(): terms = lax.all_to_all(terms, 'x', 0, 0, tiled=True)]
    ppermute x0 -> x3, starting transfers between devices: none -> 4.2 us  [body(): terms = [lax.ppermute(a, 'x', ring(step)) for step, a in zip(PLACES, terms)]]
    ppermute x3, waiting for transfers between devices: 8.44 us -> 6.58 us  [body(): lax.ppermute(a, Z, ring(step))]
    ppermute x1, waiting for transfers between devices: 2.08 us -> 0.45 us  [body(): theirs = lax.ppermute(theirs, 'core', [(0, 1), (1, 0)])]
    ppermute x3, starting transfers between devices: 3.24 us -> 4.61 us  [body(): lax.ppermute(a, Z, ring(step))]
  transfers between devices with their start and end apart: 16 -> 18, of which waited for: 5 -> 9; matrix products, arithmetic and copies ran while one was open for 3% -> 4% of each run, Pallas kernels for 27% -> 26%
where the time goes in v7:
time: 96.1 us; the launch traced here: 95.9 us
  starting transfers between devices  28.5 us (30%)
  Pallas kernels  26.8 us (28%)
  waiting for transfers between devices  24.7 us (26%)
  blocking collectives  10 us (10%)
  other arithmetic  4.45 us (5%)
    pallas_call x7, Pallas kernels, call(): pl.pallas_call(kernel, in_specs=[smem if a is info else vmem for a in ope...  26.8 us
    all_to_all x1, blocking collectives, body(): parts = lax.all_to_all(stats, Z, 0, 0, tiled=True)  10 us
    ppermute x6, starting transfers between devices, spread(): return [lax.ppermute(array, axis, ring(step)) for step in PLACES]  9.07 us
    ppermute x3, waiting for transfers between devices, body(): terms = [lax.ppermute(a, 'x', ring(step)) for step, a in zip(PLACES, terms)]  7.46 us
    ppermute x3, waiting for transfers between devices, body(): lax.ppermute(a, Z, ring(step))  6.58 us
    ppermute x3, starting transfers between devices, body(): lax.ppermute(a, Z, ring(step))  4.61 us
    ppermute x1, waiting for transfers between devices, body(): input_grads = lax.ppermute(input_grads, Z + ('x',), moves)  4.34 us
    ppermute x3, starting transfers between devices, body(): terms = [lax.ppermute(a, 'x', ring(step)) for step, a in zip(PLACES, terms)]  4.2 us
  transfers between devices with their start and end apart: 18, of which 9 were waited for; matrix products, arithmetic and copies ran while one was open for 4% of the time, Pallas kernels for 26%

profile of v7, /device:TPU:2, one launch (start us, length us, event | category | flops | bytes accessed | tf_op | source)
XLA Modules:
  0.0 95.9 jit_solution(12706629139104073207)
XLA Ops:
  1.7 1.6 %collective-permute-start.1 = (bf16[2,512,128]{2,1,0:T(8,128)(2,1)S(1)}, bf16[2,512,128]{2,1,0:T(8,128)(2,1)S(1)}, u32[]{:S(2)}, u32[]{:S(2)}) collective-permute-start(bf16[2,512,128]{2,1,0:T(8,128)(2,1)S(1)} %pad_maximum_fusion.1.pair_ref.p0_ref), channel_id=1, source_target_pairs={{0,8},{8,16},{16,24},{24,0},{1,9},{9,17},{17,25},{25,1},{2,10},{10... | collective-permute-start | bytes 786440 | tf_op jit(solution)/shard_map/ppermute | solution.py:270
  3.4 1.7 %collective-permute-start.2 = (bf16[2,512,128]{2,1,0:T(8,128)(2,1)S(1)}, bf16[2,512,128]{2,1,0:T(8,128)(2,1)S(1)}, u32[]{:S(2)}, u32[]{:S(2)}) collective-permute-start(bf16[2,512,128]{2,1,0:T(8,128)(2,1)S(1)} %pad_maximum_fusion.1.pair_ref.p0_ref), channel_id=1, source_target_pairs={{0,24},{8,0},{16,8},{24,16},{1,25},{9,1},{17,9},{25,17},{2,26},{10... | collective-permute-start | bytes 786440 | tf_op jit(solution)/shard_map/ppermute | solution.py:270
  5.0 2.0 %collective-permute-start.3 = (bf16[2,512,128]{2,1,0:T(8,128)(2,1)S(1)}, bf16[2,512,128]{2,1,0:T(8,128)(2,1)S(1)}, u32[]{:S(2)}, u32[]{:S(2)}) collective-permute-start(bf16[2,512,128]{2,1,0:T(8,128)(2,1)S(1)} %pad_maximum_fusion.1.pair_ref.p0_ref), channel_id=1, source_target_pairs={{0,16},{8,24},{16,0},{24,8},{1,17},{9,25},{17,1},{25,9},{2,18},{10... | collective-permute-start | bytes 786440 | tf_op jit(solution)/shard_map/ppermute | solution.py:270
  7.0 4.0 %collective-permute-start = (bf16[320,640]{1,0:T(8,128)(2,1)}, bf16[320,640]{1,0:T(8,128)(2,1)}, u32[]{:S(2)}, u32[]{:S(2)}) collective-permute-start(bf16[320,640]{1,0:T(8,128)(2,1)} %param.15), channel_id=1, source_target_pairs={{0,96},{32,64},{64,32},{96,0},{1,97},{33,65},{65,33},{97,1},{2,98}... | collective-permute-start | bytes 1228808 | tf_op jit(solution)/shard_map/ppermute | solution.py:279
  11.8 1.5 %dynamic-slice_multiply_fusion = (bf16[4,128,640]{2,1,0:T(8,128)(2,1)S(1)}, bf16[4,128,640]{2,1,0:T(8,128)(2,1)S(1)}) fusion(bf16[4,512,640]{2,1,0:T(8,128)(2,1)} %bitcast.11, s32[]{:T(128)S(6)} %select_n.4, bf16[4,128]{1,0:T(4,128)(2,1)S(1)} %compare_convert_fusion, bf16[4,512,640]{2,1,0:T(8,128)(2,1)} %bitcast.12), kind=kLoop, calls=%fused_computation.1 | loop fusion | flops 1310720 | bytes 2622468 | tf_op jit(solution)/shard_map/mul | solution.py:286
  13.4 2.8 %own_stats.1.refs_3_ = f32[16,512]{1,0:T(8,128)S(1)} custom-call(s32[4]{0:T(128)S(1)} %pad_add_fusion.info, bf16[4,128,640]{2,1,0:T(8,128)(2,1)S(1)} %get-tuple-element.78.q_ref, bf16[4,128,640]{2,1,0:T(8,128)(2,1)S(1)} %get-tuple-element.77.g_ref, bf16[2,512,128]{2,1,0:T(8,128)(2,1)S(1)} %pad_maximum_fusion.1.pair_ref.p0_ref, ...), custom_call_target="tpu_custom_call" | custom-call | tf_op jit(solution)/shard_map/own_stats/pallas_call | solution.py:292
  16.2 3.8 %collective-permute-done = bf16[320,640]{1,0:T(8,128)(2,1)} collective-permute-done((bf16[320,640]{1,0:T(8,128)(2,1)}, bf16[320,640]{1,0:T(8,128)(2,1)}, u32[]{:S(2)}, u32[]{:S(2)}) %collective-permute-start) | collective-permute-done | bytes 409632 | tf_op jit(solution)/shard_map/ppermute | solution.py:279
  21.9 2.6 %collective-permute-start.8 = (bf16[2,320,640]{2,1,0:T(8,128)(2,1)S(1)}, bf16[2,320,640]{2,1,0:T(8,128)(2,1)S(1)}, u32[]{:S(2)}, u32[]{:S(2)}) collective-permute-start(bf16[2,320,640]{2,1,0:T(8,128)(2,1)S(1)} %pad_maximum_fusion.w0_ref), channel_id=1, source_target_pairs={{0,24},{8,0},{16,8},{24,16},{1,25},{9,1},{17,9},{25,17},{2,26},{10... | collective-permute-start | bytes 2457608 | tf_op jit(solution)/shard_map/ppermute | solution.py:270
  24.9 4.9 %rest_stats.1 = f32[4,16,512]{2,1,0:T(8,128)S(1)} custom-call(s32[4]{0:T(128)S(1)} %pad_add_fusion.info, bf16[4,128,640]{2,1,0:T(8,128)(2,1)S(1)} %get-tuple-element.78.q_ref, bf16[4,128,640]{2,1,0:T(8,128)(2,1)S(1)} %get-tuple-element.77.g_ref, bf16[2,512,128]{2,1,0:T(8,128)(2,1)S(1)} %collective-permute-done.1.refs_0_.p1_ref, ...), custom_call_target="tpu_custom_call" | custom-call | tf_op jit(solution)/shard_map/rest_stats/pallas_call | solution.py:292
  29.8 10.0 %all_to_all.5.part_ref = f32[4,16,512]{2,1,0:T(8,128)S(1)} all-to-all(f32[4,16,512]{2,1,0:T(8,128)S(1)} %rest_stats.1), channel_id=1, replica_groups=mesh['z_high'=2,'z_low'=2,'y'=4,'x'=4,'core'=2] {'z_high','z_low'}, dimensions={0} | all-to-all | bytes 262144 | tf_op jit(solution)/shard_map/all_to_all | solution.py:318
  39.8 14.7 %local_grads.1 = (bf16[2,128,640]{2,1,0:T(8,128)(2,1)S(1)}, bf16[2,128,640]{2,1,0:T(8,128)(2,1)S(1)}, bf16[2,128,640]{2,1,0:T(8,128)(2,1)S(1)}, bf16[2,128,640]{...) custom-call(s32[4]{0:T(128)S(1)} %pad_add_fusion.info, ...), custom_call_target="tpu_custom_call" | custom-call | tf_op jit(solution)/shard_map/local_grads/pallas_call | solution.py:292
  55.2 2.7 %collective-permute-start.5 = (bf16[2,128,640]{2,1,0:T(8,128)(2,1)S(1)}, bf16[2,128,640]{2,1,0:T(8,128)(2,1)S(1)}, u32[]{:S(2)}, u32[]{:S(2)}) collective-permute-start(bf16[2,128,640]{2,1,0:T(8,128)(2,1)S(1)} %get-tuple-element.48), channel_id=1, source_target_pairs={{0,96},{32,0},{64,32},{96,64},{1,97},{33,1},{65,33},{97,65},{2,98}... | collective-permute-start | bytes 983048 | tf_op jit(solution)/shard_map/ppermute | solution.py:340
  59.8 1.7 %collective-permute-start.10 = (bf16[640,256]{1,0:T(8,128)(2,1)S(1)}, bf16[640,256]{1,0:T(8,128)(2,1)S(1)}, u32[]{:S(2)}, u32[]{:S(2)}) collective-permute-start(bf16[640,256]{1,0:T(8,128)(2,1)S(1)} %get-tuple-element.54), channel_id=1, source_target_pairs={{0,24},{8,0},{16,8},{24,16},{1,25},{9,1},{17,9},{25,17},{2,26},{10... | collective-permute-start | bytes 983048 | tf_op jit(solution)/shard_map/ppermute | solution.py:342
  61.8 6.6 %collective-permute-done.4.d1_ref = bf16[2,128,640]{2,1,0:T(8,128)(2,1)S(1)} collective-permute-done((bf16[2,128,640]{2,1,0:T(8,128)(2,1)S(1)}, bf16[2,128,640]{2,1,0:T(8,128)(2,1)S(1)}, u32[]{:S(2)}, u32[]{:S(2)}) %collective-permute-start.4) | collective-permute-done | bytes 327712 | tf_op jit(solution)/shard_map/ppermute | solution.py:340
  68.4 1.3 %collective-permute-done.11.b2_ref = bf16[640,256]{1,0:T(8,128)(2,1)S(1)} collective-permute-done((bf16[640,256]{1,0:T(8,128)(2,1)S(1)}, bf16[640,256]{1,0:T(8,128)(2,1)S(1)}, u32[]{:S(2)}, u32[]{:S(2)}) %collective-permute-start.11) | collective-permute-done | bytes 327712 | tf_op jit(solution)/shard_map/ppermute | solution.py:342
  69.7 1.7 %project_theirs.1 = (bf16[2,2,640,128]{3,2,1,0:T(8,128)(2,1)S(1)}, bf16[256,640]{1,0:T(8,128)(2,1)S(1)}) custom-call(s32[4]{0:T(128)S(1)} %pad_add_fusion.info, bf16[2,128,640]{2,1,0:T(8,128)(2,1)S(1)} %get-tuple-element.46.d0_ref, bf16[2,128,640]{2,1,0:T(8,128)(2,1)S(1)} %collective-permute-done.4.d1_ref, ...), custom_call_target="tpu_custom_call" | custom-call | tf_op jit(solution)/shard_map/project_theirs/pallas_call | solution.py:292
  71.6 1.6 %collective-permute-start.17 = (bf16[640,256]{1,0:T(8,128)(2,1)S(1)}, bf16[640,256]{1,0:T(8,128)(2,1)S(1)}, u32[]{:S(2)}, u32[]{:S(2)}) collective-permute-start(bf16[640,256]{1,0:T(8,128)(2,1)S(1)} %get-tuple-element.72), channel_id=1, source_target_pairs={{0,16},{8,24},{16,0},{24,8},{1,17},{9,25},{17,1},{25,9},{2,18},{10... | collective-permute-start | bytes 983048 | tf_op jit(solution)/shard_map/ppermute | solution.py:342
  73.7 1.6 %project_mine.1 = (bf16[640,128]{1,0:T(8,128)(2,1)S(1)}, bf16[640,128]{1,0:T(8,128)(2,1)S(1)}, bf16[640,128]{1,0:T(8,128)(2,1)S(1)}, bf16[640,128]{1,0:T(8,128)(2,1)S(1)}) custom-call(s32[4]{0:T(128)S(1)} %pad_add_fusion.info, bf16[256,640]{1,0:T(8,128)(2,1)S(1)} %get-tuple-element.63.rows_ref, ...), custom_call_target="tpu_custom_call" | custom-call | tf_op jit(solution)/shard_map/project_mine/pallas_call | solution.py:292
  75.3 1.5 %collective-permute-start.13 = (bf16[640,128]{1,0:T(8,128)(2,1)S(1)}, bf16[640,128]{1,0:T(8,128)(2,1)S(1)}, u32[]{:S(2)}, u32[]{:S(2)}) collective-permute-start(bf16[640,128]{1,0:T(8,128)(2,1)S(1)} %get-tuple-element.66), channel_id=1, source_target_pairs={{0,2},{2,4},{4,6},{6,0},{1,3},{3,5},{5,7},{7,1},{8,10},{10,12},{12... | collective-permute-start | bytes 491528 | tf_op jit(solution)/shard_map/ppermute | solution.py:359
  77.4 2.1 %collective-permute-start.15 = (bf16[640,128]{1,0:T(8,128)(2,1)S(1)}, bf16[640,128]{1,0:T(8,128)(2,1)S(1)}, u32[]{:S(2)}, u32[]{:S(2)}) collective-permute-start(bf16[640,128]{1,0:T(8,128)(2,1)S(1)} %get-tuple-element.68), channel_id=1, source_target_pairs={{0,4},{2,6},{4,0},{6,2},{1,5},{3,7},{5,1},{7,3},{8,12},{10,14},{12... | collective-permute-start | bytes 491528 | tf_op jit(solution)/shard_map/ppermute | solution.py:359
  79.5 2.6 %collective-permute-done.13.b_ref = bf16[640,128]{1,0:T(8,128)(2,1)S(1)} collective-permute-done((bf16[640,128]{1,0:T(8,128)(2,1)S(1)}, bf16[640,128]{1,0:T(8,128)(2,1)S(1)}, u32[]{:S(2)}, u32[]{:S(2)}) %collective-permute-start.13) | collective-permute-done | bytes 163872 | tf_op jit(solution)/shard_map/ppermute | solution.py:359
  83.2 3.7 %collective-permute-done.15.d_ref = bf16[640,128]{1,0:T(8,128)(2,1)S(1)} collective-permute-done((bf16[640,128]{1,0:T(8,128)(2,1)S(1)}, bf16[640,128]{1,0:T(8,128)(2,1)S(1)}, u32[]{:S(2)}, u32[]{:S(2)}) %collective-permute-start.15) | collective-permute-done | bytes 163872 | tf_op jit(solution)/shard_map/ppermute | solution.py:359
  87.1 2.9 %collective-permute-start.16 = (bf16[128,640]{1,0:T(8,128)(2,1)S(1)}, bf16[128,640]{1,0:T(8,128)(2,1)S(1)}, u32[]{:S(2)}, u32[]{:S(2)}) collective-permute-start(bf16[128,640]{1,0:T(8,128)(2,1)S(1)} %sum_groups.1), channel_id=1, source_target_pairs={{0,0},{2,32},{4,38},{6,6},{32,2},{34,34},{36,36},{38,4},{64,98},{6... | collective-permute-start | bytes 491528 | tf_op jit(solution)/shard_map/ppermute | solution.py:366
  90.9 4.3 %collective-permute-done.16 = bf16[128,640]{1,0:T(8,128)(2,1)S(1)} collective-permute-done((bf16[128,640]{1,0:T(8,128)(2,1)S(1)}, bf16[128,640]{1,0:T(8,128)(2,1)S(1)}, u32[]{:S(2)}, u32[]{:S(2)}) %collective-permute-start.16) | collective-permute-done | bytes 163872 | tf_op jit(solution)/shard_map/ppermute | solution.py:366
  (33 shorter events, 11.2 us)
Async XLA Ops:
  0.6 12.7 %copy-start = (bf16[2048,128]{1,0:T(8,128)(2,1)S(1)}, bf16[2048,128]{1,0:T(8,128)(2,1)}, u32[]{:S(2)}) copy-start(bf16[2048,128]{1,0:T(8,128)(2,1)} %sk_ref.3) | copy-start | bytes 1572868
  0.6 12.7 %copy-start.1 = (bf16[2048,128]{1,0:T(8,128)(2,1)S(1)}, bf16[2048,128]{1,0:T(8,128)(2,1)}, u32[]{:S(2)}) copy-start(bf16[2048,128]{1,0:T(8,128)(2,1)} %sv_ref.3) | copy-start | bytes 1572868
  1.7 19.4 %collective-permute-start.1 = (bf16[2,512,128]{2,1,0:T(8,128)(2,1)S(1)}, bf16[2,512,128]{2,1,0:T(8,128)(2,1)S(1)}, u32[]{:S(2)}, u32[]{:S(2)}) collective-permute-start(bf16[2,512,128]{2,1,0:T(8,128)(2,1)S(1)} %pad_maximum_fusion.1.pair_ref.p0_ref), channel_id=1, source_target_pairs={{0,8},{8,16},{16,24},{24,0},{1,9},{9,17},{17,25},{25,1},{2,10},{10... | collective-permute-start | bytes 786440 | tf_op jit(solution)/shard_map/ppermute | solution.py:270
  3.4 17.7 %collective-permute-start.2 = (bf16[2,512,128]{2,1,0:T(8,128)(2,1)S(1)}, bf16[2,512,128]{2,1,0:T(8,128)(2,1)S(1)}, u32[]{:S(2)}, u32[]{:S(2)}) collective-permute-start(bf16[2,512,128]{2,1,0:T(8,128)(2,1)S(1)} %pad_maximum_fusion.1.pair_ref.p0_ref), channel_id=1, source_target_pairs={{0,24},{8,0},{16,8},{24,16},{1,25},{9,1},{17,9},{25,17},{2,26},{10... | collective-permute-start | bytes 786440 | tf_op jit(solution)/shard_map/ppermute | solution.py:270
  5.0 16.1 %collective-permute-start.3 = (bf16[2,512,128]{2,1,0:T(8,128)(2,1)S(1)}, bf16[2,512,128]{2,1,0:T(8,128)(2,1)S(1)}, u32[]{:S(2)}, u32[]{:S(2)}) collective-permute-start(bf16[2,512,128]{2,1,0:T(8,128)(2,1)S(1)} %pad_maximum_fusion.1.pair_ref.p0_ref), channel_id=1, source_target_pairs={{0,16},{8,24},{16,0},{24,8},{1,17},{9,25},{17,1},{25,9},{2,18},{10... | collective-permute-start | bytes 786440 | tf_op jit(solution)/shard_map/ppermute | solution.py:270
  7.0 13.0 %collective-permute-start = (bf16[320,640]{1,0:T(8,128)(2,1)}, bf16[320,640]{1,0:T(8,128)(2,1)}, u32[]{:S(2)}, u32[]{:S(2)}) collective-permute-start(bf16[320,640]{1,0:T(8,128)(2,1)} %param.15), channel_id=1, source_target_pairs={{0,96},{32,64},{64,32},{96,0},{1,97},{33,65},{65,33},{97,1},{2,98}... | collective-permute-start | bytes 1228808 | tf_op jit(solution)/shard_map/ppermute | solution.py:279
  13.3 6.7 %copy-start.2 = (bf16[320,640]{1,0:T(8,128)(2,1)S(1)}, bf16[320,640]{1,0:T(8,128)(2,1)}, u32[]{:S(2)}) copy-start(bf16[320,640]{1,0:T(8,128)(2,1)} %param.15) | copy-start | bytes 1228804
  21.1 37.3 %collective-permute-start.7 = (bf16[2,320,640]{2,1,0:T(8,128)(2,1)S(1)}, bf16[2,320,640]{2,1,0:T(8,128)(2,1)S(1)}, u32[]{:S(2)}, u32[]{:S(2)}) collective-permute-start(bf16[2,320,640]{2,1,0:T(8,128)(2,1)S(1)} %pad_maximum_fusion.w0_ref), channel_id=1, source_target_pairs={{0,8},{8,16},{16,24},{24,0},{1,9},{9,17},{17,25},{25,1},{2,10},{10... | collective-permute-start | bytes 2457608 | tf_op jit(solution)/shard_map/ppermute | solution.py:270
  21.9 37.9 %collective-permute-start.8 = (bf16[2,320,640]{2,1,0:T(8,128)(2,1)S(1)}, bf16[2,320,640]{2,1,0:T(8,128)(2,1)S(1)}, u32[]{:S(2)}, u32[]{:S(2)}) collective-permute-start(bf16[2,320,640]{2,1,0:T(8,128)(2,1)S(1)} %pad_maximum_fusion.w0_ref), channel_id=1, source_target_pairs={{0,24},{8,0},{16,8},{24,16},{1,25},{9,1},{17,9},{25,17},{2,26},{10... | collective-permute-start | bytes 2457608 | tf_op jit(solution)/shard_map/ppermute | solution.py:270
  24.4 35.3 %collective-permute-start.9 = (bf16[2,320,640]{2,1,0:T(8,128)(2,1)S(1)}, bf16[2,320,640]{2,1,0:T(8,128)(2,1)S(1)}, u32[]{:S(2)}, u32[]{:S(2)}) collective-permute-start(bf16[2,320,640]{2,1,0:T(8,128)(2,1)S(1)} %pad_maximum_fusion.w0_ref), channel_id=1, source_target_pairs={{0,16},{8,24},{16,0},{24,8},{1,17},{9,25},{17,1},{25,9},{2,18},{10... | collective-permute-start | bytes 2457608 | tf_op jit(solution)/shard_map/ppermute | solution.py:270
  54.5 13.9 %collective-permute-start.4 = (bf16[2,128,640]{2,1,0:T(8,128)(2,1)S(1)}, bf16[2,128,640]{2,1,0:T(8,128)(2,1)S(1)}, u32[]{:S(2)}, u32[]{:S(2)}) collective-permute-start(bf16[2,128,640]{2,1,0:T(8,128)(2,1)S(1)} %get-tuple-element.47), channel_id=1, source_target_pairs={{0,32},{32,64},{64,96},{96,0},{1,33},{33,65},{65,97},{97,1},{2,34}... | collective-permute-start | bytes 983048 | tf_op jit(solution)/shard_map/ppermute | solution.py:340
  55.2 13.2 %collective-permute-start.5 = (bf16[2,128,640]{2,1,0:T(8,128)(2,1)S(1)}, bf16[2,128,640]{2,1,0:T(8,128)(2,1)S(1)}, u32[]{:S(2)}, u32[]{:S(2)}) collective-permute-start(bf16[2,128,640]{2,1,0:T(8,128)(2,1)S(1)} %get-tuple-element.48), channel_id=1, source_target_pairs={{0,96},{32,0},{64,32},{96,64},{1,97},{33,1},{65,33},{97,65},{2,98}... | collective-permute-start | bytes 983048 | tf_op jit(solution)/shard_map/ppermute | solution.py:340
  58.5 9.9 %collective-permute-start.6 = (bf16[2,128,640]{2,1,0:T(8,128)(2,1)S(1)}, bf16[2,128,640]{2,1,0:T(8,128)(2,1)S(1)}, u32[]{:S(2)}, u32[]{:S(2)}) collective-permute-start(bf16[2,128,640]{2,1,0:T(8,128)(2,1)S(1)} %get-tuple-element.49), channel_id=1, source_target_pairs={{0,64},{32,96},{64,0},{96,32},{1,65},{33,97},{65,1},{97,33},{2,66}... | collective-permute-start | bytes 983048 | tf_op jit(solution)/shard_map/ppermute | solution.py:340
  59.8 8.6 %collective-permute-start.10 = (bf16[640,256]{1,0:T(8,128)(2,1)S(1)}, bf16[640,256]{1,0:T(8,128)(2,1)S(1)}, u32[]{:S(2)}, u32[]{:S(2)}) collective-permute-start(bf16[640,256]{1,0:T(8,128)(2,1)S(1)} %get-tuple-element.54), channel_id=1, source_target_pairs={{0,24},{8,0},{16,8},{24,16},{1,25},{9,1},{17,9},{25,17},{2,26},{10... | collective-permute-start | bytes 983048 | tf_op jit(solution)/shard_map/ppermute | solution.py:342
  61.4 8.3 %collective-permute-start.11 = (bf16[640,256]{1,0:T(8,128)(2,1)S(1)}, bf16[640,256]{1,0:T(8,128)(2,1)S(1)}, u32[]{:S(2)}, u32[]{:S(2)}) collective-permute-start(bf16[640,256]{1,0:T(8,128)(2,1)S(1)} %get-tuple-element.55), channel_id=1, source_target_pairs={{0,8},{8,16},{16,24},{24,0},{1,9},{9,17},{17,25},{25,1},{2,10},{10... | collective-permute-start | bytes 983048 | tf_op jit(solution)/shard_map/ppermute | solution.py:342
  71.5 2.2 %collective-permute-start.12 = (bf16[2,2,640,128]{3,2,1,0:T(8,128)(2,1)S(1)}, bf16[2,2,640,128]{3,2,1,0:T(8,128)(2,1)S(1)}, u32[]{:S(2)}, u32[]{:S(2)}) collective-permute-start(bf16[2,2,640,128]{3,2,1,0:T(8,128)(2,1)S(1)} %get-tuple-element.64), channel_id=1, source_target_pairs={{0,1},{1,0},{2,3},{3,2},{4,5},{5,4},{6,7},{7,6},{8,9},{9,8},{10,11... | collective-permute-start | bytes 1966088 | tf_op jit(solution)/shard_map/ppermute | solution.py:351
  71.6 18.4 %collective-permute-start.17 = (bf16[640,256]{1,0:T(8,128)(2,1)S(1)}, bf16[640,256]{1,0:T(8,128)(2,1)S(1)}, u32[]{:S(2)}, u32[]{:S(2)}) collective-permute-start(bf16[640,256]{1,0:T(8,128)(2,1)S(1)} %get-tuple-element.72), channel_id=1, source_target_pairs={{0,16},{8,24},{16,0},{24,8},{1,17},{9,25},{17,1},{25,9},{2,18},{10... | collective-permute-start | bytes 983048 | tf_op jit(solution)/shard_map/ppermute | solution.py:342
  75.3 6.8 %collective-permute-start.13 = (bf16[640,128]{1,0:T(8,128)(2,1)S(1)}, bf16[640,128]{1,0:T(8,128)(2,1)S(1)}, u32[]{:S(2)}, u32[]{:S(2)}) collective-permute-start(bf16[640,128]{1,0:T(8,128)(2,1)S(1)} %get-tuple-element.66), channel_id=1, source_target_pairs={{0,2},{2,4},{4,6},{6,0},{1,3},{3,5},{5,7},{7,1},{8,10},{10,12},{12... | collective-permute-start | bytes 491528 | tf_op jit(solution)/shard_map/ppermute | solution.py:359
  76.8 6.4 %collective-permute-start.14 = (bf16[640,128]{1,0:T(8,128)(2,1)S(1)}, bf16[640,128]{1,0:T(8,128)(2,1)S(1)}, u32[]{:S(2)}, u32[]{:S(2)}) collective-permute-start(bf16[640,128]{1,0:T(8,128)(2,1)S(1)} %get-tuple-element.67), channel_id=1, source_target_pairs={{0,6},{2,0},{4,2},{6,4},{1,7},{3,1},{5,3},{7,5},{8,14},{10,8},{12,... | collective-permute-start | bytes 491528 | tf_op jit(solution)/shard_map/ppermute | solution.py:359
  77.4 9.6 %collective-permute-start.15 = (bf16[640,128]{1,0:T(8,128)(2,1)S(1)}, bf16[640,128]{1,0:T(8,128)(2,1)S(1)}, u32[]{:S(2)}, u32[]{:S(2)}) collective-permute-start(bf16[640,128]{1,0:T(8,128)(2,1)S(1)} %get-tuple-element.68), channel_id=1, source_target_pairs={{0,4},{2,6},{4,0},{6,2},{1,5},{3,7},{5,1},{7,3},{8,12},{10,14},{12... | collective-permute-start | bytes 491528 | tf_op jit(solution)/shard_map/ppermute | solution.py:359
  87.1 8.1 %collective-permute-start.16 = (bf16[128,640]{1,0:T(8,128)(2,1)S(1)}, bf16[128,640]{1,0:T(8,128)(2,1)S(1)}, u32[]{:S(2)}, u32[]{:S(2)}) collective-permute-start(bf16[128,640]{1,0:T(8,128)(2,1)S(1)} %sum_groups.1), channel_id=1, source_target_pairs={{0,0},{2,32},{4,38},{6,6},{32,2},{34,34},{36,36},{38,4},{64,98},{6... | collective-permute-start | bytes 491528 | tf_op jit(solution)/shard_map/ppermute | solution.py:366

commit v8 on v7

--- a/solution.py
+++ b/solution.py
@@ -150,8 +150,8 @@
 
 def grads_kernel(
     info, q_ref, g_ref, p0_ref, p1_ref, p2_ref, p3_ref, sk_ref, sv_ref, part_ref,
-    dq0_ref, dq1_ref, dq2_ref, dq3_ref, own_ref, send1_ref, send2_ref, send3_ref,
-    stat_ref, keyt_ref, dkey_ref, dvalue_ref, dself_key_ref, dself_value_ref, dself_query_ref, piece_ref,
+    dq0_ref, dq1_ref, dq2_ref, dq3_ref, dkey_ref, dvalue_ref, dself_key_ref, dself_value_ref,
+    stat_ref, keyt_ref, dself_query_ref, piece_ref,
 ):
     pair_refs = (p0_ref, p1_ref, p2_ref, p3_ref)
     parts = [
@@ -162,8 +162,6 @@
     stat_ref[GROUP : 2 * GROUP, :] = mixed / total
     for i in range(SIDE):
         keyt_ref[i] = pair_refs[i][0].T
-    dkey_ref[...] = jnp.zeros_like(dkey_ref)
-    dvalue_ref[...] = jnp.zeros_like(dvalue_ref)
 
     q, g = load_own(q_ref, info), load_own(g_ref, info)
     keys = sk_ref[response_rows(info), :]
@@ -178,16 +176,16 @@
     dself_key_ref[...] = dot_nn(dscores, q)
     dself_query_ref[...] = dot_nn(keys.T, dscores)
 
-    @pl.loop(0, GROUP, unroll=True)
-    def _(head):
+    for head in range(GROUP):
         log_sum = stat_ref[pl.ds(head, 1), :]
         delta = stat_ref[pl.ds(GROUP + head, 1), :]
         q, g = load_head(q_ref, head), load_head(g_ref, head)
         dq = jnp.zeros((HD, SIDE * HD), F32)
         for i in range(SIDE):
             probs, dscores = score_grads(pair_refs[i][0], pair_refs[i][1], q, g, log_sum, delta)
-            dvalue_ref[i] += dot_nn(probs, g)
-            dkey_ref[i] += dot_nn(dscores, q)
+            dvalue, dkey = dot_nn(probs, g), dot_nn(dscores, q)
+            dvalue_ref[i] = dvalue if head == 0 else dvalue_ref[i] + dvalue
+            dkey_ref[i] = dkey if head == 0 else dkey_ref[i] + dkey
             dq = dq + dot_nn(keyt_ref[i], dscores)
         own = dself_query_ref[:, head_lanes(head)]
         for response in range(SIDE):
@@ -199,6 +197,10 @@
             out_ref[0, :, head_lanes(head)] = piece_ref[response]
             out_ref[1, :, head_lanes(head)] = piece_ref[response ^ 1]
 
+
+def split_kernel(
+    info, dkey_ref, dvalue_ref, dself_key_ref, dself_value_ref, own_ref, send1_ref, send2_ref, send3_ref
+):
     for i, step, ref in zip(range(SIDE), (0,) + PLACES, (own_ref, send1_ref, send2_ref, send3_ref)):
         source = lax.rem(info[1] + SIDE - step, SIDE)
         slots = pl.ds(pl.multiple_of(source * HD, HD), HD)
@@ -275,13 +277,15 @@
     place_y = lax.axis_index("y").astype(jnp.int32)
     info = jnp.stack([lax.axis_index(Z).astype(jnp.int32), place_y, lax.axis_index("core").astype(jnp.int32), lax.axis_index("x").astype(jnp.int32)])
     pair = jnp.stack([doc_keys, doc_values])
-    pairs = [pair] + spread(pair, "y")
+    pairs = [pair] + [lax.ppermute(pair, "y", ring(step)) for step in PLACES[:2]]
     other = lax.ppermute(query_weight, Z, [(i, SIDE - 1 - i) for i in range(SIDE)])
 
     def own_rows(array):
         return lax.dynamic_slice_in_dim(array.reshape(SIDE, L, WIDTH), place_y * HD, HD, 1)
 
     valid = (jnp.arange(HD, dtype=jnp.int32) + place_y * HD)[None, :] < lengths[:, None]
+    far, valid = lax.optimization_barrier((pair, valid))
+    pairs.append(lax.ppermute(far, "y", ring(PLACES[2])))
     q_own = own_rows(queries)
     g_own = own_rows(out_grads) * valid[..., None].astype(out_grads.dtype)
 
@@ -307,13 +311,19 @@
         "own_stats",
     )
     weight = jnp.stack([query_weight, other])
-    weight, stats, *pairs = lax.optimization_barrier((weight, stats, *pairs))
+    stats = call(
+        rest_stats_kernel,
+        shape((STATS, SIDE * HD), F32),
+        (info, q_own, g_own, *pairs[1:3], stats),
+        "near_stats",
+    )
+    weight, stats, pairs[3] = lax.optimization_barrier((weight, stats, pairs[3]))
     weights = [weight] + spread(weight, "y")
     stats = call(
         rest_stats_kernel,
         shape((SIDE, STATS, SIDE * HD), F32),
-        (info, q_own, g_own, *pairs[1:], stats),
-        "rest_stats",
+        (info, q_own, g_own, pairs[3], stats),
+        "far_stats",
     )
     parts = lax.all_to_all(stats, Z, 0, 0, tiled=True)
 
@@ -321,26 +331,27 @@
     back_shape = shape((doc_rows + HD, 2 * HD), BF16)
     found = call(
         grads_kernel,
-        [grad_shape] * SIDE + [shape(back_shape.shape, F32)] + [back_shape] * 3,
+        [grad_shape] * SIDE + [shape((SIDE, doc_rows, HD), F32)] * 2 + [shape((L, HD), F32)] * 2,
         (info, q_own, g_own, *pairs, self_keys, self_values, parts),
         "local_grads",
         megabytes=14,
         scratch=[
             pltpu.VMEM((STATS, SIDE * HD), F32),
             pltpu.VMEM((SIDE, HD, doc_rows), BF16),
-            pltpu.VMEM((SIDE, doc_rows, HD), F32),
-            pltpu.VMEM((SIDE, doc_rows, HD), F32),
-            pltpu.VMEM((L, HD), F32),
-            pltpu.VMEM((L, HD), F32),
             pltpu.VMEM((HD, WIDTH), F32),
             pltpu.VMEM((SIDE, HD, HD), BF16),
         ],
     )
-    dq, dq_sends, own, sends = found[0], found[1:SIDE], found[SIDE], found[SIDE + 1 :]
+    dq, dq_sends = found[0], found[1:SIDE]
+    own, *sends = call(
+        split_kernel,
+        [shape(back_shape.shape, F32)] + [back_shape] * 3,
+        (info, *found[SIDE:]),
+        "split_grads",
+    )
     dq_parts = [lax.ppermute(a, Z, ring(step)) for step, a in zip(PLACES, dq_sends)]
     weights, sends = lax.optimization_barrier((weights, sends))
     backs = [lax.ppermute(a, "y", ring(SIDE - step)) for step, a in zip(PLACES, sends)]
-    dq_parts, backs[:2] = lax.optimization_barrier((dq_parts, backs[:2]))
     columns = 2 * query_weight.shape[0]
     theirs, rows = call(
         project_theirs_kernel,
@@ -357,6 +368,7 @@
         scratch=[pltpu.VMEM((SIDE, columns, HD), BF16)],
     )
     terms = [lax.ppermute(a, "x", ring(step)) for step, a in zip(PLACES, terms)]
+    terms, backs[:2] = lax.optimization_barrier((terms, backs[:2]))
     input_grads = call(sum_turn_kernel, shape((HD, columns), BF16), (term, *terms), "sum_groups")
     moves = []
     for z in range(SIDE):

time: 96.1 us -> 93.5 us (0.973)
  waiting for transfers between devices: 24.7 us -> 19.8 us
  blocking collectives: 10 us -> 12.5 us
  starting transfers between devices: 28.5 us -> 26.7 us
  Pallas kernels: 26.8 us -> 28.2 us
    ppermute x6 -> x3, starting transfers between devices: 9.07 us -> 3.64 us  [spread(): return [lax.ppermute(array, axis, ring(step)) for step in PLACES]]
    ppermute x0 -> x3, starting transfers between devices: none -> 5.29 us  [the longest x2 3.31 us: body(): lax.ppermute(pair, 'y', ring(step))]
    ppermute x3, waiting for transfers between devices: 1.35 us -> 5.94 us  [body(): lax.ppermute(a, 'y', ring(SIDE - step))]
    ppermute x1, waiting for transfers between devices: 3.83 us -> 0.01 us  [body(): lax.ppermute(query_weight, Z, [(i, SIDE - 1 - i) for i in range(SIDE)])]
    ppermute x3, waiting for transfers between devices: 7.46 us -> 4.03 us  [body(): terms = [lax.ppermute(a, 'x', ring(step)) for step, a in zip(PLACES, terms)]]
    all_to_all x1, blocking collectives: 10 us -> 12.5 us  [body(): parts = lax.all_to_all(stats, Z, 0, 0, tiled=True)]
    ppermute x1, waiting for transfers between devices: 4.34 us -> 1.84 us  [body(): input_grads = lax.ppermute(input_grads, Z + ('x',), moves)]
    pallas_call x7 -> x9, Pallas kernels: 26.8 us -> 28.2 us  [call(): pl.pallas_call(kernel, in_specs=[smem if a is info else vmem for a in ope...]
  transfers between devices with their start and end apart: 18 -> 18, of which waited for: 9 -> 10; matrix products, arithmetic and copies ran while one was open for 4% -> 4% of each run, Pallas kernels for 26% -> 28%
where the time goes in v8:
time: 93.5 us; the launch traced here: 93.2 us
  Pallas kernels  28.2 us (30%)
  starting transfers between devices  26.7 us (29%)
  waiting for transfers between devices  19.8 us (21%)
  blocking collectives  12.5 us (13%)
  other arithmetic  4.46 us (5%)
    pallas_call x9, Pallas kernels, call(): pl.pallas_call(kernel, in_specs=[smem if a is info else vmem for a in ope...  28.2 us
    all_to_all x1, blocking collectives, body(): parts = lax.all_to_all(stats, Z, 0, 0, tiled=True)  12.5 us
    ppermute x3, waiting for transfers between devices, body(): lax.ppermute(a, Z, ring(step))  6.62 us
    ppermute x3, waiting for transfers between devices, body(): lax.ppermute(a, 'y', ring(SIDE - step))  5.94 us
    ppermute x3, starting transfers between devices, body(): lax.ppermute(a, Z, ring(step))  4.47 us
    ppermute x3, starting transfers between devices, body(): terms = [lax.ppermute(a, 'x', ring(step)) for step, a in zip(PLACES, terms)]  4.22 us
    ppermute x1, starting transfers between devices, body(): lax.ppermute(query_weight, Z, [(i, SIDE - 1 - i) for i in range(SIDE)])  4.04 us
    ppermute x3, waiting for transfers between devices, body(): terms = [lax.ppermute(a, 'x', ring(step)) for step, a in zip(PLACES, terms)]  4.03 us
  transfers between devices with their start and end apart: 18, of which 10 were waited for; matrix products, arithmetic and copies ran while one was open for 4% of the time, Pallas kernels for 28%

profile of v8, /device:TPU:2, one launch (start us, length us, event | category | flops | bytes accessed | tf_op | source)
XLA Modules:
  0.0 93.2 jit_solution(8647708019324951670)
XLA Ops:
  1.7 1.6 %collective-permute-start = (bf16[2,512,128]{2,1,0:T(8,128)(2,1)S(1)}, bf16[2,512,128]{2,1,0:T(8,128)(2,1)S(1)}, u32[]{:S(2)}, u32[]{:S(2)}) collective-permute-start(bf16[2,512,128]{2,1,0:T(8,128)(2,1)S(1)} %pad_maximum_fusion.1.pair_ref.p0_ref), channel_id=1, source_target_pairs={{0,8},{8,16},{16,24},{24,0},{1,9},{9,17},{17,25},{25,1},{2,10},{10... | collective-permute-start | bytes 786440 | tf_op jit(solution)/shard_map/ppermute | solution.py:280
  3.4 1.7 %collective-permute-start.1 = (bf16[2,512,128]{2,1,0:T(8,128)(2,1)S(1)}, bf16[2,512,128]{2,1,0:T(8,128)(2,1)S(1)}, u32[]{:S(2)}, u32[]{:S(2)}) collective-permute-start(bf16[2,512,128]{2,1,0:T(8,128)(2,1)S(1)} %pad_maximum_fusion.1.pair_ref.p0_ref), channel_id=1, source_target_pairs={{0,24},{8,0},{16,8},{24,16},{1,25},{9,1},{17,9},{25,17},{2,26},{10... | collective-permute-start | bytes 786440 | tf_op jit(solution)/shard_map/ppermute | solution.py:280
  5.0 4.0 %collective-permute-start.2 = (bf16[320,640]{1,0:T(8,128)(2,1)}, bf16[320,640]{1,0:T(8,128)(2,1)}, u32[]{:S(2)}, u32[]{:S(2)}) collective-permute-start(bf16[320,640]{1,0:T(8,128)(2,1)} %param.15), channel_id=1, source_target_pairs={{0,96},{32,64},{64,32},{96,0},{1,97},{33,65},{65,33},{97,1},{2,98}... | collective-permute-start | bytes 1228808 | tf_op jit(solution)/shard_map/ppermute | solution.py:281
  9.8 2.0 %collective-permute-start.3 = (bf16[2,512,128]{2,1,0:T(8,128)(2,1)S(1)}, bf16[2,512,128]{2,1,0:T(8,128)(2,1)S(1)}, u32[]{:S(2)}, u32[]{:S(2)}) collective-permute-start(bf16[2,512,128]{2,1,0:T(8,128)(2,1)S(1)} %pad_maximum_fusion.1.pair_ref.p0_ref), channel_id=1, source_target_pairs={{0,16},{8,24},{16,0},{24,8},{1,17},{9,25},{17,1},{25,9},{2,18},{10... | collective-permute-start | bytes 786440 | tf_op jit(solution)/shard_map/ppermute | solution.py:288
  13.4 2.8 %own_stats.1.refs_2_ = f32[16,512]{1,0:T(8,128)S(1)} custom-call(s32[4]{0:T(128)S(1)} %pad_add_fusion.info, bf16[4,128,640]{2,1,0:T(8,128)(2,1)S(1)} %get-tuple-element.84.q_ref, bf16[4,128,640]{2,1,0:T(8,128)(2,1)S(1)} %get-tuple-element.83.g_ref, bf16[2,512,128]{2,1,0:T(8,128)(2,1)S(1)} %pad_maximum_fusion.1.pair_ref.p0_ref, ...), custom_call_target="tpu_custom_call" | custom-call | tf_op jit(solution)/shard_map/own_stats/pallas_call | solution.py:296
  16.2 3.5 %near_stats.1.refs_1_ = f32[16,512]{1,0:T(8,128)S(1)} custom-call(s32[4]{0:T(128)S(1)} %pad_add_fusion.info, bf16[4,128,640]{2,1,0:T(8,128)(2,1)S(1)} %get-tuple-element.84.q_ref, bf16[4,128,640]{2,1,0:T(8,128)(2,1)S(1)} %get-tuple-element.83.g_ref, bf16[2,512,128]{2,1,0:T(8,128)(2,1)S(1)} %collective-permute-done.refs_0_.p1_ref, ...), custom_call_target="tpu_custom_call" | custom-call | tf_op jit(solution)/shard_map/near_stats/pallas_call | solution.py:296
  21.6 2.6 %collective-permute-start.8 = (bf16[2,320,640]{2,1,0:T(8,128)(2,1)S(1)}, bf16[2,320,640]{2,1,0:T(8,128)(2,1)S(1)}, u32[]{:S(2)}, u32[]{:S(2)}) collective-permute-start(bf16[2,320,640]{2,1,0:T(8,128)(2,1)S(1)} %pad_maximum_fusion.w0_ref), channel_id=1, source_target_pairs={{0,24},{8,0},{16,8},{24,16},{1,25},{9,1},{17,9},{25,17},{2,26},{10... | collective-permute-start | bytes 2457608 | tf_op jit(solution)/shard_map/ppermute | solution.py:272
  24.4 2.1 %far_stats.1 = f32[4,16,512]{2,1,0:T(8,128)S(1)} custom-call(s32[4]{0:T(128)S(1)} %pad_add_fusion.info, bf16[4,128,640]{2,1,0:T(8,128)(2,1)S(1)} %get-tuple-element.84.q_ref, bf16[4,128,640]{2,1,0:T(8,128)(2,1)S(1)} %get-tuple-element.83.g_ref, bf16[2,512,128]{2,1,0:T(8,128)(2,1)S(1)} %collective-permute-done.3.refs_0_.p3_ref, f32[16,512]{1,0:T(8,128)S(1)} %near_stats.1.refs_1_), custom_call_target="tpu_custom_call" | custom-call | tf_op jit(solution)/shard_map/far_stats/pallas_call | solution.py:296
  26.5 12.5 %all_to_all.5.part_ref = f32[4,16,512]{2,1,0:T(8,128)S(1)} all-to-all(f32[4,16,512]{2,1,0:T(8,128)S(1)} %far_stats.1), channel_id=1, replica_groups=mesh['z_high'=2,'z_low'=2,'y'=4,'x'=4,'core'=2] {'z_high','z_low'}, dimensions={0} | all-to-all | bytes 262144 | tf_op jit(solution)/shard_map/all_to_all | solution.py:328
  39.1 14.7 %local_grads.1 = (bf16[2,128,640]{2,1,0:T(8,128)(2,1)S(1)}, bf16[2,128,640]{2,1,0:T(8,128)(2,1)S(1)}, bf16[2,128,640]{2,1,0:T(8,128)(2,1)S(1)}, bf16[2,128,640]{...) custom-call(s32[4]{0:T(128)S(1)} %pad_add_fusion.info, ...), custom_call_target="tpu_custom_call" | custom-call | tf_op jit(solution)/shard_map/local_grads/pallas_call | solution.py:296
  54.5 2.7 %collective-permute-start.5 = (bf16[2,128,640]{2,1,0:T(8,128)(2,1)S(1)}, bf16[2,128,640]{2,1,0:T(8,128)(2,1)S(1)}, u32[]{:S(2)}, u32[]{:S(2)}) collective-permute-start(bf16[2,128,640]{2,1,0:T(8,128)(2,1)S(1)} %get-tuple-element.50), channel_id=1, source_target_pairs={{0,96},{32,0},{64,32},{96,64},{1,97},{33,1},{65,33},{97,65},{2,98}... | collective-permute-start | bytes 983048 | tf_op jit(solution)/shard_map/ppermute | solution.py:352
  60.5 1.7 %collective-permute-done.4.d1_ref = bf16[2,128,640]{2,1,0:T(8,128)(2,1)S(1)} collective-permute-done((bf16[2,128,640]{2,1,0:T(8,128)(2,1)S(1)}, bf16[2,128,640]{2,1,0:T(8,128)(2,1)S(1)}, u32[]{:S(2)}, u32[]{:S(2)}) %collective-permute-start.4) | collective-permute-done | bytes 327712 | tf_op jit(solution)/shard_map/ppermute | solution.py:352
  62.2 3.1 %collective-permute-done.5.d2_ref = bf16[2,128,640]{2,1,0:T(8,128)(2,1)S(1)} collective-permute-done((bf16[2,128,640]{2,1,0:T(8,128)(2,1)S(1)}, bf16[2,128,640]{2,1,0:T(8,128)(2,1)S(1)}, u32[]{:S(2)}, u32[]{:S(2)}) %collective-permute-start.5) | collective-permute-done | bytes 327712 | tf_op jit(solution)/shard_map/ppermute | solution.py:352
  65.3 1.8 %collective-permute-done.6.d3_ref = bf16[2,128,640]{2,1,0:T(8,128)(2,1)S(1)} collective-permute-done((bf16[2,128,640]{2,1,0:T(8,128)(2,1)S(1)}, bf16[2,128,640]{2,1,0:T(8,128)(2,1)S(1)}, u32[]{:S(2)}, u32[]{:S(2)}) %collective-permute-start.6) | collective-permute-done | bytes 327712 | tf_op jit(solution)/shard_map/ppermute | solution.py:352
  67.1 1.7 %project_theirs.1 = (bf16[2,2,640,128]{3,2,1,0:T(8,128)(2,1)S(1)}, bf16[256,640]{1,0:T(8,128)(2,1)S(1)}) custom-call(s32[4]{0:T(128)S(1)} %pad_add_fusion.info, bf16[2,128,640]{2,1,0:T(8,128)(2,1)S(1)} %get-tuple-element.48.d0_ref, bf16[2,128,640]{2,1,0:T(8,128)(2,1)S(1)} %collective-permute-done.4.d1_ref, ...), custom_call_target="tpu_custom_call" | custom-call | tf_op jit(solution)/shard_map/project_theirs/pallas_call | solution.py:296
  69.0 2.0 %collective-permute-start.15 = (bf16[640,256]{1,0:T(8,128)(2,1)S(1)}, bf16[640,256]{1,0:T(8,128)(2,1)S(1)}, u32[]{:S(2)}, u32[]{:S(2)}) collective-permute-start(bf16[640,256]{1,0:T(8,128)(2,1)S(1)} %get-tuple-element.71), channel_id=1, source_target_pairs={{0,8},{8,16},{16,24},{24,0},{1,9},{9,17},{17,25},{25,1},{2,10},{10... | collective-permute-start | bytes 983048 | tf_op jit(solution)/shard_map/ppermute | solution.py:354
  71.0 1.6 %project_mine.1 = (bf16[640,128]{1,0:T(8,128)(2,1)S(1)}, bf16[640,128]{1,0:T(8,128)(2,1)S(1)}, bf16[640,128]{1,0:T(8,128)(2,1)S(1)}, bf16[640,128]{1,0:T(8,128)(2,1)S(1)}) custom-call(s32[4]{0:T(128)S(1)} %pad_add_fusion.info, bf16[256,640]{1,0:T(8,128)(2,1)S(1)} %get-tuple-element.64.rows_ref, ...), custom_call_target="tpu_custom_call" | custom-call | tf_op jit(solution)/shard_map/project_mine/pallas_call | solution.py:296
  72.6 1.6 %collective-permute-start.11 = (bf16[640,128]{1,0:T(8,128)(2,1)S(1)}, bf16[640,128]{1,0:T(8,128)(2,1)S(1)}, u32[]{:S(2)}, u32[]{:S(2)}) collective-permute-start(bf16[640,128]{1,0:T(8,128)(2,1)S(1)} %get-tuple-element.67), channel_id=1, source_target_pairs={{0,2},{2,4},{4,6},{6,0},{1,3},{3,5},{5,7},{7,1},{8,10},{10,12},{12... | collective-permute-start | bytes 491528 | tf_op jit(solution)/shard_map/ppermute | solution.py:370
  74.7 2.1 %collective-permute-start.13 = (bf16[640,128]{1,0:T(8,128)(2,1)S(1)}, bf16[640,128]{1,0:T(8,128)(2,1)S(1)}, u32[]{:S(2)}, u32[]{:S(2)}) collective-permute-start(bf16[640,128]{1,0:T(8,128)(2,1)S(1)} %get-tuple-element.69), channel_id=1, source_target_pairs={{0,4},{2,6},{4,0},{6,2},{1,5},{3,7},{5,1},{7,3},{8,12},{10,14},{12... | collective-permute-start | bytes 491528 | tf_op jit(solution)/shard_map/ppermute | solution.py:370
  76.8 2.2 %collective-permute-done.14.b1_ref = bf16[640,256]{1,0:T(8,128)(2,1)S(1)} collective-permute-done((bf16[640,256]{1,0:T(8,128)(2,1)S(1)}, bf16[640,256]{1,0:T(8,128)(2,1)S(1)}, u32[]{:S(2)}, u32[]{:S(2)}) %collective-permute-start.14) | collective-permute-done | bytes 327712 | tf_op jit(solution)/shard_map/ppermute | solution.py:354
  80.6 3.6 %collective-permute-done.13.d_ref = bf16[640,128]{1,0:T(8,128)(2,1)S(1)} collective-permute-done((bf16[640,128]{1,0:T(8,128)(2,1)S(1)}, bf16[640,128]{1,0:T(8,128)(2,1)S(1)}, u32[]{:S(2)}, u32[]{:S(2)}) %collective-permute-start.13) | collective-permute-done | bytes 163872 | tf_op jit(solution)/shard_map/ppermute | solution.py:370
  84.4 2.0 %collective-permute-start.16 = (bf16[128,640]{1,0:T(8,128)(2,1)S(1)}, bf16[128,640]{1,0:T(8,128)(2,1)S(1)}, u32[]{:S(2)}, u32[]{:S(2)}) collective-permute-start(bf16[128,640]{1,0:T(8,128)(2,1)S(1)} %sum_groups.1), channel_id=1, source_target_pairs={{0,0},{2,32},{4,38},{6,6},{32,2},{34,34},{36,36},{38,4},{64,98},{6... | collective-permute-start | bytes 491528 | tf_op jit(solution)/shard_map/ppermute | solution.py:378
  86.5 3.3 %collective-permute-done.17.b3_ref = bf16[640,256]{1,0:T(8,128)(2,1)S(1)} collective-permute-done((bf16[640,256]{1,0:T(8,128)(2,1)S(1)}, bf16[640,256]{1,0:T(8,128)(2,1)S(1)}, u32[]{:S(2)}, u32[]{:S(2)}) %collective-permute-start.17) | collective-permute-done | bytes 327712 | tf_op jit(solution)/shard_map/ppermute | solution.py:354
  90.7 1.8 %collective-permute-done.16 = bf16[128,640]{1,0:T(8,128)(2,1)S(1)} collective-permute-done((bf16[128,640]{1,0:T(8,128)(2,1)S(1)}, bf16[128,640]{1,0:T(8,128)(2,1)S(1)}, u32[]{:S(2)}, u32[]{:S(2)}) %collective-permute-start.16) | collective-permute-done | bytes 163872 | tf_op jit(solution)/shard_map/ppermute | solution.py:378
  (36 shorter events, 13.5 us)
Async XLA Ops:
  0.6 12.8 %copy-start = (bf16[2048,128]{1,0:T(8,128)(2,1)S(1)}, bf16[2048,128]{1,0:T(8,128)(2,1)}, u32[]{:S(2)}) copy-start(bf16[2048,128]{1,0:T(8,128)(2,1)} %sk_ref.3) | copy-start | bytes 1572868
  0.6 12.7 %copy-start.1 = (bf16[2048,128]{1,0:T(8,128)(2,1)S(1)}, bf16[2048,128]{1,0:T(8,128)(2,1)}, u32[]{:S(2)}) copy-start(bf16[2048,128]{1,0:T(8,128)(2,1)} %sv_ref.3) | copy-start | bytes 1572868
  1.7 14.4 %collective-permute-start = (bf16[2,512,128]{2,1,0:T(8,128)(2,1)S(1)}, bf16[2,512,128]{2,1,0:T(8,128)(2,1)S(1)}, u32[]{:S(2)}, u32[]{:S(2)}) collective-permute-start(bf16[2,512,128]{2,1,0:T(8,128)(2,1)S(1)} %pad_maximum_fusion.1.pair_ref.p0_ref), channel_id=1, source_target_pairs={{0,8},{8,16},{16,24},{24,0},{1,9},{9,17},{17,25},{25,1},{2,10},{10... | collective-permute-start | bytes 786440 | tf_op jit(solution)/shard_map/ppermute | solution.py:280
  3.4 12.8 %collective-permute-start.1 = (bf16[2,512,128]{2,1,0:T(8,128)(2,1)S(1)}, bf16[2,512,128]{2,1,0:T(8,128)(2,1)S(1)}, u32[]{:S(2)}, u32[]{:S(2)}) collective-permute-start(bf16[2,512,128]{2,1,0:T(8,128)(2,1)S(1)} %pad_maximum_fusion.1.pair_ref.p0_ref), channel_id=1, source_target_pairs={{0,24},{8,0},{16,8},{24,16},{1,25},{9,1},{17,9},{25,17},{2,26},{10... | collective-permute-start | bytes 786440 | tf_op jit(solution)/shard_map/ppermute | solution.py:280
  5.0 14.6 %collective-permute-start.2 = (bf16[320,640]{1,0:T(8,128)(2,1)}, bf16[320,640]{1,0:T(8,128)(2,1)}, u32[]{:S(2)}, u32[]{:S(2)}) collective-permute-start(bf16[320,640]{1,0:T(8,128)(2,1)} %param.15), channel_id=1, source_target_pairs={{0,96},{32,64},{64,32},{96,0},{1,97},{33,65},{65,33},{97,1},{2,98}... | collective-permute-start | bytes 1228808 | tf_op jit(solution)/shard_map/ppermute | solution.py:281
  9.8 11.0 %collective-permute-start.3 = (bf16[2,512,128]{2,1,0:T(8,128)(2,1)S(1)}, bf16[2,512,128]{2,1,0:T(8,128)(2,1)S(1)}, u32[]{:S(2)}, u32[]{:S(2)}) collective-permute-start(bf16[2,512,128]{2,1,0:T(8,128)(2,1)S(1)} %pad_maximum_fusion.1.pair_ref.p0_ref), channel_id=1, source_target_pairs={{0,16},{8,24},{16,0},{24,8},{1,17},{9,25},{17,1},{25,9},{2,18},{10... | collective-permute-start | bytes 786440 | tf_op jit(solution)/shard_map/ppermute | solution.py:288
  13.3 6.4 %copy-start.2 = (bf16[320,640]{1,0:T(8,128)(2,1)S(1)}, bf16[320,640]{1,0:T(8,128)(2,1)}, u32[]{:S(2)}) copy-start(bf16[320,640]{1,0:T(8,128)(2,1)} %param.15) | copy-start | bytes 1228804
  20.8 37.7 %collective-permute-start.7 = (bf16[2,320,640]{2,1,0:T(8,128)(2,1)S(1)}, bf16[2,320,640]{2,1,0:T(8,128)(2,1)S(1)}, u32[]{:S(2)}, u32[]{:S(2)}) collective-permute-start(bf16[2,320,640]{2,1,0:T(8,128)(2,1)S(1)} %pad_maximum_fusion.w0_ref), channel_id=1, source_target_pairs={{0,8},{8,16},{16,24},{24,0},{1,9},{9,17},{17,25},{25,1},{2,10},{10... | collective-permute-start | bytes 2457608 | tf_op jit(solution)/shard_map/ppermute | solution.py:272
  21.6 38.9 %collective-permute-start.8 = (bf16[2,320,640]{2,1,0:T(8,128)(2,1)S(1)}, bf16[2,320,640]{2,1,0:T(8,128)(2,1)S(1)}, u32[]{:S(2)}, u32[]{:S(2)}) collective-permute-start(bf16[2,320,640]{2,1,0:T(8,128)(2,1)S(1)} %pad_maximum_fusion.w0_ref), channel_id=1, source_target_pairs={{0,24},{8,0},{16,8},{24,16},{1,25},{9,1},{17,9},{25,17},{2,26},{10... | collective-permute-start | bytes 2457608 | tf_op jit(solution)/shard_map/ppermute | solution.py:272
  24.1 36.3 %collective-permute-start.9 = (bf16[2,320,640]{2,1,0:T(8,128)(2,1)S(1)}, bf16[2,320,640]{2,1,0:T(8,128)(2,1)S(1)}, u32[]{:S(2)}, u32[]{:S(2)}) collective-permute-start(bf16[2,320,640]{2,1,0:T(8,128)(2,1)S(1)} %pad_maximum_fusion.w0_ref), channel_id=1, source_target_pairs={{0,16},{8,24},{16,0},{24,8},{1,17},{9,25},{17,1},{25,9},{2,18},{10... | collective-permute-start | bytes 2457608 | tf_op jit(solution)/shard_map/ppermute | solution.py:272
  53.8 8.4 %collective-permute-start.4 = (bf16[2,128,640]{2,1,0:T(8,128)(2,1)S(1)}, bf16[2,128,640]{2,1,0:T(8,128)(2,1)S(1)}, u32[]{:S(2)}, u32[]{:S(2)}) collective-permute-start(bf16[2,128,640]{2,1,0:T(8,128)(2,1)S(1)} %get-tuple-element.49), channel_id=1, source_target_pairs={{0,32},{32,64},{64,96},{96,0},{1,33},{33,65},{65,97},{97,1},{2,34}... | collective-permute-start | bytes 983048 | tf_op jit(solution)/shard_map/ppermute | solution.py:352
  54.5 10.8 %collective-permute-start.5 = (bf16[2,128,640]{2,1,0:T(8,128)(2,1)S(1)}, bf16[2,128,640]{2,1,0:T(8,128)(2,1)S(1)}, u32[]{:S(2)}, u32[]{:S(2)}) collective-permute-start(bf16[2,128,640]{2,1,0:T(8,128)(2,1)S(1)} %get-tuple-element.50), channel_id=1, source_target_pairs={{0,96},{32,0},{64,32},{96,64},{1,97},{33,1},{65,33},{97,65},{2,98}... | collective-permute-start | bytes 983048 | tf_op jit(solution)/shard_map/ppermute | solution.py:352
  58.5 8.6 %collective-permute-start.6 = (bf16[2,128,640]{2,1,0:T(8,128)(2,1)S(1)}, bf16[2,128,640]{2,1,0:T(8,128)(2,1)S(1)}, u32[]{:S(2)}, u32[]{:S(2)}) collective-permute-start(bf16[2,128,640]{2,1,0:T(8,128)(2,1)S(1)} %get-tuple-element.51), channel_id=1, source_target_pairs={{0,64},{32,96},{64,0},{96,32},{1,65},{33,97},{65,1},{97,33},{2,66}... | collective-permute-start | bytes 983048 | tf_op jit(solution)/shard_map/ppermute | solution.py:352
  68.8 2.2 %collective-permute-start.10 = (bf16[2,2,640,128]{3,2,1,0:T(8,128)(2,1)S(1)}, bf16[2,2,640,128]{3,2,1,0:T(8,128)(2,1)S(1)}, u32[]{:S(2)}, u32[]{:S(2)}) collective-permute-start(bf16[2,2,640,128]{3,2,1,0:T(8,128)(2,1)S(1)} %get-tuple-element.65), channel_id=1, source_target_pairs={{0,1},{1,0},{2,3},{3,2},{4,5},{5,4},{6,7},{7,6},{8,9},{9,8},{10,11... | collective-permute-start | bytes 1966088 | tf_op jit(solution)/shard_map/ppermute | solution.py:362
  68.9 10.1 %collective-permute-start.14 = (bf16[640,256]{1,0:T(8,128)(2,1)S(1)}, bf16[640,256]{1,0:T(8,128)(2,1)S(1)}, u32[]{:S(2)}, u32[]{:S(2)}) collective-permute-start(bf16[640,256]{1,0:T(8,128)(2,1)S(1)} %get-tuple-element.70), channel_id=1, source_target_pairs={{0,24},{8,0},{16,8},{24,16},{1,25},{9,1},{17,9},{25,17},{2,26},{10... | collective-permute-start | bytes 983048 | tf_op jit(solution)/shard_map/ppermute | solution.py:354
  69.0 11.2 %collective-permute-start.15 = (bf16[640,256]{1,0:T(8,128)(2,1)S(1)}, bf16[640,256]{1,0:T(8,128)(2,1)S(1)}, u32[]{:S(2)}, u32[]{:S(2)}) collective-permute-start(bf16[640,256]{1,0:T(8,128)(2,1)S(1)} %get-tuple-element.71), channel_id=1, source_target_pairs={{0,8},{8,16},{16,24},{24,0},{1,9},{9,17},{17,25},{25,1},{2,10},{10... | collective-permute-start | bytes 983048 | tf_op jit(solution)/shard_map/ppermute | solution.py:354
  72.6 7.6 %collective-permute-start.11 = (bf16[640,128]{1,0:T(8,128)(2,1)S(1)}, bf16[640,128]{1,0:T(8,128)(2,1)S(1)}, u32[]{:S(2)}, u32[]{:S(2)}) collective-permute-start(bf16[640,128]{1,0:T(8,128)(2,1)S(1)} %get-tuple-element.67), channel_id=1, source_target_pairs={{0,2},{2,4},{4,6},{6,0},{1,3},{3,5},{5,7},{7,1},{8,10},{10,12},{12... | collective-permute-start | bytes 491528 | tf_op jit(solution)/shard_map/ppermute | solution.py:370
  74.2 6.5 %collective-permute-start.12 = (bf16[640,128]{1,0:T(8,128)(2,1)S(1)}, bf16[640,128]{1,0:T(8,128)(2,1)S(1)}, u32[]{:S(2)}, u32[]{:S(2)}) collective-permute-start(bf16[640,128]{1,0:T(8,128)(2,1)S(1)} %get-tuple-element.68), channel_id=1, source_target_pairs={{0,6},{2,0},{4,2},{6,4},{1,7},{3,1},{5,3},{7,5},{8,14},{10,8},{12,... | collective-permute-start | bytes 491528 | tf_op jit(solution)/shard_map/ppermute | solution.py:370
  74.7 9.6 %collective-permute-start.13 = (bf16[640,128]{1,0:T(8,128)(2,1)S(1)}, bf16[640,128]{1,0:T(8,128)(2,1)S(1)}, u32[]{:S(2)}, u32[]{:S(2)}) collective-permute-start(bf16[640,128]{1,0:T(8,128)(2,1)S(1)} %get-tuple-element.69), channel_id=1, source_target_pairs={{0,4},{2,6},{4,0},{6,2},{1,5},{3,7},{5,1},{7,3},{8,12},{10,14},{12... | collective-permute-start | bytes 491528 | tf_op jit(solution)/shard_map/ppermute | solution.py:370
  79.0 10.8 %collective-permute-start.17 = (bf16[640,256]{1,0:T(8,128)(2,1)S(1)}, bf16[640,256]{1,0:T(8,128)(2,1)S(1)}, u32[]{:S(2)}, u32[]{:S(2)}) collective-permute-start(bf16[640,256]{1,0:T(8,128)(2,1)S(1)} %get-tuple-element.78), channel_id=1, source_target_pairs={{0,16},{8,24},{16,0},{24,8},{1,17},{9,25},{17,1},{25,9},{2,18},{10... | collective-permute-start | bytes 983048 | tf_op jit(solution)/shard_map/ppermute | solution.py:354
  84.4 8.1 %collective-permute-start.16 = (bf16[128,640]{1,0:T(8,128)(2,1)S(1)}, bf16[128,640]{1,0:T(8,128)(2,1)S(1)}, u32[]{:S(2)}, u32[]{:S(2)}) collective-permute-start(bf16[128,640]{1,0:T(8,128)(2,1)S(1)} %sum_groups.1), channel_id=1, source_target_pairs={{0,0},{2,32},{4,38},{6,6},{32,2},{34,34},{36,36},{38,4},{64,98},{6... | collective-permute-start | bytes 491528 | tf_op jit(solution)/shard_map/ppermute | solution.py:378

commit v9 on v8

--- a/solution.py
+++ b/solution.py
@@ -257,7 +257,7 @@
 
     def put(part, block, at, terms):
         terms = terms + theirs_ref[part, block, at, :].astype(F32)
-        out_ref[columns[block] ^ part, at, :] = terms.astype(BF16)
+        out_ref[columns[block] ^ 1 ^ part, at, :] = terms.astype(BF16)
 
     project_blocks(info, (w0_ref, w1_ref, w2_ref, w3_ref), info[2], rows_ref[...], put)
     for step, ref in zip((0,) + PLACES, (o0_ref, o1_ref, o2_ref, o3_ref)):
@@ -373,8 +373,8 @@
     moves = []
     for z in range(SIDE):
         for x in range(SIDE):
-            stays = x in (z, SIDE - 1 - z)
-            moves.append((z * SIDE + x, z * SIDE + x if stays else (z ^ 1) * SIDE + (x ^ 1)))
+            partner = x in (z, SIDE - 1 - z)
+            moves.append((z * SIDE + x, (z ^ 1) * SIDE + x if partner else z * SIDE + (x ^ 1)))
     input_grads = lax.ppermute(input_grads, Z + ("x",), moves)
     grads = call(
         finish_kernel,

time: 93.5 us -> 91.7 us (0.981)
  starting transfers between devices: 26.7 us -> 25.6 us
    ppermute x1, waiting for transfers between devices: 1.84 us -> 0.01 us  [body(): input_grads = lax.ppermute(input_grads, Z + ('x',), moves)]
    ppermute x3, waiting for transfers between devices: 5.94 us -> 7.02 us  [body(): lax.ppermute(a, 'y', ring(SIDE - step))]
    ppermute x1, starting transfers between devices: 2.03 us -> 0.95 us  [body(): input_grads = lax.ppermute(input_grads, Z + ('x',), moves)]
  transfers between devices with their start and end apart: 18 -> 18, of which waited for: 10 -> 9; matrix products, arithmetic and copies ran while one was open for 4% -> 4% of each run, Pallas kernels for 28% -> 29%
where the time goes in v9:
time: 91.7 us; the launch traced here: 91.4 us
  Pallas kernels  28.2 us (31%)
  starting transfers between devices  25.6 us (28%)
  waiting for transfers between devices  19.1 us (21%)
  blocking collectives  12.5 us (14%)
  other arithmetic  4.46 us (5%)
    pallas_call x9, Pallas kernels, call(): pl.pallas_call(kernel, in_specs=[smem if a is info else vmem for a in ope...  28.2 us
    all_to_all x1, blocking collectives, body(): parts = lax.all_to_all(stats, Z, 0, 0, tiled=True)  12.5 us
    ppermute x3, waiting for transfers between devices, body(): lax.ppermute(a, 'y', ring(SIDE - step))  7.02 us
    ppermute x3, waiting for transfers between devices, body(): lax.ppermute(a, Z, ring(step))  6.62 us
    ppermute x3, starting transfers between devices, body(): lax.ppermute(a, Z, ring(step))  4.47 us
    ppermute x3, starting transfers between devices, body(): terms = [lax.ppermute(a, 'x', ring(step)) for step, a in zip(PLACES, terms)]  4.22 us
    ppermute x1, starting transfers between devices, body(): lax.ppermute(query_weight, Z, [(i, SIDE - 1 - i) for i in range(SIDE)])  4.04 us
    ppermute x3, waiting for transfers between devices, body(): terms = [lax.ppermute(a, 'x', ring(step)) for step, a in zip(PLACES, terms)]  4.03 us
  transfers between devices with their start and end apart: 18, of which 9 were waited for; matrix products, arithmetic and copies ran while one was open for 4% of the time, Pallas kernels for 29%

profile of v9, /device:TPU:2, one launch (start us, length us, event | category | flops | bytes accessed | tf_op | source)
XLA Modules:
  0.0 91.4 jit_solution(14883419927140413885)
XLA Ops:
  1.7 1.6 %collective-permute-start = (bf16[2,512,128]{2,1,0:T(8,128)(2,1)S(1)}, bf16[2,512,128]{2,1,0:T(8,128)(2,1)S(1)}, u32[]{:S(2)}, u32[]{:S(2)}) collective-permute-start(bf16[2,512,128]{2,1,0:T(8,128)(2,1)S(1)} %pad_maximum_fusion.1.pair_ref.p0_ref), channel_id=1, source_target_pairs={{0,8},{8,16},{16,24},{24,0},{1,9},{9,17},{17,25},{25,1},{2,10},{10... | collective-permute-start | bytes 786440 | tf_op jit(solution)/shard_map/ppermute | solution.py:280
  3.4 1.7 %collective-permute-start.1 = (bf16[2,512,128]{2,1,0:T(8,128)(2,1)S(1)}, bf16[2,512,128]{2,1,0:T(8,128)(2,1)S(1)}, u32[]{:S(2)}, u32[]{:S(2)}) collective-permute-start(bf16[2,512,128]{2,1,0:T(8,128)(2,1)S(1)} %pad_maximum_fusion.1.pair_ref.p0_ref), channel_id=1, source_target_pairs={{0,24},{8,0},{16,8},{24,16},{1,25},{9,1},{17,9},{25,17},{2,26},{10... | collective-permute-start | bytes 786440 | tf_op jit(solution)/shard_map/ppermute | solution.py:280
  5.0 4.0 %collective-permute-start.2 = (bf16[320,640]{1,0:T(8,128)(2,1)}, bf16[320,640]{1,0:T(8,128)(2,1)}, u32[]{:S(2)}, u32[]{:S(2)}) collective-permute-start(bf16[320,640]{1,0:T(8,128)(2,1)} %param.15), channel_id=1, source_target_pairs={{0,96},{32,64},{64,32},{96,0},{1,97},{33,65},{65,33},{97,1},{2,98}... | collective-permute-start | bytes 1228808 | tf_op jit(solution)/shard_map/ppermute | solution.py:281
  9.8 2.0 %collective-permute-start.3 = (bf16[2,512,128]{2,1,0:T(8,128)(2,1)S(1)}, bf16[2,512,128]{2,1,0:T(8,128)(2,1)S(1)}, u32[]{:S(2)}, u32[]{:S(2)}) collective-permute-start(bf16[2,512,128]{2,1,0:T(8,128)(2,1)S(1)} %pad_maximum_fusion.1.pair_ref.p0_ref), channel_id=1, source_target_pairs={{0,16},{8,24},{16,0},{24,8},{1,17},{9,25},{17,1},{25,9},{2,18},{10... | collective-permute-start | bytes 786440 | tf_op jit(solution)/shard_map/ppermute | solution.py:288
  11.8 1.5 %dynamic-slice_multiply_fusion = (bf16[4,128,640]{2,1,0:T(8,128)(2,1)S(1)}, bf16[4,128,640]{2,1,0:T(8,128)(2,1)S(1)}) fusion(bf16[4,512,640]{2,1,0:T(8,128)(2,1)} %bitcast.11, s32[]{:T(128)S(6)} %select_n.4, bf16[4,128]{1,0:T(4,128)(2,1)S(1)} %convert_element_type.4, bf16[4,512,640]{2,1,0:T(8,128)(2,1)} %bitcast.12), kind=kLoop, calls=%fused_computation.1 | loop fusion | flops 1310720 | bytes 2622468 | tf_op jit(solution)/shard_map/mul | solution.py:290
  13.4 2.8 %own_stats.1.refs_2_ = f32[16,512]{1,0:T(8,128)S(1)} custom-call(s32[4]{0:T(128)S(1)} %pad_add_fusion.info, bf16[4,128,640]{2,1,0:T(8,128)(2,1)S(1)} %get-tuple-element.84.q_ref, bf16[4,128,640]{2,1,0:T(8,128)(2,1)S(1)} %get-tuple-element.83.g_ref, bf16[2,512,128]{2,1,0:T(8,128)(2,1)S(1)} %pad_maximum_fusion.1.pair_ref.p0_ref, ...), custom_call_target="tpu_custom_call" | custom-call | tf_op jit(solution)/shard_map/own_stats/pallas_call | solution.py:296
  16.2 3.5 %near_stats.1.refs_1_ = f32[16,512]{1,0:T(8,128)S(1)} custom-call(s32[4]{0:T(128)S(1)} %pad_add_fusion.info, bf16[4,128,640]{2,1,0:T(8,128)(2,1)S(1)} %get-tuple-element.84.q_ref, bf16[4,128,640]{2,1,0:T(8,128)(2,1)S(1)} %get-tuple-element.83.g_ref, bf16[2,512,128]{2,1,0:T(8,128)(2,1)S(1)} %collective-permute-done.refs_0_.p1_ref, ...), custom_call_target="tpu_custom_call" | custom-call | tf_op jit(solution)/shard_map/near_stats/pallas_call | solution.py:296
  21.6 2.6 %collective-permute-start.8 = (bf16[2,320,640]{2,1,0:T(8,128)(2,1)S(1)}, bf16[2,320,640]{2,1,0:T(8,128)(2,1)S(1)}, u32[]{:S(2)}, u32[]{:S(2)}) collective-permute-start(bf16[2,320,640]{2,1,0:T(8,128)(2,1)S(1)} %pad_maximum_fusion.w0_ref), channel_id=1, source_target_pairs={{0,24},{8,0},{16,8},{24,16},{1,25},{9,1},{17,9},{25,17},{2,26},{10... | collective-permute-start | bytes 2457608 | tf_op jit(solution)/shard_map/ppermute | solution.py:272
  24.4 2.1 %far_stats.1 = f32[4,16,512]{2,1,0:T(8,128)S(1)} custom-call(s32[4]{0:T(128)S(1)} %pad_add_fusion.info, bf16[4,128,640]{2,1,0:T(8,128)(2,1)S(1)} %get-tuple-element.84.q_ref, bf16[4,128,640]{2,1,0:T(8,128)(2,1)S(1)} %get-tuple-element.83.g_ref, bf16[2,512,128]{2,1,0:T(8,128)(2,1)S(1)} %collective-permute-done.3.refs_0_.p3_ref, f32[16,512]{1,0:T(8,128)S(1)} %near_stats.1.refs_1_), custom_call_target="tpu_custom_call" | custom-call | tf_op jit(solution)/shard_map/far_stats/pallas_call | solution.py:296
  26.5 12.5 %all_to_all.5.part_ref = f32[4,16,512]{2,1,0:T(8,128)S(1)} all-to-all(f32[4,16,512]{2,1,0:T(8,128)S(1)} %far_stats.1), channel_id=1, replica_groups=mesh['z_high'=2,'z_low'=2,'y'=4,'x'=4,'core'=2] {'z_high','z_low'}, dimensions={0} | all-to-all | bytes 262144 | tf_op jit(solution)/shard_map/all_to_all | solution.py:328
  39.1 14.7 %local_grads.1 = (bf16[2,128,640]{2,1,0:T(8,128)(2,1)S(1)}, bf16[2,128,640]{2,1,0:T(8,128)(2,1)S(1)}, bf16[2,128,640]{2,1,0:T(8,128)(2,1)S(1)}, bf16[2,128,640]{...) custom-call(s32[4]{0:T(128)S(1)} %pad_add_fusion.info, ...), custom_call_target="tpu_custom_call" | custom-call | tf_op jit(solution)/shard_map/local_grads/pallas_call | solution.py:296
  54.5 2.7 %collective-permute-start.5 = (bf16[2,128,640]{2,1,0:T(8,128)(2,1)S(1)}, bf16[2,128,640]{2,1,0:T(8,128)(2,1)S(1)}, u32[]{:S(2)}, u32[]{:S(2)}) collective-permute-start(bf16[2,128,640]{2,1,0:T(8,128)(2,1)S(1)} %get-tuple-element.50), channel_id=1, source_target_pairs={{0,96},{32,0},{64,32},{96,64},{1,97},{33,1},{65,33},{97,65},{2,98}... | collective-permute-start | bytes 983048 | tf_op jit(solution)/shard_map/ppermute | solution.py:352
  57.1 1.4 %collective-permute-done.7.w1_ref = bf16[2,320,640]{2,1,0:T(8,128)(2,1)S(1)} collective-permute-done((bf16[2,320,640]{2,1,0:T(8,128)(2,1)S(1)}, bf16[2,320,640]{2,1,0:T(8,128)(2,1)S(1)}, u32[]{:S(2)}, u32[]{:S(2)}) %collective-permute-start.7) | collective-permute-done | bytes 819232 | tf_op jit(solution)/shard_map/ppermute | solution.py:272
  60.5 1.7 %collective-permute-done.4.d1_ref = bf16[2,128,640]{2,1,0:T(8,128)(2,1)S(1)} collective-permute-done((bf16[2,128,640]{2,1,0:T(8,128)(2,1)S(1)}, bf16[2,128,640]{2,1,0:T(8,128)(2,1)S(1)}, u32[]{:S(2)}, u32[]{:S(2)}) %collective-permute-start.4) | collective-permute-done | bytes 327712 | tf_op jit(solution)/shard_map/ppermute | solution.py:352
  62.2 3.1 %collective-permute-done.5.d2_ref = bf16[2,128,640]{2,1,0:T(8,128)(2,1)S(1)} collective-permute-done((bf16[2,128,640]{2,1,0:T(8,128)(2,1)S(1)}, bf16[2,128,640]{2,1,0:T(8,128)(2,1)S(1)}, u32[]{:S(2)}, u32[]{:S(2)}) %collective-permute-start.5) | collective-permute-done | bytes 327712 | tf_op jit(solution)/shard_map/ppermute | solution.py:352
  65.3 1.8 %collective-permute-done.6.d3_ref = bf16[2,128,640]{2,1,0:T(8,128)(2,1)S(1)} collective-permute-done((bf16[2,128,640]{2,1,0:T(8,128)(2,1)S(1)}, bf16[2,128,640]{2,1,0:T(8,128)(2,1)S(1)}, u32[]{:S(2)}, u32[]{:S(2)}) %collective-permute-start.6) | collective-permute-done | bytes 327712 | tf_op jit(solution)/shard_map/ppermute | solution.py:352
  67.1 1.7 %project_theirs.1 = (bf16[2,2,640,128]{3,2,1,0:T(8,128)(2,1)S(1)}, bf16[256,640]{1,0:T(8,128)(2,1)S(1)}) custom-call(s32[4]{0:T(128)S(1)} %pad_add_fusion.info, bf16[2,128,640]{2,1,0:T(8,128)(2,1)S(1)} %get-tuple-element.48.d0_ref, bf16[2,128,640]{2,1,0:T(8,128)(2,1)S(1)} %collective-permute-done.4.d1_ref, ...), custom_call_target="tpu_custom_call" | custom-call | tf_op jit(solution)/shard_map/project_theirs/pallas_call | solution.py:296
  69.0 2.0 %collective-permute-start.15 = (bf16[640,256]{1,0:T(8,128)(2,1)S(1)}, bf16[640,256]{1,0:T(8,128)(2,1)S(1)}, u32[]{:S(2)}, u32[]{:S(2)}) collective-permute-start(bf16[640,256]{1,0:T(8,128)(2,1)S(1)} %get-tuple-element.71), channel_id=1, source_target_pairs={{0,8},{8,16},{16,24},{24,0},{1,9},{9,17},{17,25},{25,1},{2,10},{10... | collective-permute-start | bytes 983048 | tf_op jit(solution)/shard_map/ppermute | solution.py:354
  71.0 1.6 %project_mine.1 = (bf16[640,128]{1,0:T(8,128)(2,1)S(1)}, bf16[640,128]{1,0:T(8,128)(2,1)S(1)}, bf16[640,128]{1,0:T(8,128)(2,1)S(1)}, bf16[640,128]{1,0:T(8,128)(2,1)S(1)}) custom-call(s32[4]{0:T(128)S(1)} %pad_add_fusion.info, bf16[256,640]{1,0:T(8,128)(2,1)S(1)} %get-tuple-element.64.rows_ref, ...), custom_call_target="tpu_custom_call" | custom-call | tf_op jit(solution)/shard_map/project_mine/pallas_call | solution.py:296
  72.6 1.6 %collective-permute-start.11 = (bf16[640,128]{1,0:T(8,128)(2,1)S(1)}, bf16[640,128]{1,0:T(8,128)(2,1)S(1)}, u32[]{:S(2)}, u32[]{:S(2)}) collective-permute-start(bf16[640,128]{1,0:T(8,128)(2,1)S(1)} %get-tuple-element.67), channel_id=1, source_target_pairs={{0,2},{2,4},{4,6},{6,0},{1,3},{3,5},{5,7},{7,1},{8,10},{10,12},{12... | collective-permute-start | bytes 491528 | tf_op jit(solution)/shard_map/ppermute | solution.py:370
  74.7 2.1 %collective-permute-start.13 = (bf16[640,128]{1,0:T(8,128)(2,1)S(1)}, bf16[640,128]{1,0:T(8,128)(2,1)S(1)}, u32[]{:S(2)}, u32[]{:S(2)}) collective-permute-start(bf16[640,128]{1,0:T(8,128)(2,1)S(1)} %get-tuple-element.69), channel_id=1, source_target_pairs={{0,4},{2,6},{4,0},{6,2},{1,5},{3,7},{5,1},{7,3},{8,12},{10,14},{12... | collective-permute-start | bytes 491528 | tf_op jit(solution)/shard_map/ppermute | solution.py:370
  76.8 2.2 %collective-permute-done.14.b1_ref = bf16[640,256]{1,0:T(8,128)(2,1)S(1)} collective-permute-done((bf16[640,256]{1,0:T(8,128)(2,1)S(1)}, bf16[640,256]{1,0:T(8,128)(2,1)S(1)}, u32[]{:S(2)}, u32[]{:S(2)}) %collective-permute-start.14) | collective-permute-done | bytes 327712 | tf_op jit(solution)/shard_map/ppermute | solution.py:354
  80.6 3.6 %collective-permute-done.13.d_ref = bf16[640,128]{1,0:T(8,128)(2,1)S(1)} collective-permute-done((bf16[640,128]{1,0:T(8,128)(2,1)S(1)}, bf16[640,128]{1,0:T(8,128)(2,1)S(1)}, u32[]{:S(2)}, u32[]{:S(2)}) %collective-permute-start.13) | collective-permute-done | bytes 163872 | tf_op jit(solution)/shard_map/ppermute | solution.py:370
  85.4 4.4 %collective-permute-done.17.b3_ref = bf16[640,256]{1,0:T(8,128)(2,1)S(1)} collective-permute-done((bf16[640,256]{1,0:T(8,128)(2,1)S(1)}, bf16[640,256]{1,0:T(8,128)(2,1)S(1)}, u32[]{:S(2)}, u32[]{:S(2)}) %collective-permute-start.17) | collective-permute-done | bytes 327712 | tf_op jit(solution)/shard_map/ppermute | solution.py:354
  (36 shorter events, 11.6 us)
Async XLA Ops:
  0.6 12.8 %copy-start = (bf16[2048,128]{1,0:T(8,128)(2,1)S(1)}, bf16[2048,128]{1,0:T(8,128)(2,1)}, u32[]{:S(2)}) copy-start(bf16[2048,128]{1,0:T(8,128)(2,1)} %sk_ref.3) | copy-start | bytes 1572868
  0.6 12.7 %copy-start.1 = (bf16[2048,128]{1,0:T(8,128)(2,1)S(1)}, bf16[2048,128]{1,0:T(8,128)(2,1)}, u32[]{:S(2)}) copy-start(bf16[2048,128]{1,0:T(8,128)(2,1)} %sv_ref.3) | copy-start | bytes 1572868
  1.7 14.4 %collective-permute-start = (bf16[2,512,128]{2,1,0:T(8,128)(2,1)S(1)}, bf16[2,512,128]{2,1,0:T(8,128)(2,1)S(1)}, u32[]{:S(2)}, u32[]{:S(2)}) collective-permute-start(bf16[2,512,128]{2,1,0:T(8,128)(2,1)S(1)} %pad_maximum_fusion.1.pair_ref.p0_ref), channel_id=1, source_target_pairs={{0,8},{8,16},{16,24},{24,0},{1,9},{9,17},{17,25},{25,1},{2,10},{10... | collective-permute-start | bytes 786440 | tf_op jit(solution)/shard_map/ppermute | solution.py:280
  3.4 12.8 %collective-permute-start.1 = (bf16[2,512,128]{2,1,0:T(8,128)(2,1)S(1)}, bf16[2,512,128]{2,1,0:T(8,128)(2,1)S(1)}, u32[]{:S(2)}, u32[]{:S(2)}) collective-permute-start(bf16[2,512,128]{2,1,0:T(8,128)(2,1)S(1)} %pad_maximum_fusion.1.pair_ref.p0_ref), channel_id=1, source_target_pairs={{0,24},{8,0},{16,8},{24,16},{1,25},{9,1},{17,9},{25,17},{2,26},{10... | collective-permute-start | bytes 786440 | tf_op jit(solution)/shard_map/ppermute | solution.py:280
  5.0 14.6 %collective-permute-start.2 = (bf16[320,640]{1,0:T(8,128)(2,1)}, bf16[320,640]{1,0:T(8,128)(2,1)}, u32[]{:S(2)}, u32[]{:S(2)}) collective-permute-start(bf16[320,640]{1,0:T(8,128)(2,1)} %param.15), channel_id=1, source_target_pairs={{0,96},{32,64},{64,32},{96,0},{1,97},{33,65},{65,33},{97,1},{2,98}... | collective-permute-start | bytes 1228808 | tf_op jit(solution)/shard_map/ppermute | solution.py:281
  9.8 11.0 %collective-permute-start.3 = (bf16[2,512,128]{2,1,0:T(8,128)(2,1)S(1)}, bf16[2,512,128]{2,1,0:T(8,128)(2,1)S(1)}, u32[]{:S(2)}, u32[]{:S(2)}) collective-permute-start(bf16[2,512,128]{2,1,0:T(8,128)(2,1)S(1)} %pad_maximum_fusion.1.pair_ref.p0_ref), channel_id=1, source_target_pairs={{0,16},{8,24},{16,0},{24,8},{1,17},{9,25},{17,1},{25,9},{2,18},{10... | collective-permute-start | bytes 786440 | tf_op jit(solution)/shard_map/ppermute | solution.py:288
  13.3 6.4 %copy-start.2 = (bf16[320,640]{1,0:T(8,128)(2,1)S(1)}, bf16[320,640]{1,0:T(8,128)(2,1)}, u32[]{:S(2)}) copy-start(bf16[320,640]{1,0:T(8,128)(2,1)} %param.15) | copy-start | bytes 1228804
  20.8 37.7 %collective-permute-start.7 = (bf16[2,320,640]{2,1,0:T(8,128)(2,1)S(1)}, bf16[2,320,640]{2,1,0:T(8,128)(2,1)S(1)}, u32[]{:S(2)}, u32[]{:S(2)}) collective-permute-start(bf16[2,320,640]{2,1,0:T(8,128)(2,1)S(1)} %pad_maximum_fusion.w0_ref), channel_id=1, source_target_pairs={{0,8},{8,16},{16,24},{24,0},{1,9},{9,17},{17,25},{25,1},{2,10},{10... | collective-permute-start | bytes 2457608 | tf_op jit(solution)/shard_map/ppermute | solution.py:272
  21.6 38.9 %collective-permute-start.8 = (bf16[2,320,640]{2,1,0:T(8,128)(2,1)S(1)}, bf16[2,320,640]{2,1,0:T(8,128)(2,1)S(1)}, u32[]{:S(2)}, u32[]{:S(2)}) collective-permute-start(bf16[2,320,640]{2,1,0:T(8,128)(2,1)S(1)} %pad_maximum_fusion.w0_ref), channel_id=1, source_target_pairs={{0,24},{8,0},{16,8},{24,16},{1,25},{9,1},{17,9},{25,17},{2,26},{10... | collective-permute-start | bytes 2457608 | tf_op jit(solution)/shard_map/ppermute | solution.py:272
  24.1 36.3 %collective-permute-start.9 = (bf16[2,320,640]{2,1,0:T(8,128)(2,1)S(1)}, bf16[2,320,640]{2,1,0:T(8,128)(2,1)S(1)}, u32[]{:S(2)}, u32[]{:S(2)}) collective-permute-start(bf16[2,320,640]{2,1,0:T(8,128)(2,1)S(1)} %pad_maximum_fusion.w0_ref), channel_id=1, source_target_pairs={{0,16},{8,24},{16,0},{24,8},{1,17},{9,25},{17,1},{25,9},{2,18},{10... | collective-permute-start | bytes 2457608 | tf_op jit(solution)/shard_map/ppermute | solution.py:272
  53.8 8.4 %collective-permute-start.4 = (bf16[2,128,640]{2,1,0:T(8,128)(2,1)S(1)}, bf16[2,128,640]{2,1,0:T(8,128)(2,1)S(1)}, u32[]{:S(2)}, u32[]{:S(2)}) collective-permute-start(bf16[2,128,640]{2,1,0:T(8,128)(2,1)S(1)} %get-tuple-element.49), channel_id=1, source_target_pairs={{0,32},{32,64},{64,96},{96,0},{1,33},{33,65},{65,97},{97,1},{2,34}... | collective-permute-start | bytes 983048 | tf_op jit(solution)/shard_map/ppermute | solution.py:352
  54.5 10.8 %collective-permute-start.5 = (bf16[2,128,640]{2,1,0:T(8,128)(2,1)S(1)}, bf16[2,128,640]{2,1,0:T(8,128)(2,1)S(1)}, u32[]{:S(2)}, u32[]{:S(2)}) collective-permute-start(bf16[2,128,640]{2,1,0:T(8,128)(2,1)S(1)} %get-tuple-element.50), channel_id=1, source_target_pairs={{0,96},{32,0},{64,32},{96,64},{1,97},{33,1},{65,33},{97,65},{2,98}... | collective-permute-start | bytes 983048 | tf_op jit(solution)/shard_map/ppermute | solution.py:352
  58.5 8.6 %collective-permute-start.6 = (bf16[2,128,640]{2,1,0:T(8,128)(2,1)S(1)}, bf16[2,128,640]{2,1,0:T(8,128)(2,1)S(1)}, u32[]{:S(2)}, u32[]{:S(2)}) collective-permute-start(bf16[2,128,640]{2,1,0:T(8,128)(2,1)S(1)} %get-tuple-element.51), channel_id=1, source_target_pairs={{0,64},{32,96},{64,0},{96,32},{1,65},{33,97},{65,1},{97,33},{2,66}... | collective-permute-start | bytes 983048 | tf_op jit(solution)/shard_map/ppermute | solution.py:352
  68.8 2.2 %collective-permute-start.10 = (bf16[2,2,640,128]{3,2,1,0:T(8,128)(2,1)S(1)}, bf16[2,2,640,128]{3,2,1,0:T(8,128)(2,1)S(1)}, u32[]{:S(2)}, u32[]{:S(2)}) collective-permute-start(bf16[2,2,640,128]{3,2,1,0:T(8,128)(2,1)S(1)} %get-tuple-element.65), channel_id=1, source_target_pairs={{0,1},{1,0},{2,3},{3,2},{4,5},{5,4},{6,7},{7,6},{8,9},{9,8},{10,11... | collective-permute-start | bytes 1966088 | tf_op jit(solution)/shard_map/ppermute | solution.py:362
  68.9 10.1 %collective-permute-start.14 = (bf16[640,256]{1,0:T(8,128)(2,1)S(1)}, bf16[640,256]{1,0:T(8,128)(2,1)S(1)}, u32[]{:S(2)}, u32[]{:S(2)}) collective-permute-start(bf16[640,256]{1,0:T(8,128)(2,1)S(1)} %get-tuple-element.70), channel_id=1, source_target_pairs={{0,24},{8,0},{16,8},{24,16},{1,25},{9,1},{17,9},{25,17},{2,26},{10... | collective-permute-start | bytes 983048 | tf_op jit(solution)/shard_map/ppermute | solution.py:354
  69.0 11.2 %collective-permute-start.15 = (bf16[640,256]{1,0:T(8,128)(2,1)S(1)}, bf16[640,256]{1,0:T(8,128)(2,1)S(1)}, u32[]{:S(2)}, u32[]{:S(2)}) collective-permute-start(bf16[640,256]{1,0:T(8,128)(2,1)S(1)} %get-tuple-element.71), channel_id=1, source_target_pairs={{0,8},{8,16},{16,24},{24,0},{1,9},{9,17},{17,25},{25,1},{2,10},{10... | collective-permute-start | bytes 983048 | tf_op jit(solution)/shard_map/ppermute | solution.py:354
  72.6 7.6 %collective-permute-start.11 = (bf16[640,128]{1,0:T(8,128)(2,1)S(1)}, bf16[640,128]{1,0:T(8,128)(2,1)S(1)}, u32[]{:S(2)}, u32[]{:S(2)}) collective-permute-start(bf16[640,128]{1,0:T(8,128)(2,1)S(1)} %get-tuple-element.67), channel_id=1, source_target_pairs={{0,2},{2,4},{4,6},{6,0},{1,3},{3,5},{5,7},{7,1},{8,10},{10,12},{12... | collective-permute-start | bytes 491528 | tf_op jit(solution)/shard_map/ppermute | solution.py:370
  74.2 6.5 %collective-permute-start.12 = (bf16[640,128]{1,0:T(8,128)(2,1)S(1)}, bf16[640,128]{1,0:T(8,128)(2,1)S(1)}, u32[]{:S(2)}, u32[]{:S(2)}) collective-permute-start(bf16[640,128]{1,0:T(8,128)(2,1)S(1)} %get-tuple-element.68), channel_id=1, source_target_pairs={{0,6},{2,0},{4,2},{6,4},{1,7},{3,1},{5,3},{7,5},{8,14},{10,8},{12,... | collective-permute-start | bytes 491528 | tf_op jit(solution)/shard_map/ppermute | solution.py:370
  74.7 9.6 %collective-permute-start.13 = (bf16[640,128]{1,0:T(8,128)(2,1)S(1)}, bf16[640,128]{1,0:T(8,128)(2,1)S(1)}, u32[]{:S(2)}, u32[]{:S(2)}) collective-permute-start(bf16[640,128]{1,0:T(8,128)(2,1)S(1)} %get-tuple-element.69), channel_id=1, source_target_pairs={{0,4},{2,6},{4,0},{6,2},{1,5},{3,7},{5,1},{7,3},{8,12},{10,14},{12... | collective-permute-start | bytes 491528 | tf_op jit(solution)/shard_map/ppermute | solution.py:370
  79.0 10.8 %collective-permute-start.17 = (bf16[640,256]{1,0:T(8,128)(2,1)S(1)}, bf16[640,256]{1,0:T(8,128)(2,1)S(1)}, u32[]{:S(2)}, u32[]{:S(2)}) collective-permute-start(bf16[640,256]{1,0:T(8,128)(2,1)S(1)} %get-tuple-element.78), channel_id=1, source_target_pairs={{0,16},{8,24},{16,0},{24,8},{1,17},{9,25},{17,1},{25,9},{2,18},{10... | collective-permute-start | bytes 983048 | tf_op jit(solution)/shard_map/ppermute | solution.py:354
  84.4 6.3 %collective-permute-start.16 = (bf16[128,640]{1,0:T(8,128)(2,1)S(1)}, bf16[128,640]{1,0:T(8,128)(2,1)S(1)}, u32[]{:S(2)}, u32[]{:S(2)}) collective-permute-start(bf16[128,640]{1,0:T(8,128)(2,1)S(1)} %sum_groups.1), channel_id=1, source_target_pairs={{0,32},{2,0},{4,6},{6,38},{32,34},{34,2},{36,4},{38,36},{64,66},{6... | collective-permute-start | bytes 491528 | tf_op jit(solution)/shard_map/ppermute | solution.py:378

commit v10 on v9

--- a/solution.py
+++ b/solution.py
@@ -368,7 +368,7 @@
         scratch=[pltpu.VMEM((SIDE, columns, HD), BF16)],
     )
     terms = [lax.ppermute(a, "x", ring(step)) for step, a in zip(PLACES, terms)]
-    terms, backs[:2] = lax.optimization_barrier((terms, backs[:2]))
+    terms, backs[0], backs[2] = lax.optimization_barrier((terms, backs[0], backs[2]))
     input_grads = call(sum_turn_kernel, shape((HD, columns), BF16), (term, *terms), "sum_groups")
     moves = []
     for z in range(SIDE):

time: 91.7 us -> 92.6 us (level); the launches traced: 91.4 us -> 91.1 us
  no operation moved by 1% of the time
where the time goes in v10:
time: 92.6 us; the launch traced here: 91.1 us
  Pallas kernels  28.2 us (30%)
  starting transfers between devices  24.9 us (27%)
  waiting for transfers between devices  19.5 us (21%)
  blocking collectives  12.5 us (13%)
  other arithmetic  4.46 us (5%)
    pallas_call x9, Pallas kernels, call(): pl.pallas_call(kernel, in_specs=[smem if a is info else vmem for a in ope...  28.2 us
    all_to_all x1, blocking collectives, body(): parts = lax.all_to_all(stats, Z, 0, 0, tiled=True)  12.5 us
    ppermute x3, waiting for transfers between devices, body(): lax.ppermute(a, 'y', ring(SIDE - step))  7.72 us
    ppermute x3, waiting for transfers between devices, body(): lax.ppermute(a, Z, ring(step))  6.62 us
    ppermute x3, starting transfers between devices, body(): lax.ppermute(a, Z, ring(step))  4.47 us
    ppermute x3, starting transfers between devices, body(): terms = [lax.ppermute(a, 'x', ring(step)) for step, a in zip(PLACES, terms)]  4.22 us
    ppermute x1, starting transfers between devices, body(): lax.ppermute(query_weight, Z, [(i, SIDE - 1 - i) for i in range(SIDE)])  4.04 us
    ppermute x3, waiting for transfers between devices, body(): terms = [lax.ppermute(a, 'x', ring(step)) for step, a in zip(PLACES, terms)]  3.74 us
  transfers between devices with their start and end apart: 18, of which 9 were waited for; matrix products, arithmetic and copies ran while one was open for 4% of the time, Pallas kernels for 29%

profile of v10, /device:TPU:2, one launch (start us, length us, event | category | flops | bytes accessed | tf_op | source)
XLA Modules:
  0.0 91.1 jit_solution(2245427652845170001)
XLA Ops:
  1.7 1.6 %collective-permute-start = (bf16[2,512,128]{2,1,0:T(8,128)(2,1)S(1)}, bf16[2,512,128]{2,1,0:T(8,128)(2,1)S(1)}, u32[]{:S(2)}, u32[]{:S(2)}) collective-permute-start(bf16[2,512,128]{2,1,0:T(8,128)(2,1)S(1)} %pad_maximum_fusion.1.pair_ref.p0_ref), channel_id=1, source_target_pairs={{0,8},{8,16},{16,24},{24,0},{1,9},{9,17},{17,25},{25,1},{2,10},{10... | collective-permute-start | bytes 786440 | tf_op jit(solution)/shard_map/ppermute | solution.py:280
  3.4 1.7 %collective-permute-start.1 = (bf16[2,512,128]{2,1,0:T(8,128)(2,1)S(1)}, bf16[2,512,128]{2,1,0:T(8,128)(2,1)S(1)}, u32[]{:S(2)}, u32[]{:S(2)}) collective-permute-start(bf16[2,512,128]{2,1,0:T(8,128)(2,1)S(1)} %pad_maximum_fusion.1.pair_ref.p0_ref), channel_id=1, source_target_pairs={{0,24},{8,0},{16,8},{24,16},{1,25},{9,1},{17,9},{25,17},{2,26},{10... | collective-permute-start | bytes 786440 | tf_op jit(solution)/shard_map/ppermute | solution.py:280
  5.0 4.0 %collective-permute-start.2 = (bf16[320,640]{1,0:T(8,128)(2,1)}, bf16[320,640]{1,0:T(8,128)(2,1)}, u32[]{:S(2)}, u32[]{:S(2)}) collective-permute-start(bf16[320,640]{1,0:T(8,128)(2,1)} %param.15), channel_id=1, source_target_pairs={{0,96},{32,64},{64,32},{96,0},{1,97},{33,65},{65,33},{97,1},{2,98}... | collective-permute-start | bytes 1228808 | tf_op jit(solution)/shard_map/ppermute | solution.py:281
  9.8 2.0 %collective-permute-start.3 = (bf16[2,512,128]{2,1,0:T(8,128)(2,1)S(1)}, bf16[2,512,128]{2,1,0:T(8,128)(2,1)S(1)}, u32[]{:S(2)}, u32[]{:S(2)}) collective-permute-start(bf16[2,512,128]{2,1,0:T(8,128)(2,1)S(1)} %pad_maximum_fusion.1.pair_ref.p0_ref), channel_id=1, source_target_pairs={{0,16},{8,24},{16,0},{24,8},{1,17},{9,25},{17,1},{25,9},{2,18},{10... | collective-permute-start | bytes 786440 | tf_op jit(solution)/shard_map/ppermute | solution.py:288
  11.8 1.5 %dynamic-slice_multiply_fusion = (bf16[4,128,640]{2,1,0:T(8,128)(2,1)S(1)}, bf16[4,128,640]{2,1,0:T(8,128)(2,1)S(1)}) fusion(bf16[4,512,640]{2,1,0:T(8,128)(2,1)} %bitcast.11, s32[]{:T(128)S(6)} %select_n.4, bf16[4,128]{1,0:T(4,128)(2,1)S(1)} %convert_element_type.4, bf16[4,512,640]{2,1,0:T(8,128)(2,1)} %bitcast.12), kind=kLoop, calls=%fused_computation.1 | loop fusion | flops 1310720 | bytes 2622468 | tf_op jit(solution)/shard_map/mul | solution.py:290
  13.4 2.8 %own_stats.1.refs_2_ = f32[16,512]{1,0:T(8,128)S(1)} custom-call(s32[4]{0:T(128)S(1)} %pad_add_fusion.info, bf16[4,128,640]{2,1,0:T(8,128)(2,1)S(1)} %get-tuple-element.84.q_ref, bf16[4,128,640]{2,1,0:T(8,128)(2,1)S(1)} %get-tuple-element.83.g_ref, bf16[2,512,128]{2,1,0:T(8,128)(2,1)S(1)} %pad_maximum_fusion.1.pair_ref.p0_ref, ...), custom_call_target="tpu_custom_call" | custom-call | tf_op jit(solution)/shard_map/own_stats/pallas_call | solution.py:296
  16.2 3.5 %near_stats.1.refs_1_ = f32[16,512]{1,0:T(8,128)S(1)} custom-call(s32[4]{0:T(128)S(1)} %pad_add_fusion.info, bf16[4,128,640]{2,1,0:T(8,128)(2,1)S(1)} %get-tuple-element.84.q_ref, bf16[4,128,640]{2,1,0:T(8,128)(2,1)S(1)} %get-tuple-element.83.g_ref, bf16[2,512,128]{2,1,0:T(8,128)(2,1)S(1)} %collective-permute-done.refs_0_.p1_ref, ...), custom_call_target="tpu_custom_call" | custom-call | tf_op jit(solution)/shard_map/near_stats/pallas_call | solution.py:296
  21.6 2.6 %collective-permute-start.8 = (bf16[2,320,640]{2,1,0:T(8,128)(2,1)S(1)}, bf16[2,320,640]{2,1,0:T(8,128)(2,1)S(1)}, u32[]{:S(2)}, u32[]{:S(2)}) collective-permute-start(bf16[2,320,640]{2,1,0:T(8,128)(2,1)S(1)} %pad_maximum_fusion.w0_ref), channel_id=1, source_target_pairs={{0,24},{8,0},{16,8},{24,16},{1,25},{9,1},{17,9},{25,17},{2,26},{10... | collective-permute-start | bytes 2457608 | tf_op jit(solution)/shard_map/ppermute | solution.py:272
  24.4 2.1 %far_stats.1 = f32[4,16,512]{2,1,0:T(8,128)S(1)} custom-call(s32[4]{0:T(128)S(1)} %pad_add_fusion.info, bf16[4,128,640]{2,1,0:T(8,128)(2,1)S(1)} %get-tuple-element.84.q_ref, bf16[4,128,640]{2,1,0:T(8,128)(2,1)S(1)} %get-tuple-element.83.g_ref, bf16[2,512,128]{2,1,0:T(8,128)(2,1)S(1)} %collective-permute-done.3.refs_0_.p3_ref, f32[16,512]{1,0:T(8,128)S(1)} %near_stats.1.refs_1_), custom_call_target="tpu_custom_call" | custom-call | tf_op jit(solution)/shard_map/far_stats/pallas_call | solution.py:296
  26.5 12.5 %all_to_all.5.part_ref = f32[4,16,512]{2,1,0:T(8,128)S(1)} all-to-all(f32[4,16,512]{2,1,0:T(8,128)S(1)} %far_stats.1), channel_id=1, replica_groups=mesh['z_high'=2,'z_low'=2,'y'=4,'x'=4,'core'=2] {'z_high','z_low'}, dimensions={0} | all-to-all | bytes 262144 | tf_op jit(solution)/shard_map/all_to_all | solution.py:328
  39.1 14.7 %local_grads.1 = (bf16[2,128,640]{2,1,0:T(8,128)(2,1)S(1)}, bf16[2,128,640]{2,1,0:T(8,128)(2,1)S(1)}, bf16[2,128,640]{2,1,0:T(8,128)(2,1)S(1)}, bf16[2,128,640]{...) custom-call(s32[4]{0:T(128)S(1)} %pad_add_fusion.info, ...), custom_call_target="tpu_custom_call" | custom-call | tf_op jit(solution)/shard_map/local_grads/pallas_call | solution.py:296
  54.5 2.7 %collective-permute-start.5 = (bf16[2,128,640]{2,1,0:T(8,128)(2,1)S(1)}, bf16[2,128,640]{2,1,0:T(8,128)(2,1)S(1)}, u32[]{:S(2)}, u32[]{:S(2)}) collective-permute-start(bf16[2,128,640]{2,1,0:T(8,128)(2,1)S(1)} %get-tuple-element.50), channel_id=1, source_target_pairs={{0,96},{32,0},{64,32},{96,64},{1,97},{33,1},{65,33},{97,65},{2,98}... | collective-permute-start | bytes 983048 | tf_op jit(solution)/shard_map/ppermute | solution.py:352
  57.1 1.4 %collective-permute-done.7.w1_ref = bf16[2,320,640]{2,1,0:T(8,128)(2,1)S(1)} collective-permute-done((bf16[2,320,640]{2,1,0:T(8,128)(2,1)S(1)}, bf16[2,320,640]{2,1,0:T(8,128)(2,1)S(1)}, u32[]{:S(2)}, u32[]{:S(2)}) %collective-permute-start.7) | collective-permute-done | bytes 819232 | tf_op jit(solution)/shard_map/ppermute | solution.py:272
  60.5 1.7 %collective-permute-done.4.d1_ref = bf16[2,128,640]{2,1,0:T(8,128)(2,1)S(1)} collective-permute-done((bf16[2,128,640]{2,1,0:T(8,128)(2,1)S(1)}, bf16[2,128,640]{2,1,0:T(8,128)(2,1)S(1)}, u32[]{:S(2)}, u32[]{:S(2)}) %collective-permute-start.4) | collective-permute-done | bytes 327712 | tf_op jit(solution)/shard_map/ppermute | solution.py:352
  62.2 3.1 %collective-permute-done.5.d2_ref = bf16[2,128,640]{2,1,0:T(8,128)(2,1)S(1)} collective-permute-done((bf16[2,128,640]{2,1,0:T(8,128)(2,1)S(1)}, bf16[2,128,640]{2,1,0:T(8,128)(2,1)S(1)}, u32[]{:S(2)}, u32[]{:S(2)}) %collective-permute-start.5) | collective-permute-done | bytes 327712 | tf_op jit(solution)/shard_map/ppermute | solution.py:352
  65.3 1.8 %collective-permute-done.6.d3_ref = bf16[2,128,640]{2,1,0:T(8,128)(2,1)S(1)} collective-permute-done((bf16[2,128,640]{2,1,0:T(8,128)(2,1)S(1)}, bf16[2,128,640]{2,1,0:T(8,128)(2,1)S(1)}, u32[]{:S(2)}, u32[]{:S(2)}) %collective-permute-start.6) | collective-permute-done | bytes 327712 | tf_op jit(solution)/shard_map/ppermute | solution.py:352
  67.1 1.7 %project_theirs.1 = (bf16[2,2,640,128]{3,2,1,0:T(8,128)(2,1)S(1)}, bf16[256,640]{1,0:T(8,128)(2,1)S(1)}) custom-call(s32[4]{0:T(128)S(1)} %pad_add_fusion.info, bf16[2,128,640]{2,1,0:T(8,128)(2,1)S(1)} %get-tuple-element.48.d0_ref, bf16[2,128,640]{2,1,0:T(8,128)(2,1)S(1)} %collective-permute-done.4.d1_ref, ...), custom_call_target="tpu_custom_call" | custom-call | tf_op jit(solution)/shard_map/project_theirs/pallas_call | solution.py:296
  69.0 2.1 %collective-permute-start.15 = (bf16[640,256]{1,0:T(8,128)(2,1)S(1)}, bf16[640,256]{1,0:T(8,128)(2,1)S(1)}, u32[]{:S(2)}, u32[]{:S(2)}) collective-permute-start(bf16[640,256]{1,0:T(8,128)(2,1)S(1)} %get-tuple-element.71), channel_id=1, source_target_pairs={{0,16},{8,24},{16,0},{24,8},{1,17},{9,25},{17,1},{25,9},{2,18},{10... | collective-permute-start | bytes 983048 | tf_op jit(solution)/shard_map/ppermute | solution.py:354
  71.1 1.6 %project_mine.1 = (bf16[640,128]{1,0:T(8,128)(2,1)S(1)}, bf16[640,128]{1,0:T(8,128)(2,1)S(1)}, bf16[640,128]{1,0:T(8,128)(2,1)S(1)}, bf16[640,128]{1,0:T(8,128)(2,1)S(1)}) custom-call(s32[4]{0:T(128)S(1)} %pad_add_fusion.info, bf16[256,640]{1,0:T(8,128)(2,1)S(1)} %get-tuple-element.64.rows_ref, ...), custom_call_target="tpu_custom_call" | custom-call | tf_op jit(solution)/shard_map/project_mine/pallas_call | solution.py:296
  72.7 1.6 %collective-permute-start.11 = (bf16[640,128]{1,0:T(8,128)(2,1)S(1)}, bf16[640,128]{1,0:T(8,128)(2,1)S(1)}, u32[]{:S(2)}, u32[]{:S(2)}) collective-permute-start(bf16[640,128]{1,0:T(8,128)(2,1)S(1)} %get-tuple-element.67), channel_id=1, source_target_pairs={{0,2},{2,4},{4,6},{6,0},{1,3},{3,5},{5,7},{7,1},{8,10},{10,12},{12... | collective-permute-start | bytes 491528 | tf_op jit(solution)/shard_map/ppermute | solution.py:370
  74.8 2.1 %collective-permute-start.13 = (bf16[640,128]{1,0:T(8,128)(2,1)S(1)}, bf16[640,128]{1,0:T(8,128)(2,1)S(1)}, u32[]{:S(2)}, u32[]{:S(2)}) collective-permute-start(bf16[640,128]{1,0:T(8,128)(2,1)S(1)} %get-tuple-element.69), channel_id=1, source_target_pairs={{0,4},{2,6},{4,0},{6,2},{1,5},{3,7},{5,1},{7,3},{8,12},{10,14},{12... | collective-permute-start | bytes 491528 | tf_op jit(solution)/shard_map/ppermute | solution.py:370
  76.9 2.6 %collective-permute-done.14.b1_ref = bf16[640,256]{1,0:T(8,128)(2,1)S(1)} collective-permute-done((bf16[640,256]{1,0:T(8,128)(2,1)S(1)}, bf16[640,256]{1,0:T(8,128)(2,1)S(1)}, u32[]{:S(2)}, u32[]{:S(2)}) %collective-permute-start.14) | collective-permute-done | bytes 327712 | tf_op jit(solution)/shard_map/ppermute | solution.py:354
  80.7 3.5 %collective-permute-done.13.d_ref = bf16[640,128]{1,0:T(8,128)(2,1)S(1)} collective-permute-done((bf16[640,128]{1,0:T(8,128)(2,1)S(1)}, bf16[640,128]{1,0:T(8,128)(2,1)S(1)}, u32[]{:S(2)}, u32[]{:S(2)}) %collective-permute-start.13) | collective-permute-done | bytes 163872 | tf_op jit(solution)/shard_map/ppermute | solution.py:370
  85.4 4.1 %collective-permute-done.17.b2_ref = bf16[640,256]{1,0:T(8,128)(2,1)S(1)} collective-permute-done((bf16[640,256]{1,0:T(8,128)(2,1)S(1)}, bf16[640,256]{1,0:T(8,128)(2,1)S(1)}, u32[]{:S(2)}, u32[]{:S(2)}) %collective-permute-start.17) | collective-permute-done | bytes 327712 | tf_op jit(solution)/shard_map/ppermute | solution.py:354
  (36 shorter events, 11.3 us)
Async XLA Ops:
  0.6 12.8 %copy-start = (bf16[2048,128]{1,0:T(8,128)(2,1)S(1)}, bf16[2048,128]{1,0:T(8,128)(2,1)}, u32[]{:S(2)}) copy-start(bf16[2048,128]{1,0:T(8,128)(2,1)} %sk_ref.3) | copy-start | bytes 1572868
  0.6 12.7 %copy-start.1 = (bf16[2048,128]{1,0:T(8,128)(2,1)S(1)}, bf16[2048,128]{1,0:T(8,128)(2,1)}, u32[]{:S(2)}) copy-start(bf16[2048,128]{1,0:T(8,128)(2,1)} %sv_ref.3) | copy-start | bytes 1572868
  1.7 14.4 %collective-permute-start = (bf16[2,512,128]{2,1,0:T(8,128)(2,1)S(1)}, bf16[2,512,128]{2,1,0:T(8,128)(2,1)S(1)}, u32[]{:S(2)}, u32[]{:S(2)}) collective-permute-start(bf16[2,512,128]{2,1,0:T(8,128)(2,1)S(1)} %pad_maximum_fusion.1.pair_ref.p0_ref), channel_id=1, source_target_pairs={{0,8},{8,16},{16,24},{24,0},{1,9},{9,17},{17,25},{25,1},{2,10},{10... | collective-permute-start | bytes 786440 | tf_op jit(solution)/shard_map/ppermute | solution.py:280
  3.4 12.8 %collective-permute-start.1 = (bf16[2,512,128]{2,1,0:T(8,128)(2,1)S(1)}, bf16[2,512,128]{2,1,0:T(8,128)(2,1)S(1)}, u32[]{:S(2)}, u32[]{:S(2)}) collective-permute-start(bf16[2,512,128]{2,1,0:T(8,128)(2,1)S(1)} %pad_maximum_fusion.1.pair_ref.p0_ref), channel_id=1, source_target_pairs={{0,24},{8,0},{16,8},{24,16},{1,25},{9,1},{17,9},{25,17},{2,26},{10... | collective-permute-start | bytes 786440 | tf_op jit(solution)/shard_map/ppermute | solution.py:280
  5.0 14.6 %collective-permute-start.2 = (bf16[320,640]{1,0:T(8,128)(2,1)}, bf16[320,640]{1,0:T(8,128)(2,1)}, u32[]{:S(2)}, u32[]{:S(2)}) collective-permute-start(bf16[320,640]{1,0:T(8,128)(2,1)} %param.15), channel_id=1, source_target_pairs={{0,96},{32,64},{64,32},{96,0},{1,97},{33,65},{65,33},{97,1},{2,98}... | collective-permute-start | bytes 1228808 | tf_op jit(solution)/shard_map/ppermute | solution.py:281
  9.8 11.0 %collective-permute-start.3 = (bf16[2,512,128]{2,1,0:T(8,128)(2,1)S(1)}, bf16[2,512,128]{2,1,0:T(8,128)(2,1)S(1)}, u32[]{:S(2)}, u32[]{:S(2)}) collective-permute-start(bf16[2,512,128]{2,1,0:T(8,128)(2,1)S(1)} %pad_maximum_fusion.1.pair_ref.p0_ref), channel_id=1, source_target_pairs={{0,16},{8,24},{16,0},{24,8},{1,17},{9,25},{17,1},{25,9},{2,18},{10... | collective-permute-start | bytes 786440 | tf_op jit(solution)/shard_map/ppermute | solution.py:288
  13.3 6.4 %copy-start.2 = (bf16[320,640]{1,0:T(8,128)(2,1)S(1)}, bf16[320,640]{1,0:T(8,128)(2,1)}, u32[]{:S(2)}) copy-start(bf16[320,640]{1,0:T(8,128)(2,1)} %param.15) | copy-start | bytes 1228804
  20.8 37.7 %collective-permute-start.7 = (bf16[2,320,640]{2,1,0:T(8,128)(2,1)S(1)}, bf16[2,320,640]{2,1,0:T(8,128)(2,1)S(1)}, u32[]{:S(2)}, u32[]{:S(2)}) collective-permute-start(bf16[2,320,640]{2,1,0:T(8,128)(2,1)S(1)} %pad_maximum_fusion.w0_ref), channel_id=1, source_target_pairs={{0,8},{8,16},{16,24},{24,0},{1,9},{9,17},{17,25},{25,1},{2,10},{10... | collective-permute-start | bytes 2457608 | tf_op jit(solution)/shard_map/ppermute | solution.py:272
  21.6 38.9 %collective-permute-start.8 = (bf16[2,320,640]{2,1,0:T(8,128)(2,1)S(1)}, bf16[2,320,640]{2,1,0:T(8,128)(2,1)S(1)}, u32[]{:S(2)}, u32[]{:S(2)}) collective-permute-start(bf16[2,320,640]{2,1,0:T(8,128)(2,1)S(1)} %pad_maximum_fusion.w0_ref), channel_id=1, source_target_pairs={{0,24},{8,0},{16,8},{24,16},{1,25},{9,1},{17,9},{25,17},{2,26},{10... | collective-permute-start | bytes 2457608 | tf_op jit(solution)/shard_map/ppermute | solution.py:272
  24.1 36.3 %collective-permute-start.9 = (bf16[2,320,640]{2,1,0:T(8,128)(2,1)S(1)}, bf16[2,320,640]{2,1,0:T(8,128)(2,1)S(1)}, u32[]{:S(2)}, u32[]{:S(2)}) collective-permute-start(bf16[2,320,640]{2,1,0:T(8,128)(2,1)S(1)} %pad_maximum_fusion.w0_ref), channel_id=1, source_target_pairs={{0,16},{8,24},{16,0},{24,8},{1,17},{9,25},{17,1},{25,9},{2,18},{10... | collective-permute-start | bytes 2457608 | tf_op jit(solution)/shard_map/ppermute | solution.py:272
  53.8 8.4 %collective-permute-start.4 = (bf16[2,128,640]{2,1,0:T(8,128)(2,1)S(1)}, bf16[2,128,640]{2,1,0:T(8,128)(2,1)S(1)}, u32[]{:S(2)}, u32[]{:S(2)}) collective-permute-start(bf16[2,128,640]{2,1,0:T(8,128)(2,1)S(1)} %get-tuple-element.49), channel_id=1, source_target_pairs={{0,32},{32,64},{64,96},{96,0},{1,33},{33,65},{65,97},{97,1},{2,34}... | collective-permute-start | bytes 983048 | tf_op jit(solution)/shard_map/ppermute | solution.py:352
  54.5 10.8 %collective-permute-start.5 = (bf16[2,128,640]{2,1,0:T(8,128)(2,1)S(1)}, bf16[2,128,640]{2,1,0:T(8,128)(2,1)S(1)}, u32[]{:S(2)}, u32[]{:S(2)}) collective-permute-start(bf16[2,128,640]{2,1,0:T(8,128)(2,1)S(1)} %get-tuple-element.50), channel_id=1, source_target_pairs={{0,96},{32,0},{64,32},{96,64},{1,97},{33,1},{65,33},{97,65},{2,98}... | collective-permute-start | bytes 983048 | tf_op jit(solution)/shard_map/ppermute | solution.py:352
  58.5 8.6 %collective-permute-start.6 = (bf16[2,128,640]{2,1,0:T(8,128)(2,1)S(1)}, bf16[2,128,640]{2,1,0:T(8,128)(2,1)S(1)}, u32[]{:S(2)}, u32[]{:S(2)}) collective-permute-start(bf16[2,128,640]{2,1,0:T(8,128)(2,1)S(1)} %get-tuple-element.51), channel_id=1, source_target_pairs={{0,64},{32,96},{64,0},{96,32},{1,65},{33,97},{65,1},{97,33},{2,66}... | collective-permute-start | bytes 983048 | tf_op jit(solution)/shard_map/ppermute | solution.py:352
  68.8 2.3 %collective-permute-start.10 = (bf16[2,2,640,128]{3,2,1,0:T(8,128)(2,1)S(1)}, bf16[2,2,640,128]{3,2,1,0:T(8,128)(2,1)S(1)}, u32[]{:S(2)}, u32[]{:S(2)}) collective-permute-start(bf16[2,2,640,128]{3,2,1,0:T(8,128)(2,1)S(1)} %get-tuple-element.65), channel_id=1, source_target_pairs={{0,1},{1,0},{2,3},{3,2},{4,5},{5,4},{6,7},{7,6},{8,9},{9,8},{10,11... | collective-permute-start | bytes 1966088 | tf_op jit(solution)/shard_map/ppermute | solution.py:362
  68.9 10.6 %collective-permute-start.14 = (bf16[640,256]{1,0:T(8,128)(2,1)S(1)}, bf16[640,256]{1,0:T(8,128)(2,1)S(1)}, u32[]{:S(2)}, u32[]{:S(2)}) collective-permute-start(bf16[640,256]{1,0:T(8,128)(2,1)S(1)} %get-tuple-element.70), channel_id=1, source_target_pairs={{0,24},{8,0},{16,8},{24,16},{1,25},{9,1},{17,9},{25,17},{2,26},{10... | collective-permute-start | bytes 983048 | tf_op jit(solution)/shard_map/ppermute | solution.py:354
  69.0 11.5 %collective-permute-start.15 = (bf16[640,256]{1,0:T(8,128)(2,1)S(1)}, bf16[640,256]{1,0:T(8,128)(2,1)S(1)}, u32[]{:S(2)}, u32[]{:S(2)}) collective-permute-start(bf16[640,256]{1,0:T(8,128)(2,1)S(1)} %get-tuple-element.71), channel_id=1, source_target_pairs={{0,16},{8,24},{16,0},{24,8},{1,17},{9,25},{17,1},{25,9},{2,18},{10... | collective-permute-start | bytes 983048 | tf_op jit(solution)/shard_map/ppermute | solution.py:354
  72.7 7.8 %collective-permute-start.11 = (bf16[640,128]{1,0:T(8,128)(2,1)S(1)}, bf16[640,128]{1,0:T(8,128)(2,1)S(1)}, u32[]{:S(2)}, u32[]{:S(2)}) collective-permute-start(bf16[640,128]{1,0:T(8,128)(2,1)S(1)} %get-tuple-element.67), channel_id=1, source_target_pairs={{0,2},{2,4},{4,6},{6,0},{1,3},{3,5},{5,7},{7,1},{8,10},{10,12},{12... | collective-permute-start | bytes 491528 | tf_op jit(solution)/shard_map/ppermute | solution.py:370
  74.3 6.5 %collective-permute-start.12 = (bf16[640,128]{1,0:T(8,128)(2,1)S(1)}, bf16[640,128]{1,0:T(8,128)(2,1)S(1)}, u32[]{:S(2)}, u32[]{:S(2)}) collective-permute-start(bf16[640,128]{1,0:T(8,128)(2,1)S(1)} %get-tuple-element.68), channel_id=1, source_target_pairs={{0,6},{2,0},{4,2},{6,4},{1,7},{3,1},{5,3},{7,5},{8,14},{10,8},{12,... | collective-permute-start | bytes 491528 | tf_op jit(solution)/shard_map/ppermute | solution.py:370
  74.8 9.5 %collective-permute-start.13 = (bf16[640,128]{1,0:T(8,128)(2,1)S(1)}, bf16[640,128]{1,0:T(8,128)(2,1)S(1)}, u32[]{:S(2)}, u32[]{:S(2)}) collective-permute-start(bf16[640,128]{1,0:T(8,128)(2,1)S(1)} %get-tuple-element.69), channel_id=1, source_target_pairs={{0,4},{2,6},{4,0},{6,2},{1,5},{3,7},{5,1},{7,3},{8,12},{10,14},{12... | collective-permute-start | bytes 491528 | tf_op jit(solution)/shard_map/ppermute | solution.py:370
  79.5 10.0 %collective-permute-start.17 = (bf16[640,256]{1,0:T(8,128)(2,1)S(1)}, bf16[640,256]{1,0:T(8,128)(2,1)S(1)}, u32[]{:S(2)}, u32[]{:S(2)}) collective-permute-start(bf16[640,256]{1,0:T(8,128)(2,1)S(1)} %get-tuple-element.77), channel_id=1, source_target_pairs={{0,8},{8,16},{16,24},{24,0},{1,9},{9,17},{17,25},{25,1},{2,10},{10... | collective-permute-start | bytes 983048 | tf_op jit(solution)/shard_map/ppermute | solution.py:354
  84.4 6.0 %collective-permute-start.16 = (bf16[128,640]{1,0:T(8,128)(2,1)S(1)}, bf16[128,640]{1,0:T(8,128)(2,1)S(1)}, u32[]{:S(2)}, u32[]{:S(2)}) collective-permute-start(bf16[128,640]{1,0:T(8,128)(2,1)S(1)} %sum_groups.1), channel_id=1, source_target_pairs={{0,32},{2,0},{4,6},{6,38},{32,34},{34,2},{36,4},{38,36},{64,66},{6... | collective-permute-start | bytes 491528 | tf_op jit(solution)/shard_map/ppermute | solution.py:378
